TPU v7x, 32 devices: a whole 2x2x4 slice. The times are simulated.
32 devices in a mesh: gx: 2 (over x), gy: 4 (over z), gz: 4 (over y, core).
Axes of the slice: x: 2, y: 2, z: 4, core: 2. Of those that a mesh axis runs over, the one named last changes fastest.
Arguments:
- coeffs: float32 [32, 512, 512], P(('gx', 'gy', 'gz')), may hold values from -6 to 6
- transfer: float32 [4, 32, 512, 1024], P(None, ('gx', 'gy', 'gz')), may hold values from -0.1875 to 0.1875
Outputs:
- result: float32 [32, 512, 512], P(('gx', 'gy', 'gz'))
All inputs are finite; a program needn't handle non-finite values.
Results may differ from a plain program's by a relative error of at most 0.0001.
Values sent between devices are 32-bit elements; how exact they have to be, the bound alone decides.
No kernel may reach another device: no remote copies, remote signals or barrier semaphores. Data moves between devices by JAX's collectives and lax.ppermute only.
A program may use at most 64 MiB of HBM per device.

v0:
```python
import jax
import jax.numpy as jnp
from jax import lax
from jax.sharding import PartitionSpec as P

LEVELS = 4


def from_partner(block, axis, stride):
    count = lax.axis_size(axis)
    route = []
    for low in range(count):
        high = low | 1 << stride
        if high != low and high < count:
            route += [(low, high), (high, low)]
    return lax.ppermute(block, axis, route)


def apply_level(matrix, own, other, upper):
    lower_part = jnp.where(upper == 1, other, own)
    upper_part = jnp.where(upper == 1, own, other)
    stacked = jnp.concatenate([lower_part, upper_part], axis=0)
    return jnp.dot(
        matrix, stacked, precision=lax.Precision.HIGHEST, preferred_element_type=jnp.float32
    )


def per_device(coeffs, transfer):
    nbits = lax.axis_size(("gx", "gy", "gz")).bit_length() - 1
    index = lax.axis_index(("gx", "gy", "gz"))
    current = coeffs[0]
    half = current.shape[1] // 2
    for level in range(LEVELS):
        bit = nbits - 1 - level
        upper = index >> bit & 1
        matrix = transfer[level, 0]
        left_own = current[:, :half]
        right_own = current[:, half:]
        left_other = from_partner(left_own, ("gx", "gy", "gz"), bit)
        right_other = from_partner(right_own, ("gx", "gy", "gz"), bit)
        left_new = apply_level(matrix, left_own, left_other, upper)
        right_new = apply_level(matrix, right_own, right_other, upper)
        current = jnp.concatenate([left_new, right_new], axis=1)
    return current[None]


def solution(mesh):
    placed = (P(("gx", "gy", "gz"), None, None), P(None, ("gx", "gy", "gz"), None, None))
    return jax.shard_map(
        per_device,
        mesh=mesh,
        in_specs=placed,
        out_specs=P(("gx", "gy", "gz"), None, None),
        check_vma=False,
    )
```

profile of v0, /device:TPU:0, one launch (start us, length us, event | category | flops | bytes accessed | tf_op | source)
XLA Modules:
  0.0 113.7 jit_solution(17892650001392174571)
XLA Ops:
  0.0 1.1 slice.24
  1.1 3.0 %collective-permute-start = (f32[512,256]{1,0:T(8,128)S(1)}, f32[512,256]{1,0:T(8,128)S(1)}, u32[]{:S(2)}, u32[]{:S(2)}) collective-permute-start(f32[512,256]{1,0:T(8,128)S(1)} %slice.24), channel_id=1, source_target_pairs={{0,16},{16,0},{1,17},{17,1},{2,18},{18,2},{3,19},{19,3},{4,20},{20... | collective-permute-start | bytes 1572872 | tf_op jit(solution)/shard_map/ppermute | solution.py:16
  4.1 11.9 %collective-permute-done = f32[512,256]{1,0:T(8,128)S(1)} collective-permute-done((f32[512,256]{1,0:T(8,128)S(1)}, f32[512,256]{1,0:T(8,128)S(1)}, u32[]{:S(2)}, u32[]{:S(2)}) %collective-permute-start) | collective-permute-done | bytes 524320 | tf_op jit(solution)/shard_map/ppermute | solution.py:16
  16.0 1.3 %broadcast_select_fusion.3 = (f32[512,256]{1,0:T(8,128)S(1)}, f32[512,256]{1,0:T(8,128)S(1)}, f32[512,256]{1,0:T(8,128)S(1)}) fusion(f32[512,256]{1,0:T(8,128)S(1)} %collective-permute-done, pred[]{:T(512)S(6)} %eq.11, f32[512,512]{1,0:T(8,128)} %bitcast.56), kind=kLoop, calls=%fused_computation.60 | loop fusion | flops 262144 | bytes 3145729 | tf_op jit(solution)/shard_map/jit(_where)/select_n | solution.py:20
  17.3 1.8 %collective-permute-start.4 = (f32[512,256]{1,0:T(8,128)S(1)}, f32[512,256]{1,0:T(8,128)S(1)}, u32[]{:S(2)}, u32[]{:S(2)}) collective-permute-start(f32[512,256]{1,0:T(8,128)S(1)} %get-tuple-element.15), channel_id=1, source_target_pairs={{0,16},{16,0},{1,17},{17,1},{2,18},{18,2},{3,19},{19,3},{4,20},{20... | collective-permute-start | bytes 1572872 | tf_op jit(solution)/shard_map/ppermute | solution.py:16
  19.1 0.0 copy-start
  19.2 5.3 %fusion.24 = f32[512,256]{0,1:T(8,128)S(1)} fusion(f32[4,1,512,1024]{3,2,1,0:T(8,128)} %param.3, f32[512,256]{1,0:T(8,128)S(1)} %get-tuple-element.6, f32[512,256]{1,0:T(8,128)S(1)} %get-tuple-element.5), kind=kOutput, calls=%fused_computation.24 | convolution fusion | flops 1610874880 | bytes 3670016 | tf_op jit(solution)/shard_map/dot_general | solution.py:23
  24.4 2.7 %collective-permute-start.1 = (f32[512,256]{0,1:T(8,128)S(1)}, f32[512,256]{0,1:T(8,128)S(1)}, u32[]{:S(2)}, u32[]{:S(2)}) collective-permute-start(f32[512,256]{0,1:T(8,128)S(1)} %fusion.24), channel_id=1, source_target_pairs={{0,8},{8,0},{1,9},{9,1},{2,10},{10,2},{3,11},{11,3},{4,12},{12,4},... | collective-permute-start | bytes 1572872 | tf_op jit(solution)/shard_map/ppermute | solution.py:16
  27.1 3.4 %collective-permute-done.4 = f32[512,256]{1,0:T(8,128)S(1)} collective-permute-done((f32[512,256]{1,0:T(8,128)S(1)}, f32[512,256]{1,0:T(8,128)S(1)}, u32[]{:S(2)}, u32[]{:S(2)}) %collective-permute-start.4) | collective-permute-done | bytes 524320 | tf_op jit(solution)/shard_map/ppermute | solution.py:16
  30.5 1.1 broadcast_select_fusion.1
  31.6 5.3 %fusion.27 = f32[512,256]{0,1:T(8,128)S(1)} fusion(f32[4,1,512,1024]{3,2,1,0:T(8,128)} %param.3, f32[512,256]{1,0:T(8,128)S(1)} %get-tuple-element.8, f32[512,256]{1,0:T(8,128)S(1)} %get-tuple-element.7), kind=kOutput, calls=%fused_computation.25 | convolution fusion | flops 1610874880 | bytes 3670016 | tf_op jit(solution)/shard_map/dot_general | solution.py:23
  36.9 2.6 %collective-permute-start.5 = (f32[512,256]{0,1:T(8,128)S(1)}, f32[512,256]{0,1:T(8,128)S(1)}, u32[]{:S(2)}, u32[]{:S(2)}) collective-permute-start(f32[512,256]{0,1:T(8,128)S(1)} %fusion.27), channel_id=1, source_target_pairs={{0,8},{8,0},{1,9},{9,1},{2,10},{10,2},{3,11},{11,3},{4,12},{12,4},... | collective-permute-start | bytes 1572872 | tf_op jit(solution)/shard_map/ppermute | solution.py:16
  39.5 22.1 %collective-permute-done.1 = f32[512,256]{0,1:T(8,128)S(1)} collective-permute-done((f32[512,256]{0,1:T(8,128)S(1)}, f32[512,256]{0,1:T(8,128)S(1)}, u32[]{:S(2)}, u32[]{:S(2)}) %collective-permute-start.1) | collective-permute-done | bytes 524320 | tf_op jit(solution)/shard_map/ppermute | solution.py:16
  61.5 0.1 broadcast_select_fusion.7
  61.7 0.0 copy-done
  61.7 1.9 %fusion.30 = f32[512,256]{0,1:T(8,128)S(1)} fusion(f32[4,1,512,1024]{3,2,1,0:T(8,128)S(1)} %copy-done, f32[512,256]{0,1:T(8,128)S(1)} %get-tuple-element.14, f32[512,256]{0,1:T(8,128)S(1)} %get-tuple-element.13), kind=kOutput, calls=%fused_computation.26 | convolution fusion | flops 1610874880 | bytes 3670016 | tf_op jit(solution)/shard_map/dot_general | solution.py:23
  63.6 0.1 collective-permute-start.2
  63.7 8.0 %collective-permute-done.5 = f32[512,256]{0,1:T(8,128)S(1)} collective-permute-done((f32[512,256]{0,1:T(8,128)S(1)}, f32[512,256]{0,1:T(8,128)S(1)}, u32[]{:S(2)}, u32[]{:S(2)}) %collective-permute-start.5) | collective-permute-done | bytes 524320 | tf_op jit(solution)/shard_map/ppermute | solution.py:16
  71.7 0.1 broadcast_select_fusion.5
  71.8 1.9 %fusion.33 = f32[512,256]{0,1:T(8,128)S(1)} fusion(f32[4,1,512,1024]{3,2,1,0:T(8,128)S(1)} %copy-done, f32[512,256]{0,1:T(8,128)S(1)} %get-tuple-element.21, f32[512,256]{0,1:T(8,128)S(1)} %get-tuple-element.20), kind=kOutput, calls=%fused_computation.27 | convolution fusion | flops 1610874880 | bytes 3670016 | tf_op jit(solution)/shard_map/dot_general | solution.py:23
  73.8 0.7 collective-permute-start.6
  74.4 8.5 %collective-permute-done.2 = f32[512,256]{0,1:T(8,128)S(1)} collective-permute-done((f32[512,256]{0,1:T(8,128)S(1)}, f32[512,256]{0,1:T(8,128)S(1)}, u32[]{:S(2)}, u32[]{:S(2)}) %collective-permute-start.2) | collective-permute-done | bytes 524320 | tf_op jit(solution)/shard_map/ppermute | solution.py:16
  82.9 0.1 broadcast_select_fusion.11
  83.0 2.1 %fusion.36 = f32[512,256]{0,1:T(8,128)S(1)} fusion(f32[4,1,512,1024]{3,2,1,0:T(8,128)S(1)} %copy-done, f32[512,256]{0,1:T(8,128)S(1)} %get-tuple-element.12, f32[512,256]{0,1:T(8,128)S(1)} %get-tuple-element.11), kind=kOutput, calls=%fused_computation.28 | convolution fusion | flops 1610874880 | bytes 3670016 | tf_op jit(solution)/shard_map/dot_general | solution.py:23
  85.2 1.6 %collective-permute-start.3 = (f32[512,256]{0,1:T(8,128)S(1)}, f32[512,256]{0,1:T(8,128)S(1)}, u32[]{:S(2)}, u32[]{:S(2)}) collective-permute-start(f32[512,256]{0,1:T(8,128)S(1)} %fusion.36), channel_id=1, source_target_pairs={{0,2},{2,0},{1,3},{3,1},{4,6},{6,4},{5,7},{7,5},{8,10},{10,8},{9,1... | collective-permute-start | bytes 1572872 | tf_op jit(solution)/shard_map/ppermute | solution.py:16
  86.8 7.3 %collective-permute-done.6 = f32[512,256]{0,1:T(8,128)S(1)} collective-permute-done((f32[512,256]{0,1:T(8,128)S(1)}, f32[512,256]{0,1:T(8,128)S(1)}, u32[]{:S(2)}, u32[]{:S(2)}) %collective-permute-start.6) | collective-permute-done | bytes 524320 | tf_op jit(solution)/shard_map/ppermute | solution.py:16
  94.1 0.1 broadcast_select_fusion.9
  94.2 1.9 %fusion.39 = f32[512,256]{0,1:T(8,128)S(1)} fusion(f32[4,1,512,1024]{3,2,1,0:T(8,128)S(1)} %copy-done, f32[512,256]{0,1:T(8,128)S(1)} %get-tuple-element.19, f32[512,256]{0,1:T(8,128)S(1)} %get-tuple-element.18), kind=kOutput, calls=%fused_computation.29 | convolution fusion | flops 1610874880 | bytes 3670016 | tf_op jit(solution)/shard_map/dot_general | solution.py:23
  96.1 1.6 %collective-permute-start.7 = (f32[512,256]{0,1:T(8,128)S(1)}, f32[512,256]{0,1:T(8,128)S(1)}, u32[]{:S(2)}, u32[]{:S(2)}) collective-permute-start(f32[512,256]{0,1:T(8,128)S(1)} %fusion.39), channel_id=1, source_target_pairs={{0,2},{2,0},{1,3},{3,1},{4,6},{6,4},{5,7},{7,5},{8,10},{10,8},{9,1... | collective-permute-start | bytes 1572872 | tf_op jit(solution)/shard_map/ppermute | solution.py:16
  97.7 1.4 %collective-permute-done.3 = f32[512,256]{0,1:T(8,128)S(1)} collective-permute-done((f32[512,256]{0,1:T(8,128)S(1)}, f32[512,256]{0,1:T(8,128)S(1)}, u32[]{:S(2)}, u32[]{:S(2)}) %collective-permute-start.3) | collective-permute-done | bytes 524320 | tf_op jit(solution)/shard_map/ppermute | solution.py:16
  99.1 0.1 broadcast_select_fusion.15
  99.2 1.9 %fusion.42 = f32[512,256]{0,1:T(8,128)S(1)} fusion(f32[4,1,512,1024]{3,2,1,0:T(8,128)S(1)} %copy-done, f32[512,256]{0,1:T(8,128)S(1)} %get-tuple-element.10, f32[512,256]{0,1:T(8,128)S(1)} %get-tuple-element.9), kind=kOutput, calls=%fused_computation.30 | convolution fusion | flops 1610874880 | bytes 3670016 | tf_op jit(solution)/shard_map/dot_general | solution.py:23
  101.2 9.1 %collective-permute-done.7 = f32[512,256]{0,1:T(8,128)S(1)} collective-permute-done((f32[512,256]{0,1:T(8,128)S(1)}, f32[512,256]{0,1:T(8,128)S(1)}, u32[]{:S(2)}, u32[]{:S(2)}) %collective-permute-start.7) | collective-permute-done | bytes 524320 | tf_op jit(solution)/shard_map/ppermute | solution.py:16
  110.2 0.1 broadcast_select_fusion.13
  110.4 1.9 %fusion.45 = f32[512,256]{0,1:T(8,128)S(1)} fusion(f32[4,1,512,1024]{3,2,1,0:T(8,128)S(1)} %copy-done, f32[512,256]{0,1:T(8,128)S(1)} %get-tuple-element.17, f32[512,256]{0,1:T(8,128)S(1)} %get-tuple-element.16), kind=kOutput, calls=%fused_computation.31 | convolution fusion | flops 1610874880 | bytes 3670016 | tf_op jit(solution)/shard_map/dot_general | solution.py:23
  112.3 0.1 maximum_bitcast_fusion
  112.4 1.3 %copy.3 = f32[1,512,512]{2,1,0:T(8,128)} copy(f32[1,512,512]{1,2,0:T(8,128)S(1)} %maximum_bitcast_fusion) | data formatting | bytes 2097152 | tf_op jit(solution)/shard_map/broadcast_in_dim | solution.py:44
Async XLA Ops:
  1.1 14.9 %collective-permute-start = (f32[512,256]{1,0:T(8,128)S(1)}, f32[512,256]{1,0:T(8,128)S(1)}, u32[]{:S(2)}, u32[]{:S(2)}) collective-permute-start(f32[512,256]{1,0:T(8,128)S(1)} %slice.24), channel_id=1, source_target_pairs={{0,16},{16,0},{1,17},{17,1},{2,18},{18,2},{3,19},{19,3},{4,20},{20... | collective-permute-start | bytes 1572872 | tf_op jit(solution)/shard_map/ppermute | solution.py:16
  17.3 13.2 %collective-permute-start.4 = (f32[512,256]{1,0:T(8,128)S(1)}, f32[512,256]{1,0:T(8,128)S(1)}, u32[]{:S(2)}, u32[]{:S(2)}) collective-permute-start(f32[512,256]{1,0:T(8,128)S(1)} %get-tuple-element.15), channel_id=1, source_target_pairs={{0,16},{16,0},{1,17},{17,1},{2,18},{18,2},{3,19},{19,3},{4,20},{20... | collective-permute-start | bytes 1572872 | tf_op jit(solution)/shard_map/ppermute | solution.py:16
  19.1 42.5 %copy-start = (f32[4,1,512,1024]{3,2,1,0:T(8,128)S(1)}, f32[4,1,512,1024]{3,2,1,0:T(8,128)}, u32[]{:S(2)}) copy-start(f32[4,1,512,1024]{3,2,1,0:T(8,128)} %param.3) | copy-start | bytes 25165828
  24.4 37.1 %collective-permute-start.1 = (f32[512,256]{0,1:T(8,128)S(1)}, f32[512,256]{0,1:T(8,128)S(1)}, u32[]{:S(2)}, u32[]{:S(2)}) collective-permute-start(f32[512,256]{0,1:T(8,128)S(1)} %fusion.24), channel_id=1, source_target_pairs={{0,8},{8,0},{1,9},{9,1},{2,10},{10,2},{3,11},{11,3},{4,12},{12,4},... | collective-permute-start | bytes 1572872 | tf_op jit(solution)/shard_map/ppermute | solution.py:16
  36.9 34.8 %collective-permute-start.5 = (f32[512,256]{0,1:T(8,128)S(1)}, f32[512,256]{0,1:T(8,128)S(1)}, u32[]{:S(2)}, u32[]{:S(2)}) collective-permute-start(f32[512,256]{0,1:T(8,128)S(1)} %fusion.27), channel_id=1, source_target_pairs={{0,8},{8,0},{1,9},{9,1},{2,10},{10,2},{3,11},{11,3},{4,12},{12,4},... | collective-permute-start | bytes 1572872 | tf_op jit(solution)/shard_map/ppermute | solution.py:16
  63.6 19.3 %collective-permute-start.2 = (f32[512,256]{0,1:T(8,128)S(1)}, f32[512,256]{0,1:T(8,128)S(1)}, u32[]{:S(2)}, u32[]{:S(2)}) collective-permute-start(f32[512,256]{0,1:T(8,128)S(1)} %fusion.30), channel_id=1, source_target_pairs={{0,4},{4,0},{1,5},{5,1},{2,6},{6,2},{3,7},{7,3},{8,12},{12,8},{9,1... | collective-permute-start | bytes 1572872 | tf_op jit(solution)/shard_map/ppermute | solution.py:16
  73.8 20.3 %collective-permute-start.6 = (f32[512,256]{0,1:T(8,128)S(1)}, f32[512,256]{0,1:T(8,128)S(1)}, u32[]{:S(2)}, u32[]{:S(2)}) collective-permute-start(f32[512,256]{0,1:T(8,128)S(1)} %fusion.33), channel_id=1, source_target_pairs={{0,4},{4,0},{1,5},{5,1},{2,6},{6,2},{3,7},{7,3},{8,12},{12,8},{9,1... | collective-permute-start | bytes 1572872 | tf_op jit(solution)/shard_map/ppermute | solution.py:16
  85.2 13.9 %collective-permute-start.3 = (f32[512,256]{0,1:T(8,128)S(1)}, f32[512,256]{0,1:T(8,128)S(1)}, u32[]{:S(2)}, u32[]{:S(2)}) collective-permute-start(f32[512,256]{0,1:T(8,128)S(1)} %fusion.36), channel_id=1, source_target_pairs={{0,2},{2,0},{1,3},{3,1},{4,6},{6,4},{5,7},{7,5},{8,10},{10,8},{9,1... | collective-permute-start | bytes 1572872 | tf_op jit(solution)/shard_map/ppermute | solution.py:16
  96.1 14.1 %collective-permute-start.7 = (f32[512,256]{0,1:T(8,128)S(1)}, f32[512,256]{0,1:T(8,128)S(1)}, u32[]{:S(2)}, u32[]{:S(2)}) collective-permute-start(f32[512,256]{0,1:T(8,128)S(1)} %fusion.39), channel_id=1, source_target_pairs={{0,2},{2,0},{1,3},{3,1},{4,6},{6,4},{5,7},{7,5},{8,10},{10,8},{9,1... | collective-permute-start | bytes 1572872 | tf_op jit(solution)/shard_map/ppermute | solution.py:16
where the time goes:
time: 114 us
  waiting for transfers between devices  71.7 us (63%)
  matrix products  22.3 us (20%)
  starting transfers between devices  14 us (12%)
  other arithmetic  3.19 us (3%)
  local copies, waits for them, and re-layouts  2.39 us (2%)
    ppermute x8, waiting for transfers between devices, from_partner(): return lax.ppermute(block, axis, route)  71.7 us
    dot_general x8, matrix products, apply_level(): jnp.dot(matrix, stacked, precision=lax.Precision.HIGHEST, preferred_eleme...  22.3 us
    ppermute x8, starting transfers between devices, from_partner(): return lax.ppermute(block, axis, route)  14 us
    select_n x8, other arithmetic, apply_level(): lower_part = jnp.where(upper == 1, other, own)  3.12 us
  transfers between devices with their start and end apart: 8, of which 8 were waited for; matrix products, arithmetic and copies ran while one was open for 19% of the time, Pallas kernels for 0%

commit v1 on v0

v1 whole, which is shorter than its diff:
```python
import jax
import jax.numpy as jnp
from jax import lax
from jax.experimental import pallas as pl
from jax.experimental.pallas import tpu as pltpu
from jax.sharding import PartitionSpec as P

AXES = ("gx", "gy", "gz")
F32, BF16 = jnp.float32, jnp.bfloat16
VMEM = pl.BlockSpec(memory_space=pltpu.VMEM)
HBM = pl.BlockSpec(memory_space=pltpu.HBM)
ANY = pl.BlockSpec(memory_space=pl.ANY)
CHUNKS = (2, 3, 3, 4, 4)
X_GROUPS = ((0,), (1,), (2,), (3,), (4,))
Z_GROUPS = ((0,), (1,), (2,), (3,), (4,))
Y_GROUPS = ((0,), (1,), (2,), (3,), (4,))
DIRECT = (0,)
RESULT_BLOCKS = ((0, 3), (3, 4))
COST = 4000000000
ORDER = (
    "in0 x0 in1 x1",
    "x2 m0 a0 m2",
    "x3 x4 m1 a1",
    "a2 b0 p1 a3",
    "p2 a4 q1 p3",
    "p4 m3 q2 q3",
    "c0 b1 q4 b2",
    "c1 b3 c2 b4",
    "c3 c4 d0 d1",
)


def bit_of(bit):
    index = lax.axis_index(AXES[0])
    for axis in AXES[1:]:
        index = index * lax.axis_size(axis) + lax.axis_index(axis)
    return index >> bit & 1


def send(block, partner):
    count = lax.axis_size(AXES)
    return lax.ppermute(block, AXES, [(i, partner(i)) for i in range(count)])


def split(x):
    high = x.astype(BF16)
    return high, (x - high.astype(F32)).astype(BF16)


def dot_t(a, b):
    return lax.dot_general(a, b, (((1,), (1,)), ((), ())), preferred_element_type=F32)


def product(x, mh, ml):
    rows = x.shape[0]
    xh, xl = split(x)
    both = dot_t(jnp.concatenate([xh, xl], axis=0), mh)
    return both[:rows] + (both[rows:] + dot_t(xh, ml))


def product_t(x, mh, ml):
    rows = x.shape[0]
    xh, xl = split(x)
    both = dot_t(mh, jnp.concatenate([xh, xl], axis=0))
    return both[:, :rows] + (both[:, rows:] + dot_t(ml, xh))


def stacked(own, other, upper):
    return jnp.concatenate(
        [jnp.where(upper == 1, other, own), jnp.where(upper == 1, own, other)], axis=1
    )


def joined(blocks):
    return blocks[0] if len(blocks) == 1 else jnp.concatenate(blocks, axis=0)


class Chain:
    def __init__(self):
        self.last = None

    def __call__(self, name, body, args, outs, scratch=(), in_place=None, in_hbm=(), out_hbm=False):
        args, n = list(args), len(args)
        specs = [VMEM] * n
        for i in in_hbm:
            args[i] = pltpu.with_memory_space_constraint(args[i], pltpu.HBM)
            specs[i] = HBM
        if in_place is not None:
            specs[in_place] = HBM if out_hbm else ANY
        if self.last is not None and not any(a is self.last for a in args):
            args.append(self.last)
            specs.append(ANY)

        def kernel(*refs):
            body(*refs[:n], *refs[len(args) :])

        results = pl.pallas_call(
            kernel,
            out_shape=outs,
            in_specs=specs,
            out_specs=[HBM, VMEM] if out_hbm else [VMEM if in_place is None else ANY] * len(outs),
            scratch_shapes=scratch,
            input_output_aliases={} if in_place is None else {in_place: 0},
            compiler_params=pltpu.CompilerParams(vmem_limit_bytes=8 * 2**20),
            cost_estimate=pl.CostEstimate(
                flops=COST, bytes_accessed=1000, transcendentals=0
            ),
            name=name,
        )(*args)
        self.last = results[-1]
        return list(results)


def per_device(coeffs, transfer):
    nbits = lax.axis_size(AXES).bit_length() - 1
    bits = [nbits - 1 - level for level in range(transfer.shape[0])]
    rank, rhs = coeffs.shape[1:]
    sizes = [c * rhs // 16 for c in CHUNKS]
    n = len(sizes)
    ends = [sum(sizes[: s + 1]) for s in range(n)]
    unit = rhs // 4
    chain = Chain()

    def rows(chunks):
        return jax.ShapeDtypeStruct((sum(sizes[k] for k in chunks), rank), F32)

    def across(level):
        return lambda i: i ^ 1 << bits[level]

    def middle(i):
        both = 1 << bits[1] | 1 << bits[2]
        return i ^ both if (i >> bits[1] ^ i >> bits[2]) & 1 else i ^ 1

    def is_middle():
        return bit_of(bits[1]) != bit_of(bits[2])

    def pieces(store, chunks):
        found = []
        for group, array in store.items():
            at = 0
            for k in group:
                if k in chunks:
                    if found and found[-1][0] is array:
                        found[-1][1][1] = at + sizes[k]
                    else:
                        found.append((array, [at, at + sizes[k]]))
                at += sizes[k]
        return found

    def step_in(part):
        mine = [g for i, g in enumerate(X_GROUPS) if (i == 0) == (part == 0)]
        start = ends[mine[0][0]] - sizes[mine[0][0]]
        width = sum(sizes[k] for g in mine for k in g)
        low = start // 128 * 128
        high = -(-(start + width) // 128) * 128

        def fetched(c_ref, *refs):
            outs, (held, sem) = refs[:-2], refs[-2:]
            copy = pltpu.make_async_copy(c_ref.at[0, :, low:high], held, sem)
            copy.start()
            copy.wait()
            lay(held[...], start - low, outs)

        def whole(c_ref, *outs):
            lay(c_ref[0], start, outs)

        def lay(block, at, outs):
            for o_ref in outs:
                o_ref[...] = block[:, at : at + o_ref.shape[0]].T
                at += o_ref.shape[0]

        scratch = [pltpu.VMEM((rank, high - low), F32), pltpu.SemaphoreType.DMA]
        out = chain(
            "columns",
            whole if part else fetched,
            [coeffs],
            [rows(g) for g in mine],
            scratch=[] if part else scratch,
            in_hbm=[] if part else [0],
        )
        c0.update(zip(mine, out))

    def step_m(level):
        def body(t_ref, h_ref, l_ref):
            h_ref[...], l_ref[...] = split(t_ref[level, 0])

        matrix[level] = chain(
            "matrix",
            body,
            [transfer],
            [jax.ShapeDtypeStruct((rank, 2 * rank), BF16)] * 2,
        )

    def step_x(i):
        group = X_GROUPS[i]
        c0[group] = chain("order", lambda *_: None, [c0[group]], [rows(group)], in_place=0)[0]
        x[group] = send(c0[group], across(0))

    def level(name, number, mine, other, outs):
        args = [p[0] for p in mine] + [a for p in other for a in p[:-1]]

        def body(*refs):
            out_refs = refs[len(args) + 2 :]
            h, l = refs[len(args) : len(args) + 2]
            own = joined([r[slice(*p[-1])] for r, p in zip(refs, mine)])
            at, blocks = len(mine), []
            for p in other:
                block = refs[at][slice(*p[-1])]
                if len(p) == 3:
                    block = jnp.where(is_middle(), block, refs[at + 1][slice(*p[-1])])
                at += len(p) - 1
                blocks.append(block)
            y = product(stacked(own, joined(blocks), bit_of(bits[number])), h[...], l[...])
            at = 0
            for o in out_refs:
                o[...] = y[at : at + o.shape[0]]
                at += o.shape[0]

        return chain(name, body, args + matrix[number], outs)

    def step_a(i):
        group = X_GROUPS[i]
        out = level(
            "level0",
            0,
            pieces(c0, group),
            pieces(x, group),
            [rows([k]) for k in group],
        )
        for k, c in zip(group, out):
            c1[(k,)] = c
            if k in DIRECT:
                got[k] = (send(c, across(1)),)
            else:
                got[k] = send(c, middle)

    def step_p(k):
        def body(own, other, o_ref):
            o_ref[...] = jnp.where(is_middle(), other[...], own[...])

        passed = chain("pass", body, [c1[(k,)], got[k]], [rows([k])])[0]
        got[k] = send(passed, across(2))

    def step_q(k):
        kept = chain("order", lambda *_: None, [got[k]], [rows([k])], in_place=0)[0]
        got[k] = (send(kept, middle), kept)

    def step_b(i):
        group = Z_GROUPS[i]
        other = [(*got[k], [0, sizes[k]]) for k in group]
        c2[group] = level("level1", 1, pieces(c1, group), other, [rows(group)])[0]
        z[group] = send(c2[group], across(2))

    def step_c(i):
        group = Y_GROUPS[i]
        c3[group] = level("level2", 2, pieces(c2, group), pieces(z, group), [rows(group)])[0]
        y[group] = send(c3[group], across(3))

    def step_d(j):
        first, stop = (b * unit for b in RESULT_BLOCKS[j])
        args, cuts = [], []
        for store in (c3, y):
            for group in Y_GROUPS:
                begin = ends[group[0]] - sizes[group[0]]
                cut = slice(max(first - begin, 0), min(stop, ends[group[-1]]) - begin)
                if cut.start < cut.stop:
                    args.append(store[group])
                    cuts.append(cut)
        p = len(args) // 2

        def body(*refs):
            held, sem = refs[-2:]
            h, l, o_ref, mark = refs[2 * p], refs[2 * p + 1], refs[-4], refs[-3]
            mark[...] = jnp.zeros_like(mark)
            own = joined([r[cut] for r, cut in zip(refs[:p], cuts)])
            other = joined([r[cut] for r, cut in zip(refs[p:], cuts[p:])])
            both = stacked(own, other, bit_of(bits[3]))
            copies = []
            for half in range(2):
                part = slice(half * rank // 2, (half + 1) * rank // 2)
                held[part] = product_t(both, h[part], l[part])
                copies.append(
                    pltpu.make_async_copy(
                        held.at[part], o_ref.at[0, part, first:stop], sem.at[half]
                    )
                )
                copies[-1].start()
            for copy in copies:
                copy.wait()

        args += matrix[3]
        in_place = None
        if result:
            in_place = len(args)
            args.append(result[-1])
        result.append(
            chain(
                "level3",
                body,
                args,
                [pltpu.HBM(coeffs.shape, F32), jax.ShapeDtypeStruct((8, 128), F32)],
                scratch=[
                    pltpu.VMEM((rank, stop - first), F32),
                    pltpu.SemaphoreType.DMA((2,)),
                ],
                in_place=in_place,
                out_hbm=True,
            )[0]
        )

    c0, x, c1, got, c2, z, c3, y, matrix, result = ({} for _ in range(10))
    result = []
    steps = {"in": step_in, "m": step_m, "x": step_x, "a": step_a, "p": step_p}
    steps |= {"q": step_q, "b": step_b, "c": step_c, "d": step_d}
    for words in ORDER:
        for word in words.split():
            steps[word[:-1]](int(word[-1]))
    return result[-1]


def solution(mesh):
    placed = (P(AXES, None, None), P(None, AXES, None, None))
    return jax.shard_map(
        per_device,
        mesh=mesh,
        in_specs=placed,
        out_specs=P(AXES, None, None),
        check_vma=False,
    )
```

time: 114 us -> 75.9 us (0.67)
  waiting for transfers between devices: 71.7 us -> 13.2 us
  starting transfers between devices: 14 us -> 42 us
  matrix products: 22.3 us -> 0 us
  Pallas kernels: 0 us -> 18.9 us
  other arithmetic: 3.19 us -> 0.01 us
    ppermute x8 -> x28, waiting for transfers between devices: 71.7 us -> 13.2 us  [send(): return lax.ppermute(block, AXES, [(i, partner(i)) for i in range(count)])]
    ppermute x8 -> x28, starting transfers between devices: 14 us -> 42 us  [send(): return lax.ppermute(block, AXES, [(i, partner(i)) for i in range(count)])]
    dot_general x8 -> x0, matrix products: 22.3 us -> none  [apply_level(): jnp.dot(matrix, stacked, precision=lax.Precision.HIGHEST, preferred_eleme...]
    pallas_call x0 -> x36, Pallas kernels: none -> 18.9 us  [__call__(): pl.pallas_call(kernel, out_shape=outs, in_specs=specs, out_specs=[HBM, VM...]
    select_n x8 -> x0, other arithmetic: 3.12 us -> none  [apply_level(): lower_part = jnp.where(upper == 1, other, own)]
    unnamed x2 -> x6, local copies, waits for them, and re-layouts: 0.01 us -> 1.36 us
    broadcast_in_dim x1 -> x0, local copies, waits for them, and re-layouts: 1.31 us -> none  [per_device(): return current[None]]
  transfers between devices with their start and end apart: 8 -> 28, of which waited for: 8 -> 8; matrix products, arithmetic and copies ran while one was open for 19% -> 0% of each run, Pallas kernels for 0% -> 21%
where the time goes in v1:
time: 75.9 us; the launch traced here: 75.8 us
  starting transfers between devices  42 us (55%)
  Pallas kernels  18.9 us (25%)
  waiting for transfers between devices  13.2 us (17%)
  local copies, waits for them, and re-layouts  1.36 us (2%)
    ppermute x28, starting transfers between devices, send(): return lax.ppermute(block, AXES, [(i, partner(i)) for i in range(count)])  42 us
    pallas_call x36, Pallas kernels, __call__(): pl.pallas_call(kernel, out_shape=outs, in_specs=specs, out_specs=[HBM, VM...  18.9 us
    ppermute x28, waiting for transfers between devices, send(): return lax.ppermute(block, AXES, [(i, partner(i)) for i in range(count)])  13.2 us
  transfers between devices with their start and end apart: 28, of which 8 were waited for; matrix products, arithmetic and copies ran while one was open for 0% of the time, Pallas kernels for 21%

profile of v1, /device:TPU:0, one launch (start us, length us, event | category | flops | bytes accessed | tf_op | source)
XLA Modules:
  0.0 75.8 jit_solution(4751364569585393591)
XLA Ops:
  0.0 1.1 %columns.2.refs_0_ = f32[64,512]{1,0:T(8,128)S(1)} custom-call(f32[1,512,512]{2,1,0:T(8,128)} %refs_0_.7), custom_call_target="tpu_custom_call" | custom-call | flops 4000000000 | bytes 1000 | tf_op jit(solution)/shard_map/columns/pallas_call | solution.py:97
  1.1 3.0 %collective-permute-start = (f32[64,512]{1,0:T(8,128)S(1)}, f32[64,512]{1,0:T(8,128)S(1)}, u32[]{:S(2)}, u32[]{:S(2)}) collective-permute-start(f32[64,512]{1,0:T(8,128)S(1)} %order.9.refs_1_.refs_0_), channel_id=1, source_target_pairs={{0,16},{1,17},{2,18},{3,19},{4,20},{5,21},{6,22},{7,23},{8,24},{9,... | collective-permute-start | bytes 393224 | tf_op jit(solution)/shard_map/ppermute | solution.py:42
  4.1 0.6 columns.3
  4.7 1.2 %collective-permute-start.3 = (f32[96,512]{1,0:T(8,128)S(1)}, f32[96,512]{1,0:T(8,128)S(1)}, u32[]{:S(2)}, u32[]{:S(2)}) collective-permute-start(f32[96,512]{1,0:T(8,128)S(1)} %order.10.refs_1_.refs_0_), channel_id=1, source_target_pairs={{0,16},{1,17},{2,18},{3,19},{4,20},{5,21},{6,22},{7,23},{8,24},{9,... | collective-permute-start | bytes 589832 | tf_op jit(solution)/shard_map/ppermute | solution.py:42
  5.9 0.9 %collective-permute-start.2 = (f32[96,512]{1,0:T(8,128)S(1)}, f32[96,512]{1,0:T(8,128)S(1)}, u32[]{:S(2)}, u32[]{:S(2)}) collective-permute-start(f32[96,512]{1,0:T(8,128)S(1)} %order.11.refs_1_.refs_0_), channel_id=1, source_target_pairs={{0,16},{1,17},{2,18},{3,19},{4,20},{5,21},{6,22},{7,23},{8,24},{9,... | collective-permute-start | bytes 589832 | tf_op jit(solution)/shard_map/ppermute | solution.py:42
  6.9 1.3 %slice-done.1 = s8[4194304]{0:T(1024)(128)(4,1)S(1)} async-done(((s8[8388608]{0:T(1024)(128)(4,1)}), s8[4194304]{0:T(1024)(128)(4,1)S(1)}, s32[]{:S(2)}) %slice-start.1) | async-done | bytes 4194328
  8.5 0.8 %level0.5.refs_1_.refs_0_ = f32[64,512]{1,0:T(8,128)S(1)} custom-call(f32[64,512]{1,0:T(8,128)S(1)} %order.9.refs_1_.refs_0_, f32[64,512]{1,0:T(8,128)S(1)} %collective-permute-done.refs_1_, bf16[512,1024]{1,0:T(8,128)(2,1)S(1)} %get-tuple-element.24.refs_2_, bf16[512,1024]{1,0:T(8,128)(2,1)S(1)} %get-tuple-element.25.refs_3_), custom_call_target="tpu_custom_call" | custom-call | flops 4000000000 | bytes 1000 | tf_op jit(solution)/shard_map/level0/pallas_call | solution.py:97
  9.5 3.0 %collective-permute-start.7 = (f32[64,512]{1,0:T(8,128)S(1)}, f32[64,512]{1,0:T(8,128)S(1)}, u32[]{:S(2)}, u32[]{:S(2)}) collective-permute-start(f32[64,512]{1,0:T(8,128)S(1)} %level0.5.refs_1_.refs_0_), channel_id=1, source_target_pairs={{0,8},{1,9},{2,10},{3,11},{4,12},{5,13},{6,14},{7,15},{8,0},{9,1},... | collective-permute-start | bytes 393224 | tf_op jit(solution)/shard_map/ppermute | solution.py:42
  12.6 1.6 %collective-permute-start.5 = (f32[128,512]{1,0:T(8,128)S(1)}, f32[128,512]{1,0:T(8,128)S(1)}, u32[]{:S(2)}, u32[]{:S(2)}) collective-permute-start(f32[128,512]{1,0:T(8,128)S(1)} %order.12.refs_1_.refs_0_), channel_id=1, source_target_pairs={{0,16},{1,17},{2,18},{3,19},{4,20},{5,21},{6,22},{7,23},{8,24},{9,... | collective-permute-start | bytes 786440 | tf_op jit(solution)/shard_map/ppermute | solution.py:42
  14.9 0.8 %level0.6.refs_4_.refs_0_ = f32[96,512]{1,0:T(8,128)S(1)} custom-call(f32[96,512]{1,0:T(8,128)S(1)} %order.10.refs_1_.refs_0_, f32[96,512]{1,0:T(8,128)S(1)} %collective-permute-done.3.refs_1_, bf16[512,1024]{1,0:T(8,128)(2,1)S(1)} %get-tuple-element.24.refs_2_, bf16[512,1024]{1,0:T(8,128)(2,1)S(1)} %get-tuple-element.25.refs_3_, ...), custom_call_target="tpu_custom_call" | custom-call | flops 4000000000 | bytes 1000 | tf_op jit(solution)/shard_map/level0/pallas_call | solution.py:97
  15.8 1.0 %collective-permute-done.2.refs_1_ = f32[96,512]{1,0:T(8,128)S(1)} collective-permute-done((f32[96,512]{1,0:T(8,128)S(1)}, f32[96,512]{1,0:T(8,128)S(1)}, u32[]{:S(2)}, u32[]{:S(2)}) %collective-permute-start.2) | collective-permute-done | bytes 196640 | tf_op jit(solution)/shard_map/ppermute | solution.py:42
  16.8 0.8 %level0.7.refs_4_.refs_0_ = f32[96,512]{1,0:T(8,128)S(1)} custom-call(f32[96,512]{1,0:T(8,128)S(1)} %order.11.refs_1_.refs_0_, f32[96,512]{1,0:T(8,128)S(1)} %collective-permute-done.2.refs_1_, bf16[512,1024]{1,0:T(8,128)(2,1)S(1)} %get-tuple-element.24.refs_2_, bf16[512,1024]{1,0:T(8,128)(2,1)S(1)} %get-tuple-element.25.refs_3_, ...), custom_call_target="tpu_custom_call" | custom-call | flops 4000000000 | bytes 1000 | tf_op jit(solution)/shard_map/level0/pallas_call | solution.py:97
  17.7 1.1 %collective-permute-done.7.refs_1_ = f32[64,512]{1,0:T(8,128)S(1)} collective-permute-done((f32[64,512]{1,0:T(8,128)S(1)}, f32[64,512]{1,0:T(8,128)S(1)}, u32[]{:S(2)}, u32[]{:S(2)}) %collective-permute-start.7) | collective-permute-done | bytes 131104 | tf_op jit(solution)/shard_map/ppermute | solution.py:42
  18.8 0.8 %level1.5.refs_2_.refs_0_ = f32[64,512]{1,0:T(8,128)S(1)} custom-call(f32[64,512]{1,0:T(8,128)S(1)} %level0.5.refs_1_.refs_0_, f32[64,512]{1,0:T(8,128)S(1)} %collective-permute-done.7.refs_1_, bf16[512,1024]{1,0:T(8,128)(2,1)S(1)} %get-tuple-element.28.refs_2_.refs_3_, bf16[512,1024]{1,0:T(8,128)(2,1)S(1)} %get-tuple-element.27.refs_4_.refs_3_, ...), custom_call_target="tpu_custom_call" | custom-call | flops 4000000000 | bytes 1000 | tf_op jit(solution)/shard_map/level1/pallas_call | solution.py:97
  19.5 2.6 %collective-permute-start.13 = (f32[64,512]{1,0:T(8,128)S(1)}, f32[64,512]{1,0:T(8,128)S(1)}, u32[]{:S(2)}, u32[]{:S(2)}) collective-permute-start(f32[64,512]{1,0:T(8,128)S(1)} %level1.5.refs_2_.refs_0_), channel_id=1, source_target_pairs={{0,4},{1,5},{2,6},{3,7},{4,0},{5,1},{6,2},{7,3},{8,12},{9,13},{10,... | collective-permute-start | bytes 393224 | tf_op jit(solution)/shard_map/ppermute | solution.py:42
  22.2 3.1 %collective-permute-start.10 = (f32[96,512]{1,0:T(8,128)S(1)}, f32[96,512]{1,0:T(8,128)S(1)}, u32[]{:S(2)}, u32[]{:S(2)}) collective-permute-start(f32[96,512]{1,0:T(8,128)S(1)} %pass.4.refs_4_), channel_id=1, source_target_pairs={{0,4},{1,5},{2,6},{3,7},{4,0},{5,1},{6,2},{7,3},{8,12},{9,13},{10,... | collective-permute-start | bytes 589832 | tf_op jit(solution)/shard_map/ppermute | solution.py:42
  25.3 0.8 level0.8.refs_2_.refs_0_
  26.2 1.8 %collective-permute-start.15 = (f32[96,512]{1,0:T(8,128)S(1)}, f32[96,512]{1,0:T(8,128)S(1)}, u32[]{:S(2)}, u32[]{:S(2)}) collective-permute-start(f32[96,512]{1,0:T(8,128)S(1)} %pass.5.refs_4_), channel_id=1, source_target_pairs={{0,4},{1,5},{2,6},{3,7},{4,0},{5,1},{6,2},{7,3},{8,12},{9,13},{10,... | collective-permute-start | bytes 589832 | tf_op jit(solution)/shard_map/ppermute | solution.py:42
  27.9 0.7 level0.9.refs_1_.refs_0_
  28.7 1.3 %collective-permute-done.10.refs_0_ = f32[96,512]{1,0:T(8,128)S(1)} collective-permute-done((f32[96,512]{1,0:T(8,128)S(1)}, f32[96,512]{1,0:T(8,128)S(1)}, u32[]{:S(2)}, u32[]{:S(2)}) %collective-permute-start.10) | collective-permute-done | bytes 196640 | tf_op jit(solution)/shard_map/ppermute | solution.py:42
  30.1 3.8 %collective-permute-start.14 = (f32[128,512]{1,0:T(8,128)S(1)}, f32[128,512]{1,0:T(8,128)S(1)}, u32[]{:S(2)}, u32[]{:S(2)}) collective-permute-start(f32[128,512]{1,0:T(8,128)S(1)} %pass.6.refs_2_), channel_id=1, source_target_pairs={{0,4},{1,5},{2,6},{3,7},{4,0},{5,1},{6,2},{7,3},{8,12},{9,13},{10,... | collective-permute-start | bytes 786440 | tf_op jit(solution)/shard_map/ppermute | solution.py:42
  34.0 5.6 %collective-permute-start.11 = (f32[128,512]{1,0:T(8,128)S(1)}, f32[128,512]{1,0:T(8,128)S(1)}, u32[]{:S(2)}, u32[]{:S(2)}) collective-permute-start(f32[128,512]{1,0:T(8,128)S(1)} %pass.7.refs_1_), channel_id=1, source_target_pairs={{0,4},{1,5},{2,6},{3,7},{4,0},{5,1},{6,2},{7,3},{8,12},{9,13},{10,... | collective-permute-start | bytes 786440 | tf_op jit(solution)/shard_map/ppermute | solution.py:42
  40.0 0.5 collective-permute-start.19
  40.5 0.8 %level2.5.refs_5_.refs_0_ = f32[64,512]{1,0:T(8,128)S(1)} custom-call(f32[64,512]{1,0:T(8,128)S(1)} %level1.5.refs_2_.refs_0_, f32[64,512]{1,0:T(8,128)S(1)} %collective-permute-done.13.refs_1_, bf16[512,1024]{1,0:T(8,128)(2,1)S(1)} %get-tuple-element.29.refs_2_, bf16[512,1024]{1,0:T(8,128)(2,1)S(1)} %get-tuple-element.26.refs_1_.refs_3_, ...), custom_call_target="tpu_custom_call" | custom-call | flops 4000000000 | bytes 1000 | tf_op jit(solution)/shard_map/level2/pallas_call | solution.py:97
  41.2 1.6 %collective-permute-start.24 = (f32[64,512]{1,0:T(8,128)S(1)}, f32[64,512]{1,0:T(8,128)S(1)}, u32[]{:S(2)}, u32[]{:S(2)}) collective-permute-start(f32[64,512]{1,0:T(8,128)S(1)} %level2.5.refs_5_.refs_0_), channel_id=1, source_target_pairs={{0,2},{1,3},{2,0},{3,1},{4,6},{5,7},{6,4},{7,5},{8,10},{9,11},{10,... | collective-permute-start | bytes 393224 | tf_op jit(solution)/shard_map/ppermute | solution.py:42
  42.8 0.8 %level1.6.refs_1_.refs_0_ = f32[96,512]{1,0:T(8,128)S(1)} custom-call(f32[96,512]{1,0:T(8,128)S(1)} %level0.6.refs_4_.refs_0_, f32[96,512]{1,0:T(8,128)S(1)} %collective-permute-done.12.refs_1_, f32[96,512]{1,0:T(8,128)S(1)} %order.14.refs_2_, bf16[512,1024]{1,0:T(8,128)(2,1)S(1)} %get-tuple-element.28.refs_2_.refs_3_, ...), custom_call_target="tpu_custom_call" | custom-call | flops 4000000000 | bytes 1000 | tf_op jit(solution)/shard_map/level1/pallas_call | solution.py:97
  43.6 2.7 %collective-permute-start.20 = (f32[96,512]{1,0:T(8,128)S(1)}, f32[96,512]{1,0:T(8,128)S(1)}, u32[]{:S(2)}, u32[]{:S(2)}) collective-permute-start(f32[96,512]{1,0:T(8,128)S(1)} %level1.6.refs_1_.refs_0_), channel_id=1, source_target_pairs={{0,4},{1,5},{2,6},{3,7},{4,0},{5,1},{6,2},{7,3},{8,12},{9,13},{10,... | collective-permute-start | bytes 589832 | tf_op jit(solution)/shard_map/ppermute | solution.py:42
  46.4 0.8 %level1.7.refs_4_.refs_0_ = f32[96,512]{1,0:T(8,128)S(1)} custom-call(f32[96,512]{1,0:T(8,128)S(1)} %level0.7.refs_4_.refs_0_, f32[96,512]{1,0:T(8,128)S(1)} %collective-permute-done.17.refs_1_, f32[96,512]{1,0:T(8,128)S(1)} %order.15.refs_1_.refs_2_, bf16[512,1024]{1,0:T(8,128)(2,1)S(1)} %get-tuple-element.28.refs_2_.refs_3_, ...), custom_call_target="tpu_custom_call" | custom-call | flops 4000000000 | bytes 1000 | tf_op jit(solution)/shard_map/level1/pallas_call | solution.py:97
  47.2 2.4 %collective-permute-start.18 = (f32[96,512]{1,0:T(8,128)S(1)}, f32[96,512]{1,0:T(8,128)S(1)}, u32[]{:S(2)}, u32[]{:S(2)}) collective-permute-start(f32[96,512]{1,0:T(8,128)S(1)} %level1.7.refs_4_.refs_0_), channel_id=1, source_target_pairs={{0,4},{1,5},{2,6},{3,7},{4,0},{5,1},{6,2},{7,3},{8,12},{9,13},{10,... | collective-permute-start | bytes 589832 | tf_op jit(solution)/shard_map/ppermute | solution.py:42
  49.6 1.1 %collective-permute-done.20.refs_1_ = f32[96,512]{1,0:T(8,128)S(1)} collective-permute-done((f32[96,512]{1,0:T(8,128)S(1)}, f32[96,512]{1,0:T(8,128)S(1)}, u32[]{:S(2)}, u32[]{:S(2)}) %collective-permute-start.20) | collective-permute-done | bytes 196640 | tf_op jit(solution)/shard_map/ppermute | solution.py:42
  50.7 0.8 %level2.6.refs_5_.refs_1_ = f32[96,512]{1,0:T(8,128)S(1)} custom-call(f32[96,512]{1,0:T(8,128)S(1)} %level1.6.refs_1_.refs_0_, f32[96,512]{1,0:T(8,128)S(1)} %collective-permute-done.20.refs_1_, bf16[512,1024]{1,0:T(8,128)(2,1)S(1)} %get-tuple-element.29.refs_2_, bf16[512,1024]{1,0:T(8,128)(2,1)S(1)} %get-tuple-element.26.refs_1_.refs_3_, ...), custom_call_target="tpu_custom_call" | custom-call | flops 4000000000 | bytes 1000 | tf_op jit(solution)/shard_map/level2/pallas_call | solution.py:97
  51.5 1.1 %collective-permute-start.25 = (f32[96,512]{1,0:T(8,128)S(1)}, f32[96,512]{1,0:T(8,128)S(1)}, u32[]{:S(2)}, u32[]{:S(2)}) collective-permute-start(f32[96,512]{1,0:T(8,128)S(1)} %level2.6.refs_5_.refs_1_), channel_id=1, source_target_pairs={{0,2},{1,3},{2,0},{3,1},{4,6},{5,7},{6,4},{7,5},{8,10},{9,11},{10,... | collective-permute-start | bytes 589832 | tf_op jit(solution)/shard_map/ppermute | solution.py:42
  52.6 0.8 %level1.8.refs_4_.refs_0_ = f32[128,512]{1,0:T(8,128)S(1)} custom-call(f32[128,512]{1,0:T(8,128)S(1)} %level0.8.refs_2_.refs_0_, f32[128,512]{1,0:T(8,128)S(1)} %collective-permute-done.19.refs_1_, f32[128,512]{1,0:T(8,128)S(1)} %order.16.refs_4_.refs_2_, bf16[512,1024]{1,0:T(8,128)(2,1)S(1)} %get-tuple-element.28.refs_2_.refs_3_, ...), custom_call_target="tpu_custom_call" | custom-call | flops 4000000000 | bytes 1000 | tf_op jit(solution)/shard_map/level1/pallas_call | solution.py:97
  53.3 2.0 %collective-permute-start.22 = (f32[128,512]{1,0:T(8,128)S(1)}, f32[128,512]{1,0:T(8,128)S(1)}, u32[]{:S(2)}, u32[]{:S(2)}) collective-permute-start(f32[128,512]{1,0:T(8,128)S(1)} %level1.8.refs_4_.refs_0_), channel_id=1, source_target_pairs={{0,4},{1,5},{2,6},{3,7},{4,0},{5,1},{6,2},{7,3},{8,12},{9,13},{10,... | collective-permute-start | bytes 786440 | tf_op jit(solution)/shard_map/ppermute | solution.py:42
  55.4 0.8 %level2.7.refs_5_.refs_2_ = f32[96,512]{1,0:T(8,128)S(1)} custom-call(f32[96,512]{1,0:T(8,128)S(1)} %level1.7.refs_4_.refs_0_, f32[96,512]{1,0:T(8,128)S(1)} %collective-permute-done.18.refs_1_, bf16[512,1024]{1,0:T(8,128)(2,1)S(1)} %get-tuple-element.29.refs_2_, bf16[512,1024]{1,0:T(8,128)(2,1)S(1)} %get-tuple-element.26.refs_1_.refs_3_, ...), custom_call_target="tpu_custom_call" | custom-call | flops 4000000000 | bytes 1000 | tf_op jit(solution)/shard_map/level2/pallas_call | solution.py:97
  56.2 1.6 %collective-permute-start.26 = (f32[96,512]{1,0:T(8,128)S(1)}, f32[96,512]{1,0:T(8,128)S(1)}, u32[]{:S(2)}, u32[]{:S(2)}) collective-permute-start(f32[96,512]{1,0:T(8,128)S(1)} %level2.7.refs_5_.refs_2_), channel_id=1, source_target_pairs={{0,2},{1,3},{2,0},{3,1},{4,6},{5,7},{6,4},{7,5},{8,10},{9,11},{10,... | collective-permute-start | bytes 589832 | tf_op jit(solution)/shard_map/ppermute | solution.py:42
  57.8 0.8 %level1.9.refs_4_.refs_0_ = f32[128,512]{1,0:T(8,128)S(1)} custom-call(f32[128,512]{1,0:T(8,128)S(1)} %level0.9.refs_1_.refs_0_, f32[128,512]{1,0:T(8,128)S(1)} %collective-permute-done.16.refs_1_, f32[128,512]{1,0:T(8,128)S(1)} %order.17.refs_5_.refs_2_, bf16[512,1024]{1,0:T(8,128)(2,1)S(1)} %get-tuple-element.28.refs_2_.refs_3_, ...), custom_call_target="tpu_custom_call" | custom-call | flops 4000000000 | bytes 1000 | tf_op jit(solution)/shard_map/level1/pallas_call | solution.py:97
  58.5 0.9 %collective-permute-start.21 = (f32[128,512]{1,0:T(8,128)S(1)}, f32[128,512]{1,0:T(8,128)S(1)}, u32[]{:S(2)}, u32[]{:S(2)}) collective-permute-start(f32[128,512]{1,0:T(8,128)S(1)} %level1.9.refs_4_.refs_0_), channel_id=1, source_target_pairs={{0,4},{1,5},{2,6},{3,7},{4,0},{5,1},{6,2},{7,3},{8,12},{9,13},{10,... | collective-permute-start | bytes 786440 | tf_op jit(solution)/shard_map/ppermute | solution.py:42
  59.4 1.6 %collective-permute-done.22.refs_1_ = f32[128,512]{1,0:T(8,128)S(1)} collective-permute-done((f32[128,512]{1,0:T(8,128)S(1)}, f32[128,512]{1,0:T(8,128)S(1)}, u32[]{:S(2)}, u32[]{:S(2)}) %collective-permute-start.22) | collective-permute-done | bytes 262176 | tf_op jit(solution)/shard_map/ppermute | solution.py:42
  61.0 0.7 level2.8.refs_4_.refs_3_
  61.7 0.7 collective-permute-start.27
  62.4 3.3 %collective-permute-done.21.refs_1_ = f32[128,512]{1,0:T(8,128)S(1)} collective-permute-done((f32[128,512]{1,0:T(8,128)S(1)}, f32[128,512]{1,0:T(8,128)S(1)}, u32[]{:S(2)}, u32[]{:S(2)}) %collective-permute-start.21) | collective-permute-done | bytes 262176 | tf_op jit(solution)/shard_map/ppermute | solution.py:42
  65.8 0.7 level2.9.refs_10_.refs_0_
  66.5 1.1 %collective-permute-start.23 = (f32[128,512]{1,0:T(8,128)S(1)}, f32[128,512]{1,0:T(8,128)S(1)}, u32[]{:S(2)}, u32[]{:S(2)}) collective-permute-start(f32[128,512]{1,0:T(8,128)S(1)} %level2.9.refs_10_.refs_0_), channel_id=1, source_target_pairs={{0,2},{1,3},{2,0},{3,1},{4,6},{5,7},{6,4},{7,5},{8,10},{9,11},{10,... | collective-permute-start | bytes 786440 | tf_op jit(solution)/shard_map/ppermute | solution.py:42
  67.7 1.3 %collective-permute-done.27.refs_7_ = f32[128,512]{1,0:T(8,128)S(1)} collective-permute-done((f32[128,512]{1,0:T(8,128)S(1)}, f32[128,512]{1,0:T(8,128)S(1)}, u32[]{:S(2)}, u32[]{:S(2)}) %collective-permute-start.27) | collective-permute-done | bytes 262176 | tf_op jit(solution)/shard_map/ppermute | solution.py:42
  69.0 2.4 %level3.2 = (f32[1,512,512]{2,1,0:T(8,128)}, f32[8,128]{1,0:T(8,128)S(1)}) custom-call(f32[64,512]{1,0:T(8,128)S(1)} %level2.5.refs_5_.refs_0_, f32[96,512]{1,0:T(8,128)S(1)} %level2.6.refs_5_.refs_1_, f32[96,512]{1,0:T(8,128)S(1)} %level2.7.refs_5_.refs_2_, f32[128,512]{1,0:T(8,128)S(1)} %level2.8.refs_4_.refs_3_, ...), custom_call_target="tpu_custom_call" | custom-call | flops 4000000000 | bytes 1000 | tf_op jit(solution)/shard_map/level3/pallas_call | solution.py:97
  71.4 2.4 %collective-permute-done.23.refs_1_ = f32[128,512]{1,0:T(8,128)S(1)} collective-permute-done((f32[128,512]{1,0:T(8,128)S(1)}, f32[128,512]{1,0:T(8,128)S(1)}, u32[]{:S(2)}, u32[]{:S(2)}) %collective-permute-start.23) | collective-permute-done | bytes 262176 | tf_op jit(solution)/shard_map/ppermute | solution.py:42
  73.8 2.0 %level3.3 = (f32[1,512,512]{2,1,0:T(8,128)}, f32[8,128]{1,0:T(8,128)}) custom-call(f32[128,512]{1,0:T(8,128)S(1)} %level2.9.refs_10_.refs_0_, f32[128,512]{1,0:T(8,128)S(1)} %collective-permute-done.23.refs_1_, bf16[512,1024]{1,0:T(8,128)(2,1)S(1)} %get-tuple-element.31.refs_8_.refs_2_, ...), custom_call_target="tpu_custom_call", output_to_operand_aliasing={{0}: (4, {})} | custom-call | flops 4000000000 | bytes 1000 | tf_op jit(solution)/shard_map/level3/pallas_call | solution.py:97
  (51 shorter events, 2.3 us)
Async XLA Ops:
  1.1 3.0 %copy-start = (f32[1,512,512]{2,1,0:T(8,128)S(1)}, f32[1,512,512]{2,1,0:T(8,128)}, u32[]{:S(2)}) copy-start(f32[1,512,512]{2,1,0:T(8,128)} %refs_0_.7) | copy-start | bytes 3145732
  1.1 7.3 %collective-permute-start = (f32[64,512]{1,0:T(8,128)S(1)}, f32[64,512]{1,0:T(8,128)S(1)}, u32[]{:S(2)}, u32[]{:S(2)}) collective-permute-start(f32[64,512]{1,0:T(8,128)S(1)} %order.9.refs_1_.refs_0_), channel_id=1, source_target_pairs={{0,16},{1,17},{2,18},{3,19},{4,20},{5,21},{6,22},{7,23},{8,24},{9,... | collective-permute-start | bytes 393224 | tf_op jit(solution)/shard_map/ppermute | solution.py:42
  4.7 2.2 %slice-start = ((s8[8388608]{0:T(1024)(128)(4,1)}), s8[4194304]{0:T(1024)(128)(4,1)S(1)}, s32[]{:S(2)}) async-start(s8[8388608]{0:T(1024)(128)(4,1)} %bitcast), calls=%async_computation | async-start | bytes 8388608
  4.7 3.5 %slice-start.1 = ((s8[8388608]{0:T(1024)(128)(4,1)}), s8[4194304]{0:T(1024)(128)(4,1)S(1)}, s32[]{:S(2)}) async-start(s8[8388608]{0:T(1024)(128)(4,1)} %bitcast), calls=%async_computation.1 | async-start | bytes 8388608
  4.7 10.2 %collective-permute-start.3 = (f32[96,512]{1,0:T(8,128)S(1)}, f32[96,512]{1,0:T(8,128)S(1)}, u32[]{:S(2)}, u32[]{:S(2)}) collective-permute-start(f32[96,512]{1,0:T(8,128)S(1)} %order.10.refs_1_.refs_0_), channel_id=1, source_target_pairs={{0,16},{1,17},{2,18},{3,19},{4,20},{5,21},{6,22},{7,23},{8,24},{9,... | collective-permute-start | bytes 589832 | tf_op jit(solution)/shard_map/ppermute | solution.py:42
  5.9 10.9 %collective-permute-start.2 = (f32[96,512]{1,0:T(8,128)S(1)}, f32[96,512]{1,0:T(8,128)S(1)}, u32[]{:S(2)}, u32[]{:S(2)}) collective-permute-start(f32[96,512]{1,0:T(8,128)S(1)} %order.11.refs_1_.refs_0_), channel_id=1, source_target_pairs={{0,16},{1,17},{2,18},{3,19},{4,20},{5,21},{6,22},{7,23},{8,24},{9,... | collective-permute-start | bytes 589832 | tf_op jit(solution)/shard_map/ppermute | solution.py:42
  9.5 9.2 %collective-permute-start.7 = (f32[64,512]{1,0:T(8,128)S(1)}, f32[64,512]{1,0:T(8,128)S(1)}, u32[]{:S(2)}, u32[]{:S(2)}) collective-permute-start(f32[64,512]{1,0:T(8,128)S(1)} %level0.5.refs_1_.refs_0_), channel_id=1, source_target_pairs={{0,8},{1,9},{2,10},{3,11},{4,12},{5,13},{6,14},{7,15},{8,0},{9,1},... | collective-permute-start | bytes 393224 | tf_op jit(solution)/shard_map/ppermute | solution.py:42
  12.6 12.7 %collective-permute-start.5 = (f32[128,512]{1,0:T(8,128)S(1)}, f32[128,512]{1,0:T(8,128)S(1)}, u32[]{:S(2)}, u32[]{:S(2)}) collective-permute-start(f32[128,512]{1,0:T(8,128)S(1)} %order.12.refs_1_.refs_0_), channel_id=1, source_target_pairs={{0,16},{1,17},{2,18},{3,19},{4,20},{5,21},{6,22},{7,23},{8,24},{9,... | collective-permute-start | bytes 786440 | tf_op jit(solution)/shard_map/ppermute | solution.py:42
  14.1 13.8 %collective-permute-start.1 = (f32[128,512]{1,0:T(8,128)S(1)}, f32[128,512]{1,0:T(8,128)S(1)}, u32[]{:S(2)}, u32[]{:S(2)}) collective-permute-start(f32[128,512]{1,0:T(8,128)S(1)} %order.13.refs_1_.refs_0_), channel_id=1, source_target_pairs={{0,16},{1,17},{2,18},{3,19},{4,20},{5,21},{6,22},{7,23},{8,24},{9,... | collective-permute-start | bytes 786440 | tf_op jit(solution)/shard_map/ppermute | solution.py:42
  15.7 6.4 %collective-permute-start.6 = (f32[96,512]{1,0:T(8,128)S(1)}, f32[96,512]{1,0:T(8,128)S(1)}, u32[]{:S(2)}, u32[]{:S(2)}) collective-permute-start(f32[96,512]{1,0:T(8,128)S(1)} %level0.6.refs_4_.refs_0_), channel_id=1, source_target_pairs={{0,1},{1,0},{2,3},{3,2},{4,8},{5,9},{6,10},{7,11},{8,4},{9,5},{10,... | collective-permute-start | bytes 589832 | tf_op jit(solution)/shard_map/ppermute | solution.py:42
  17.6 8.5 %collective-permute-start.4 = (f32[96,512]{1,0:T(8,128)S(1)}, f32[96,512]{1,0:T(8,128)S(1)}, u32[]{:S(2)}, u32[]{:S(2)}) collective-permute-start(f32[96,512]{1,0:T(8,128)S(1)} %level0.7.refs_4_.refs_0_), channel_id=1, source_target_pairs={{0,1},{1,0},{2,3},{3,2},{4,8},{5,9},{6,10},{7,11},{8,4},{9,5},{10,... | collective-permute-start | bytes 589832 | tf_op jit(solution)/shard_map/ppermute | solution.py:42
  19.5 20.9 %collective-permute-start.13 = (f32[64,512]{1,0:T(8,128)S(1)}, f32[64,512]{1,0:T(8,128)S(1)}, u32[]{:S(2)}, u32[]{:S(2)}) collective-permute-start(f32[64,512]{1,0:T(8,128)S(1)} %level1.5.refs_2_.refs_0_), channel_id=1, source_target_pairs={{0,4},{1,5},{2,6},{3,7},{4,0},{5,1},{6,2},{7,3},{8,12},{9,13},{10,... | collective-permute-start | bytes 393224 | tf_op jit(solution)/shard_map/ppermute | solution.py:42
  22.2 7.9 %collective-permute-start.10 = (f32[96,512]{1,0:T(8,128)S(1)}, f32[96,512]{1,0:T(8,128)S(1)}, u32[]{:S(2)}, u32[]{:S(2)}) collective-permute-start(f32[96,512]{1,0:T(8,128)S(1)} %pass.4.refs_4_), channel_id=1, source_target_pairs={{0,4},{1,5},{2,6},{3,7},{4,0},{5,1},{6,2},{7,3},{8,12},{9,13},{10,... | collective-permute-start | bytes 589832 | tf_op jit(solution)/shard_map/ppermute | solution.py:42
  26.0 4.1 %collective-permute-start.9 = (f32[128,512]{1,0:T(8,128)S(1)}, f32[128,512]{1,0:T(8,128)S(1)}, u32[]{:S(2)}, u32[]{:S(2)}) collective-permute-start(f32[128,512]{1,0:T(8,128)S(1)} %level0.8.refs_2_.refs_0_), channel_id=1, source_target_pairs={{0,1},{1,0},{2,3},{3,2},{4,8},{5,9},{6,10},{7,11},{8,4},{9,5},{10,... | collective-permute-start | bytes 786440 | tf_op jit(solution)/shard_map/ppermute | solution.py:42
  26.2 13.7 %collective-permute-start.15 = (f32[96,512]{1,0:T(8,128)S(1)}, f32[96,512]{1,0:T(8,128)S(1)}, u32[]{:S(2)}, u32[]{:S(2)}) collective-permute-start(f32[96,512]{1,0:T(8,128)S(1)} %pass.5.refs_4_), channel_id=1, source_target_pairs={{0,4},{1,5},{2,6},{3,7},{4,0},{5,1},{6,2},{7,3},{8,12},{9,13},{10,... | collective-permute-start | bytes 589832 | tf_op jit(solution)/shard_map/ppermute | solution.py:42
  28.7 5.3 %collective-permute-start.8 = (f32[128,512]{1,0:T(8,128)S(1)}, f32[128,512]{1,0:T(8,128)S(1)}, u32[]{:S(2)}, u32[]{:S(2)}) collective-permute-start(f32[128,512]{1,0:T(8,128)S(1)} %level0.9.refs_1_.refs_0_), channel_id=1, source_target_pairs={{0,1},{1,0},{2,3},{3,2},{4,8},{5,9},{6,10},{7,11},{8,4},{9,5},{10,... | collective-permute-start | bytes 786440 | tf_op jit(solution)/shard_map/ppermute | solution.py:42
  30.1 12.8 %collective-permute-start.12 = (f32[96,512]{1,0:T(8,128)S(1)}, f32[96,512]{1,0:T(8,128)S(1)}, u32[]{:S(2)}, u32[]{:S(2)}) collective-permute-start(f32[96,512]{1,0:T(8,128)S(1)} %order.14.refs_2_), channel_id=1, source_target_pairs={{0,1},{1,0},{2,3},{3,2},{4,8},{5,9},{6,10},{7,11},{8,4},{9,5},{10,... | collective-permute-start | bytes 589832 | tf_op jit(solution)/shard_map/ppermute | solution.py:42
  30.1 9.8 %collective-permute-start.14 = (f32[128,512]{1,0:T(8,128)S(1)}, f32[128,512]{1,0:T(8,128)S(1)}, u32[]{:S(2)}, u32[]{:S(2)}) collective-permute-start(f32[128,512]{1,0:T(8,128)S(1)} %pass.6.refs_2_), channel_id=1, source_target_pairs={{0,4},{1,5},{2,6},{3,7},{4,0},{5,1},{6,2},{7,3},{8,12},{9,13},{10,... | collective-permute-start | bytes 786440 | tf_op jit(solution)/shard_map/ppermute | solution.py:42
  34.0 12.4 %collective-permute-start.11 = (f32[128,512]{1,0:T(8,128)S(1)}, f32[128,512]{1,0:T(8,128)S(1)}, u32[]{:S(2)}, u32[]{:S(2)}) collective-permute-start(f32[128,512]{1,0:T(8,128)S(1)} %pass.7.refs_1_), channel_id=1, source_target_pairs={{0,4},{1,5},{2,6},{3,7},{4,0},{5,1},{6,2},{7,3},{8,12},{9,13},{10,... | collective-permute-start | bytes 786440 | tf_op jit(solution)/shard_map/ppermute | solution.py:42
  39.9 6.5 %collective-permute-start.17 = (f32[96,512]{1,0:T(8,128)S(1)}, f32[96,512]{1,0:T(8,128)S(1)}, u32[]{:S(2)}, u32[]{:S(2)}) collective-permute-start(f32[96,512]{1,0:T(8,128)S(1)} %order.15.refs_1_.refs_2_), channel_id=1, source_target_pairs={{0,1},{1,0},{2,3},{3,2},{4,8},{5,9},{6,10},{7,11},{8,4},{9,5},{10,... | collective-permute-start | bytes 589832 | tf_op jit(solution)/shard_map/ppermute | solution.py:42
  40.0 12.6 %collective-permute-start.19 = (f32[128,512]{1,0:T(8,128)S(1)}, f32[128,512]{1,0:T(8,128)S(1)}, u32[]{:S(2)}, u32[]{:S(2)}) collective-permute-start(f32[128,512]{1,0:T(8,128)S(1)} %order.16.refs_4_.refs_2_), channel_id=1, source_target_pairs={{0,1},{1,0},{2,3},{3,2},{4,8},{5,9},{6,10},{7,11},{8,4},{9,5},{10,... | collective-permute-start | bytes 786440 | tf_op jit(solution)/shard_map/ppermute | solution.py:42
  41.2 26.4 %collective-permute-start.24 = (f32[64,512]{1,0:T(8,128)S(1)}, f32[64,512]{1,0:T(8,128)S(1)}, u32[]{:S(2)}, u32[]{:S(2)}) collective-permute-start(f32[64,512]{1,0:T(8,128)S(1)} %level2.5.refs_5_.refs_0_), channel_id=1, source_target_pairs={{0,2},{1,3},{2,0},{3,1},{4,6},{5,7},{6,4},{7,5},{8,10},{9,11},{10,... | collective-permute-start | bytes 393224 | tf_op jit(solution)/shard_map/ppermute | solution.py:42
  43.6 7.0 %collective-permute-start.20 = (f32[96,512]{1,0:T(8,128)S(1)}, f32[96,512]{1,0:T(8,128)S(1)}, u32[]{:S(2)}, u32[]{:S(2)}) collective-permute-start(f32[96,512]{1,0:T(8,128)S(1)} %level1.6.refs_1_.refs_0_), channel_id=1, source_target_pairs={{0,4},{1,5},{2,6},{3,7},{4,0},{5,1},{6,2},{7,3},{8,12},{9,13},{10,... | collective-permute-start | bytes 589832 | tf_op jit(solution)/shard_map/ppermute | solution.py:42
  46.4 11.4 %collective-permute-start.16 = (f32[128,512]{1,0:T(8,128)S(1)}, f32[128,512]{1,0:T(8,128)S(1)}, u32[]{:S(2)}, u32[]{:S(2)}) collective-permute-start(f32[128,512]{1,0:T(8,128)S(1)} %order.17.refs_5_.refs_2_), channel_id=1, source_target_pairs={{0,1},{1,0},{2,3},{3,2},{4,8},{5,9},{6,10},{7,11},{8,4},{9,5},{10,... | collective-permute-start | bytes 786440 | tf_op jit(solution)/shard_map/ppermute | solution.py:42
  47.2 8.2 %collective-permute-start.18 = (f32[96,512]{1,0:T(8,128)S(1)}, f32[96,512]{1,0:T(8,128)S(1)}, u32[]{:S(2)}, u32[]{:S(2)}) collective-permute-start(f32[96,512]{1,0:T(8,128)S(1)} %level1.7.refs_4_.refs_0_), channel_id=1, source_target_pairs={{0,4},{1,5},{2,6},{3,7},{4,0},{5,1},{6,2},{7,3},{8,12},{9,13},{10,... | collective-permute-start | bytes 589832 | tf_op jit(solution)/shard_map/ppermute | solution.py:42
  51.5 16.2 %collective-permute-start.25 = (f32[96,512]{1,0:T(8,128)S(1)}, f32[96,512]{1,0:T(8,128)S(1)}, u32[]{:S(2)}, u32[]{:S(2)}) collective-permute-start(f32[96,512]{1,0:T(8,128)S(1)} %level2.6.refs_5_.refs_1_), channel_id=1, source_target_pairs={{0,2},{1,3},{2,0},{3,1},{4,6},{5,7},{6,4},{7,5},{8,10},{9,11},{10,... | collective-permute-start | bytes 589832 | tf_op jit(solution)/shard_map/ppermute | solution.py:42
  53.3 7.7 %collective-permute-start.22 = (f32[128,512]{1,0:T(8,128)S(1)}, f32[128,512]{1,0:T(8,128)S(1)}, u32[]{:S(2)}, u32[]{:S(2)}) collective-permute-start(f32[128,512]{1,0:T(8,128)S(1)} %level1.8.refs_4_.refs_0_), channel_id=1, source_target_pairs={{0,4},{1,5},{2,6},{3,7},{4,0},{5,1},{6,2},{7,3},{8,12},{9,13},{10,... | collective-permute-start | bytes 786440 | tf_op jit(solution)/shard_map/ppermute | solution.py:42
  56.2 11.5 %collective-permute-start.26 = (f32[96,512]{1,0:T(8,128)S(1)}, f32[96,512]{1,0:T(8,128)S(1)}, u32[]{:S(2)}, u32[]{:S(2)}) collective-permute-start(f32[96,512]{1,0:T(8,128)S(1)} %level2.7.refs_5_.refs_2_), channel_id=1, source_target_pairs={{0,2},{1,3},{2,0},{3,1},{4,6},{5,7},{6,4},{7,5},{8,10},{9,11},{10,... | collective-permute-start | bytes 589832 | tf_op jit(solution)/shard_map/ppermute | solution.py:42
  58.5 7.3 %collective-permute-start.21 = (f32[128,512]{1,0:T(8,128)S(1)}, f32[128,512]{1,0:T(8,128)S(1)}, u32[]{:S(2)}, u32[]{:S(2)}) collective-permute-start(f32[128,512]{1,0:T(8,128)S(1)} %level1.9.refs_4_.refs_0_), channel_id=1, source_target_pairs={{0,4},{1,5},{2,6},{3,7},{4,0},{5,1},{6,2},{7,3},{8,12},{9,13},{10,... | collective-permute-start | bytes 786440 | tf_op jit(solution)/shard_map/ppermute | solution.py:42
  61.7 7.3 %collective-permute-start.27 = (f32[128,512]{1,0:T(8,128)S(1)}, f32[128,512]{1,0:T(8,128)S(1)}, u32[]{:S(2)}, u32[]{:S(2)}) collective-permute-start(f32[128,512]{1,0:T(8,128)S(1)} %level2.8.refs_4_.refs_3_), channel_id=1, source_target_pairs={{0,2},{1,3},{2,0},{3,1},{4,6},{5,7},{6,4},{7,5},{8,10},{9,11},{10,... | collective-permute-start | bytes 786440 | tf_op jit(solution)/shard_map/ppermute | solution.py:42
  66.5 7.3 %collective-permute-start.23 = (f32[128,512]{1,0:T(8,128)S(1)}, f32[128,512]{1,0:T(8,128)S(1)}, u32[]{:S(2)}, u32[]{:S(2)}) collective-permute-start(f32[128,512]{1,0:T(8,128)S(1)} %level2.9.refs_10_.refs_0_), channel_id=1, source_target_pairs={{0,2},{1,3},{2,0},{3,1},{4,6},{5,7},{6,4},{7,5},{8,10},{9,11},{10,... | collective-permute-start | bytes 786440 | tf_op jit(solution)/shard_map/ppermute | solution.py:42

commit v2 on v1

--- a/solution.py
+++ b/solution.py
@@ -10,23 +10,27 @@
 VMEM = pl.BlockSpec(memory_space=pltpu.VMEM)
 HBM = pl.BlockSpec(memory_space=pltpu.HBM)
 ANY = pl.BlockSpec(memory_space=pl.ANY)
-CHUNKS = (2, 3, 3, 4, 4)
+CHUNKS = (4, 6, 6, 8, 8)
 X_GROUPS = ((0,), (1,), (2,), (3,), (4,))
+S_GROUPS = ((0,), (1,), (2,), (3,), (4,))
+B_GROUPS = ((0,), (1,), (2,), (3,), (4,))
 Z_GROUPS = ((0,), (1,), (2,), (3,), (4,))
 Y_GROUPS = ((0,), (1,), (2,), (3,), (4,))
 DIRECT = (0,)
 RESULT_BLOCKS = ((0, 3), (3, 4))
 COST = 4000000000
+COSTS = {}
 ORDER = (
     "in0 x0 in1 x1",
-    "x2 m0 a0 m2",
-    "x3 x4 m1 a1",
+    "x2 m0 a0 x3",
+    "m1 x4 m2 a1",
     "a2 b0 p1 a3",
-    "p2 a4 q1 p3",
+    "p2 a4 p3 q1",
     "p4 m3 q2 q3",
     "c0 b1 q4 b2",
     "c1 b3 c2 b4",
-    "c3 c4 d0 d1",
+    "cc4 c3 c4 d0",
+    "dd1 d1",
 )
 
 
@@ -103,7 +107,7 @@
             input_output_aliases={} if in_place is None else {in_place: 0},
             compiler_params=pltpu.CompilerParams(vmem_limit_bytes=8 * 2**20),
             cost_estimate=pl.CostEstimate(
-                flops=COST, bytes_accessed=1000, transcendentals=0
+                flops=COSTS.get(name, COST), bytes_accessed=1000, transcendentals=0
             ),
             name=name,
         )(*args)
@@ -115,7 +119,7 @@
     nbits = lax.axis_size(AXES).bit_length() - 1
     bits = [nbits - 1 - level for level in range(transfer.shape[0])]
     rank, rhs = coeffs.shape[1:]
-    sizes = [c * rhs // 16 for c in CHUNKS]
+    sizes = [c * rhs // 32 for c in CHUNKS]
     n = len(sizes)
     ends = [sum(sizes[: s + 1]) for s in range(n)]
     unit = rhs // 4
@@ -136,14 +140,16 @@
 
     def pieces(store, chunks):
         found = []
-        for group, array in store.items():
+        for group in sorted(store):
+            arrays = store[group]
+            arrays = arrays if isinstance(arrays, tuple) else (arrays,)
             at = 0
             for k in group:
                 if k in chunks:
-                    if found and found[-1][0] is array:
-                        found[-1][1][1] = at + sizes[k]
+                    if found and found[-1][0] is arrays[0]:
+                        found[-1][-1][1] = at + sizes[k]
                     else:
-                        found.append((array, [at, at + sizes[k]]))
+                        found.append((*arrays, [at, at + sizes[k]]))
                 at += sizes[k]
         return found
 
@@ -196,7 +202,28 @@
         c0[group] = chain("order", lambda *_: None, [c0[group]], [rows(group)], in_place=0)[0]
         x[group] = send(c0[group], across(0))
 
-    def level(name, number, mine, other, outs):
+    def own_half(ref, number):
+        upper = bit_of(bits[number])
+        own = ref[:, pl.ds(pl.multiple_of(upper * rank, rank), rank)]
+        return own, ref[:, pl.ds(pl.multiple_of((1 - upper) * rank, rank), rank)]
+
+    def ahead(key, number, mine, turned=False):
+        args = [p[0] for p in mine]
+        size = sum(p[-1][1] - p[-1][0] for p in mine)
+
+        def body(*refs):
+            h, l, o = refs[len(args) :]
+            own = joined([r[slice(*p[-1])] for r, p in zip(refs, mine)])
+            times = product_t if turned else product
+            o[...] = times(own, own_half(h, number)[0], own_half(l, number)[0])
+
+        shape = (rank, size) if turned else (size, rank)
+        outs = [jax.ShapeDtypeStruct(shape, F32)]
+        done[key] = chain("ahead", body, args + matrix[number], outs)[0]
+
+    def level(name, number, mine, other, outs, key=None):
+        if key in done:
+            mine = [(done[key], [0, sum(p[-1][1] - p[-1][0] for p in mine)])]
         args = [p[0] for p in mine] + [a for p in other for a in p[:-1]]
 
         def body(*refs):
@@ -210,7 +237,10 @@
                     block = jnp.where(is_middle(), block, refs[at + 1][slice(*p[-1])])
                 at += len(p) - 1
                 blocks.append(block)
-            y = product(stacked(own, joined(blocks), bit_of(bits[number])), h[...], l[...])
+            if key in done:
+                y = own + product(joined(blocks), own_half(h, number)[1], own_half(l, number)[1])
+            else:
+                y = product(stacked(own, joined(blocks), bit_of(bits[number])), h[...], l[...])
             at = 0
             for o in out_refs:
                 o[...] = y[at : at + o.shape[0]]
@@ -218,67 +248,99 @@
 
         return chain(name, body, args + matrix[number], outs)
 
+    def inside(groups, group):
+        return [g for g in groups if set(g) <= set(group)]
+
     def step_a(i):
         group = X_GROUPS[i]
-        out = level(
-            "level0",
-            0,
-            pieces(c0, group),
-            pieces(x, group),
-            [rows([k]) for k in group],
-        )
-        for k, c in zip(group, out):
-            c1[(k,)] = c
-            if k in DIRECT:
-                got[k] = (send(c, across(1)),)
+        parts = inside(S_GROUPS, group)
+        out = level("level0", 0, pieces(c0, group), pieces(x, group), [rows(g) for g in parts])
+        for g, c in zip(parts, out):
+            c1[g] = c
+            if S_GROUPS.index(g) in DIRECT:
+                got[g] = send(c, across(1))
             else:
-                got[k] = send(c, middle)
-
-    def step_p(k):
+                got[g] = send(c, middle)
+
+    def step_p(i):
+        group = S_GROUPS[i]
+
         def body(own, other, o_ref):
             o_ref[...] = jnp.where(is_middle(), other[...], own[...])
 
-        passed = chain("pass", body, [c1[(k,)], got[k]], [rows([k])])[0]
-        got[k] = send(passed, across(2))
-
-    def step_q(k):
-        kept = chain("order", lambda *_: None, [got[k]], [rows([k])], in_place=0)[0]
-        got[k] = (send(kept, middle), kept)
+        passed = chain("pass", body, [c1[group], got[group]], [rows(group)])[0]
+        got[group] = send(passed, across(2))
+
+    def step_q(i):
+        group = S_GROUPS[i]
+        kept = chain("order", lambda *_: None, [got[group]], [rows(group)], in_place=0)[0]
+        got[group] = (send(kept, middle), kept)
 
     def step_b(i):
-        group = Z_GROUPS[i]
-        other = [(*got[k], [0, sizes[k]]) for k in group]
-        c2[group] = level("level1", 1, pieces(c1, group), other, [rows(group)])[0]
-        z[group] = send(c2[group], across(2))
+        group = B_GROUPS[i]
+        parts = inside(Z_GROUPS, group)
+        out = level(
+            "level1",
+            1,
+            pieces(c1, group),
+            pieces(got, group),
+            [rows(g) for g in parts],
+            ("b", i),
+        )
+        for g, c in zip(parts, out):
+            c2[g] = c
+            z[g] = send(c, across(2))
 
     def step_c(i):
         group = Y_GROUPS[i]
-        c3[group] = level("level2", 2, pieces(c2, group), pieces(z, group), [rows(group)])[0]
+        c3[group] = level(
+            "level2", 2, pieces(c2, group), pieces(z, group), [rows(group)], ("c", i)
+        )[0]
         y[group] = send(c3[group], across(3))
+
+    def step_bb(i):
+        ahead(("b", i), 1, pieces(c1, B_GROUPS[i]))
+
+    def step_cc(i):
+        ahead(("c", i), 2, pieces(c2, Y_GROUPS[i]))
+
+    def columns_of(store, j):
+        first, stop = (b * unit for b in RESULT_BLOCKS[j])
+        found = []
+        for group in Y_GROUPS:
+            begin = ends[group[0]] - sizes[group[0]]
+            cut = [max(first - begin, 0), min(stop, ends[group[-1]]) - begin]
+            if cut[0] < cut[1]:
+                found.append((store[group], cut))
+        return found
+
+    def step_dd(j):
+        ahead(("d", j), 3, columns_of(c3, j), turned=True)
 
     def step_d(j):
         first, stop = (b * unit for b in RESULT_BLOCKS[j])
-        args, cuts = [], []
-        for store in (c3, y):
-            for group in Y_GROUPS:
-                begin = ends[group[0]] - sizes[group[0]]
-                cut = slice(max(first - begin, 0), min(stop, ends[group[-1]]) - begin)
-                if cut.start < cut.stop:
-                    args.append(store[group])
-                    cuts.append(cut)
-        p = len(args) // 2
+        key = ("d", j)
+        mine, other = columns_of(c3, j), columns_of(y, j)
+        if key in done:
+            mine = [(done[key], [0, rank])]
+        args = [p[0] for p in mine + other] + matrix[3]
 
         def body(*refs):
             held, sem = refs[-2:]
-            h, l, o_ref, mark = refs[2 * p], refs[2 * p + 1], refs[-4], refs[-3]
+            h, l = refs[len(mine) + len(other) : len(mine) + len(other) + 2]
+            o_ref, mark = refs[-4], refs[-3]
             mark[...] = jnp.zeros_like(mark)
-            own = joined([r[cut] for r, cut in zip(refs[:p], cuts)])
-            other = joined([r[cut] for r, cut in zip(refs[p:], cuts[p:])])
-            both = stacked(own, other, bit_of(bits[3]))
+            own = joined([r[slice(*p[-1])] for r, p in zip(refs, mine)])
+            theirs = joined([r[slice(*p[-1])] for r, p in zip(refs[len(mine) :], other)])
             copies = []
             for half in range(2):
                 part = slice(half * rank // 2, (half + 1) * rank // 2)
-                held[part] = product_t(both, h[part], l[part])
+                if key in done:
+                    mh, ml = own_half(h.at[part], 3)[1], own_half(l.at[part], 3)[1]
+                    held[part] = own[part] + product_t(theirs, mh, ml)
+                else:
+                    both = stacked(own, theirs, bit_of(bits[3]))
+                    held[part] = product_t(both, h[part], l[part])
                 copies.append(
                     pltpu.make_async_copy(
                         held.at[part], o_ref.at[0, part, first:stop], sem.at[half]
@@ -288,30 +350,21 @@
             for copy in copies:
                 copy.wait()
 
-        args += matrix[3]
         in_place = None
         if result:
             in_place = len(args)
             args.append(result[-1])
+        outs = [pltpu.HBM(coeffs.shape, F32), jax.ShapeDtypeStruct((8, 128), F32)]
+        scratch = [pltpu.VMEM((rank, stop - first), F32), pltpu.SemaphoreType.DMA((2,))]
         result.append(
-            chain(
-                "level3",
-                body,
-                args,
-                [pltpu.HBM(coeffs.shape, F32), jax.ShapeDtypeStruct((8, 128), F32)],
-                scratch=[
-                    pltpu.VMEM((rank, stop - first), F32),
-                    pltpu.SemaphoreType.DMA((2,)),
-                ],
-                in_place=in_place,
-                out_hbm=True,
-            )[0]
+            chain("level3", body, args, outs, scratch, in_place=in_place, out_hbm=True)[0]
         )
 
     c0, x, c1, got, c2, z, c3, y, matrix, result = ({} for _ in range(10))
-    result = []
+    result, done = [], {}
     steps = {"in": step_in, "m": step_m, "x": step_x, "a": step_a, "p": step_p}
     steps |= {"q": step_q, "b": step_b, "c": step_c, "d": step_d}
+    steps |= {"bb": step_bb, "cc": step_cc, "dd": step_dd}
     for words in ORDER:
         for word in words.split():
             steps[word[:-1]](int(word[-1]))

time: 75.9 us -> 75.5 us (level)
  waiting for transfers between devices: 13.2 us -> 12 us
    ppermute x28, waiting for transfers between devices: 13.2 us -> 12 us  [send(): return lax.ppermute(block, AXES, [(i, partner(i)) for i in range(count)])]
    pallas_call x36 -> x38, Pallas kernels: 18.9 us -> 19.3 us  [__call__(): pl.pallas_call(kernel, out_shape=outs, in_specs=specs, out_specs=[HBM, VM...]
  transfers between devices with their start and end apart: 28 -> 28, of which waited for: 8 -> 8; matrix products, arithmetic and copies ran while one was open for 0% -> 0% of each run, Pallas kernels for 21% -> 22%
where the time goes in v2:
time: 75.5 us; the launch traced here: 75.4 us
  starting transfers between devices  42.4 us (56%)
  Pallas kernels  19.3 us (26%)
  waiting for transfers between devices  12 us (16%)
  local copies, waits for them, and re-layouts  1.36 us (2%)
    ppermute x28, starting transfers between devices, send(): return lax.ppermute(block, AXES, [(i, partner(i)) for i in range(count)])  42.4 us
    pallas_call x38, Pallas kernels, __call__(): pl.pallas_call(kernel, out_shape=outs, in_specs=specs, out_specs=[HBM, VM...  19.3 us
    ppermute x28, waiting for transfers between devices, send(): return lax.ppermute(block, AXES, [(i, partner(i)) for i in range(count)])  12 us
  transfers between devices with their start and end apart: 28, of which 8 were waited for; matrix products, arithmetic and copies ran while one was open for 0% of the time, Pallas kernels for 22%

profile of v2, /device:TPU:0, one launch (start us, length us, event | category | flops | bytes accessed | tf_op | source)
XLA Modules:
  0.0 75.4 jit_solution(8130411443570942081)
XLA Ops:
  0.0 1.1 %columns.2.refs_0_ = f32[64,512]{1,0:T(8,128)S(1)} custom-call(f32[1,512,512]{2,1,0:T(8,128)} %refs_0_.7), custom_call_target="tpu_custom_call" | custom-call | flops 4000000000 | bytes 1000 | tf_op jit(solution)/shard_map/columns/pallas_call | solution.py:101
  1.1 3.0 %collective-permute-start = (f32[64,512]{1,0:T(8,128)S(1)}, f32[64,512]{1,0:T(8,128)S(1)}, u32[]{:S(2)}, u32[]{:S(2)}) collective-permute-start(f32[64,512]{1,0:T(8,128)S(1)} %order.9.refs_1_.refs_0_), channel_id=1, source_target_pairs={{0,16},{1,17},{2,18},{3,19},{4,20},{5,21},{6,22},{7,23},{8,24},{9,... | collective-permute-start | bytes 393224 | tf_op jit(solution)/shard_map/ppermute | solution.py:46
  4.1 0.6 columns.3
  4.7 1.2 %collective-permute-start.3 = (f32[96,512]{1,0:T(8,128)S(1)}, f32[96,512]{1,0:T(8,128)S(1)}, u32[]{:S(2)}, u32[]{:S(2)}) collective-permute-start(f32[96,512]{1,0:T(8,128)S(1)} %order.10.refs_1_.refs_0_), channel_id=1, source_target_pairs={{0,16},{1,17},{2,18},{3,19},{4,20},{5,21},{6,22},{7,23},{8,24},{9,... | collective-permute-start | bytes 589832 | tf_op jit(solution)/shard_map/ppermute | solution.py:46
  5.9 0.9 %collective-permute-start.2 = (f32[96,512]{1,0:T(8,128)S(1)}, f32[96,512]{1,0:T(8,128)S(1)}, u32[]{:S(2)}, u32[]{:S(2)}) collective-permute-start(f32[96,512]{1,0:T(8,128)S(1)} %order.11.refs_1_.refs_0_), channel_id=1, source_target_pairs={{0,16},{1,17},{2,18},{3,19},{4,20},{5,21},{6,22},{7,23},{8,24},{9,... | collective-permute-start | bytes 589832 | tf_op jit(solution)/shard_map/ppermute | solution.py:46
  6.9 1.3 %slice-done.1 = s8[4194304]{0:T(1024)(128)(4,1)S(1)} async-done(((s8[8388608]{0:T(1024)(128)(4,1)}), s8[4194304]{0:T(1024)(128)(4,1)S(1)}, s32[]{:S(2)}) %slice-start.1) | async-done | bytes 4194328
  8.5 0.8 %level0.5.refs_1_.refs_0_ = f32[64,512]{1,0:T(8,128)S(1)} custom-call(f32[64,512]{1,0:T(8,128)S(1)} %order.9.refs_1_.refs_0_, f32[64,512]{1,0:T(8,128)S(1)} %collective-permute-done.refs_1_, bf16[512,1024]{1,0:T(8,128)(2,1)S(1)} %get-tuple-element.24.refs_2_, bf16[512,1024]{1,0:T(8,128)(2,1)S(1)} %get-tuple-element.25.refs_3_), custom_call_target="tpu_custom_call" | custom-call | flops 4000000000 | bytes 1000 | tf_op jit(solution)/shard_map/level0/pallas_call | solution.py:101
  9.2 3.0 %collective-permute-start.7 = (f32[64,512]{1,0:T(8,128)S(1)}, f32[64,512]{1,0:T(8,128)S(1)}, u32[]{:S(2)}, u32[]{:S(2)}) collective-permute-start(f32[64,512]{1,0:T(8,128)S(1)} %level0.5.refs_1_.refs_0_), channel_id=1, source_target_pairs={{0,8},{1,9},{2,10},{3,11},{4,12},{5,13},{6,14},{7,15},{8,0},{9,1},... | collective-permute-start | bytes 393224 | tf_op jit(solution)/shard_map/ppermute | solution.py:46
  12.6 1.6 %collective-permute-start.5 = (f32[128,512]{1,0:T(8,128)S(1)}, f32[128,512]{1,0:T(8,128)S(1)}, u32[]{:S(2)}, u32[]{:S(2)}) collective-permute-start(f32[128,512]{1,0:T(8,128)S(1)} %order.12.refs_1_.refs_0_), channel_id=1, source_target_pairs={{0,16},{1,17},{2,18},{3,19},{4,20},{5,21},{6,22},{7,23},{8,24},{9,... | collective-permute-start | bytes 786440 | tf_op jit(solution)/shard_map/ppermute | solution.py:46
  14.2 0.4 collective-permute-start.1
  15.0 0.8 %level0.6.refs_4_.refs_0_ = f32[96,512]{1,0:T(8,128)S(1)} custom-call(f32[96,512]{1,0:T(8,128)S(1)} %order.10.refs_1_.refs_0_, f32[96,512]{1,0:T(8,128)S(1)} %collective-permute-done.3.refs_1_, bf16[512,1024]{1,0:T(8,128)(2,1)S(1)} %get-tuple-element.24.refs_2_, bf16[512,1024]{1,0:T(8,128)(2,1)S(1)} %get-tuple-element.25.refs_3_, ...), custom_call_target="tpu_custom_call" | custom-call | flops 4000000000 | bytes 1000 | tf_op jit(solution)/shard_map/level0/pallas_call | solution.py:101
  15.8 1.0 %collective-permute-done.2.refs_1_ = f32[96,512]{1,0:T(8,128)S(1)} collective-permute-done((f32[96,512]{1,0:T(8,128)S(1)}, f32[96,512]{1,0:T(8,128)S(1)}, u32[]{:S(2)}, u32[]{:S(2)}) %collective-permute-start.2) | collective-permute-done | bytes 196640 | tf_op jit(solution)/shard_map/ppermute | solution.py:46
  16.8 0.8 %level0.7.refs_4_.refs_0_ = f32[96,512]{1,0:T(8,128)S(1)} custom-call(f32[96,512]{1,0:T(8,128)S(1)} %order.11.refs_1_.refs_0_, f32[96,512]{1,0:T(8,128)S(1)} %collective-permute-done.2.refs_1_, bf16[512,1024]{1,0:T(8,128)(2,1)S(1)} %get-tuple-element.24.refs_2_, bf16[512,1024]{1,0:T(8,128)(2,1)S(1)} %get-tuple-element.25.refs_3_, ...), custom_call_target="tpu_custom_call" | custom-call | flops 4000000000 | bytes 1000 | tf_op jit(solution)/shard_map/level0/pallas_call | solution.py:101
  18.1 0.8 %level1.5.refs_2_.refs_0_ = f32[64,512]{1,0:T(8,128)S(1)} custom-call(f32[64,512]{1,0:T(8,128)S(1)} %level0.5.refs_1_.refs_0_, f32[64,512]{1,0:T(8,128)S(1)} %collective-permute-done.7.refs_1_, bf16[512,1024]{1,0:T(8,128)(2,1)S(1)} %get-tuple-element.28.refs_2_.refs_3_, bf16[512,1024]{1,0:T(8,128)(2,1)S(1)} %get-tuple-element.26.refs_1_.refs_3_.refs_4_, ...), custom_call_target="tpu_custom_call" | custom-call | flops 4000000000 | bytes 1000 | tf_op jit(solution)/shard_map/level1/pallas_call | solution.py:101
  18.9 3.2 %collective-permute-start.13 = (f32[64,512]{1,0:T(8,128)S(1)}, f32[64,512]{1,0:T(8,128)S(1)}, u32[]{:S(2)}, u32[]{:S(2)}) collective-permute-start(f32[64,512]{1,0:T(8,128)S(1)} %level1.5.refs_2_.refs_0_), channel_id=1, source_target_pairs={{0,4},{1,5},{2,6},{3,7},{4,0},{5,1},{6,2},{7,3},{8,12},{9,13},{10,... | collective-permute-start | bytes 393224 | tf_op jit(solution)/shard_map/ppermute | solution.py:46
  22.2 2.8 %collective-permute-start.9 = (f32[96,512]{1,0:T(8,128)S(1)}, f32[96,512]{1,0:T(8,128)S(1)}, u32[]{:S(2)}, u32[]{:S(2)}) collective-permute-start(f32[96,512]{1,0:T(8,128)S(1)} %pass.4.refs_4_), channel_id=1, source_target_pairs={{0,4},{1,5},{2,6},{3,7},{4,0},{5,1},{6,2},{7,3},{8,12},{9,13},{10,... | collective-permute-start | bytes 589832 | tf_op jit(solution)/shard_map/ppermute | solution.py:46
  25.0 0.7 level0.8.refs_2_.refs_0_
  25.8 1.8 %collective-permute-start.15 = (f32[96,512]{1,0:T(8,128)S(1)}, f32[96,512]{1,0:T(8,128)S(1)}, u32[]{:S(2)}, u32[]{:S(2)}) collective-permute-start(f32[96,512]{1,0:T(8,128)S(1)} %pass.5.refs_4_), channel_id=1, source_target_pairs={{0,4},{1,5},{2,6},{3,7},{4,0},{5,1},{6,2},{7,3},{8,12},{9,13},{10,... | collective-permute-start | bytes 589832 | tf_op jit(solution)/shard_map/ppermute | solution.py:46
  27.6 0.7 level0.9.refs_2_.refs_0_
  28.5 5.2 %collective-permute-start.14 = (f32[128,512]{1,0:T(8,128)S(1)}, f32[128,512]{1,0:T(8,128)S(1)}, u32[]{:S(2)}, u32[]{:S(2)}) collective-permute-start(f32[128,512]{1,0:T(8,128)S(1)} %pass.6.refs_1_), channel_id=1, source_target_pairs={{0,4},{1,5},{2,6},{3,7},{4,0},{5,1},{6,2},{7,3},{8,12},{9,13},{10,... | collective-permute-start | bytes 786440 | tf_op jit(solution)/shard_map/ppermute | solution.py:46
  33.8 5.6 %collective-permute-start.11 = (f32[128,512]{1,0:T(8,128)S(1)}, f32[128,512]{1,0:T(8,128)S(1)}, u32[]{:S(2)}, u32[]{:S(2)}) collective-permute-start(f32[128,512]{1,0:T(8,128)S(1)} %pass.7.refs_1_), channel_id=1, source_target_pairs={{0,4},{1,5},{2,6},{3,7},{4,0},{5,1},{6,2},{7,3},{8,12},{9,13},{10,... | collective-permute-start | bytes 786440 | tf_op jit(solution)/shard_map/ppermute | solution.py:46
  39.7 0.5 collective-permute-start.19
  40.2 0.8 %level2.5.refs_5_.refs_0_ = f32[64,512]{1,0:T(8,128)S(1)} custom-call(f32[64,512]{1,0:T(8,128)S(1)} %level1.5.refs_2_.refs_0_, f32[64,512]{1,0:T(8,128)S(1)} %collective-permute-done.13.refs_1_, bf16[512,1024]{1,0:T(8,128)(2,1)S(1)} %get-tuple-element.29.refs_2_.refs_1_, bf16[512,1024]{1,0:T(8,128)(2,1)S(1)} %get-tuple-element.27.refs_4_.refs_3_.refs_2_, ...), custom_call_target="tpu_custom_call" | custom-call | flops 4000000000 | bytes 1000 | tf_op jit(solution)/shard_map/level2/pallas_call | solution.py:101
  41.0 1.6 %collective-permute-start.23 = (f32[64,512]{1,0:T(8,128)S(1)}, f32[64,512]{1,0:T(8,128)S(1)}, u32[]{:S(2)}, u32[]{:S(2)}) collective-permute-start(f32[64,512]{1,0:T(8,128)S(1)} %level2.5.refs_5_.refs_0_), channel_id=1, source_target_pairs={{0,2},{1,3},{2,0},{3,1},{4,6},{5,7},{6,4},{7,5},{8,10},{9,11},{10,... | collective-permute-start | bytes 393224 | tf_op jit(solution)/shard_map/ppermute | solution.py:46
  42.6 0.8 %level1.6.refs_1_.refs_0_ = f32[96,512]{1,0:T(8,128)S(1)} custom-call(f32[96,512]{1,0:T(8,128)S(1)} %level0.6.refs_4_.refs_0_, f32[96,512]{1,0:T(8,128)S(1)} %collective-permute-done.12.refs_1_, f32[96,512]{1,0:T(8,128)S(1)} %order.14.refs_2_, bf16[512,1024]{1,0:T(8,128)(2,1)S(1)} %get-tuple-element.28.refs_2_.refs_3_, ...), custom_call_target="tpu_custom_call" | custom-call | flops 4000000000 | bytes 1000 | tf_op jit(solution)/shard_map/level1/pallas_call | solution.py:101
  43.4 2.5 %collective-permute-start.20 = (f32[96,512]{1,0:T(8,128)S(1)}, f32[96,512]{1,0:T(8,128)S(1)}, u32[]{:S(2)}, u32[]{:S(2)}) collective-permute-start(f32[96,512]{1,0:T(8,128)S(1)} %level1.6.refs_1_.refs_0_), channel_id=1, source_target_pairs={{0,4},{1,5},{2,6},{3,7},{4,0},{5,1},{6,2},{7,3},{8,12},{9,13},{10,... | collective-permute-start | bytes 589832 | tf_op jit(solution)/shard_map/ppermute | solution.py:46
  45.9 0.8 %level1.7.refs_4_.refs_0_ = f32[96,512]{1,0:T(8,128)S(1)} custom-call(f32[96,512]{1,0:T(8,128)S(1)} %level0.7.refs_4_.refs_0_, f32[96,512]{1,0:T(8,128)S(1)} %collective-permute-done.17.refs_1_, f32[96,512]{1,0:T(8,128)S(1)} %order.15.refs_1_.refs_2_, bf16[512,1024]{1,0:T(8,128)(2,1)S(1)} %get-tuple-element.28.refs_2_.refs_3_, ...), custom_call_target="tpu_custom_call" | custom-call | flops 4000000000 | bytes 1000 | tf_op jit(solution)/shard_map/level1/pallas_call | solution.py:101
  46.7 2.4 %collective-permute-start.18 = (f32[96,512]{1,0:T(8,128)S(1)}, f32[96,512]{1,0:T(8,128)S(1)}, u32[]{:S(2)}, u32[]{:S(2)}) collective-permute-start(f32[96,512]{1,0:T(8,128)S(1)} %level1.7.refs_4_.refs_0_), channel_id=1, source_target_pairs={{0,4},{1,5},{2,6},{3,7},{4,0},{5,1},{6,2},{7,3},{8,12},{9,13},{10,... | collective-permute-start | bytes 589832 | tf_op jit(solution)/shard_map/ppermute | solution.py:46
  49.2 1.0 %collective-permute-done.20.refs_1_ = f32[96,512]{1,0:T(8,128)S(1)} collective-permute-done((f32[96,512]{1,0:T(8,128)S(1)}, f32[96,512]{1,0:T(8,128)S(1)}, u32[]{:S(2)}, u32[]{:S(2)}) %collective-permute-start.20) | collective-permute-done | bytes 196640 | tf_op jit(solution)/shard_map/ppermute | solution.py:46
  50.2 0.8 %level2.6.refs_5_.refs_1_ = f32[96,512]{1,0:T(8,128)S(1)} custom-call(f32[96,512]{1,0:T(8,128)S(1)} %level1.6.refs_1_.refs_0_, f32[96,512]{1,0:T(8,128)S(1)} %collective-permute-done.20.refs_1_, bf16[512,1024]{1,0:T(8,128)(2,1)S(1)} %get-tuple-element.29.refs_2_.refs_1_, bf16[512,1024]{1,0:T(8,128)(2,1)S(1)} %get-tuple-element.27.refs_4_.refs_3_.refs_2_, ...), custom_call_target="tpu_custom_call" | custom-call | flops 4000000000 | bytes 1000 | tf_op jit(solution)/shard_map/level2/pallas_call | solution.py:101
  51.0 1.2 %collective-permute-start.24 = (f32[96,512]{1,0:T(8,128)S(1)}, f32[96,512]{1,0:T(8,128)S(1)}, u32[]{:S(2)}, u32[]{:S(2)}) collective-permute-start(f32[96,512]{1,0:T(8,128)S(1)} %level2.6.refs_5_.refs_1_), channel_id=1, source_target_pairs={{0,2},{1,3},{2,0},{3,1},{4,6},{5,7},{6,4},{7,5},{8,10},{9,11},{10,... | collective-permute-start | bytes 589832 | tf_op jit(solution)/shard_map/ppermute | solution.py:46
  52.1 0.8 %level1.8.refs_4_.refs_0_ = f32[128,512]{1,0:T(8,128)S(1)} custom-call(f32[128,512]{1,0:T(8,128)S(1)} %level0.8.refs_2_.refs_0_, f32[128,512]{1,0:T(8,128)S(1)} %collective-permute-done.19.refs_1_, f32[128,512]{1,0:T(8,128)S(1)} %order.16.refs_4_.refs_2_, bf16[512,1024]{1,0:T(8,128)(2,1)S(1)} %get-tuple-element.28.refs_2_.refs_3_, ...), custom_call_target="tpu_custom_call" | custom-call | flops 4000000000 | bytes 1000 | tf_op jit(solution)/shard_map/level1/pallas_call | solution.py:101
  52.9 1.8 %collective-permute-start.22 = (f32[128,512]{1,0:T(8,128)S(1)}, f32[128,512]{1,0:T(8,128)S(1)}, u32[]{:S(2)}, u32[]{:S(2)}) collective-permute-start(f32[128,512]{1,0:T(8,128)S(1)} %level1.8.refs_4_.refs_0_), channel_id=1, source_target_pairs={{0,4},{1,5},{2,6},{3,7},{4,0},{5,1},{6,2},{7,3},{8,12},{9,13},{10,... | collective-permute-start | bytes 786440 | tf_op jit(solution)/shard_map/ppermute | solution.py:46
  54.9 0.8 %level2.7.refs_5_.refs_2_ = f32[96,512]{1,0:T(8,128)S(1)} custom-call(f32[96,512]{1,0:T(8,128)S(1)} %level1.7.refs_4_.refs_0_, f32[96,512]{1,0:T(8,128)S(1)} %collective-permute-done.18.refs_1_, bf16[512,1024]{1,0:T(8,128)(2,1)S(1)} %get-tuple-element.29.refs_2_.refs_1_, bf16[512,1024]{1,0:T(8,128)(2,1)S(1)} %get-tuple-element.27.refs_4_.refs_3_.refs_2_, ...), custom_call_target="tpu_custom_call" | custom-call | flops 4000000000 | bytes 1000 | tf_op jit(solution)/shard_map/level2/pallas_call | solution.py:101
  55.7 1.4 %collective-permute-start.25 = (f32[96,512]{1,0:T(8,128)S(1)}, f32[96,512]{1,0:T(8,128)S(1)}, u32[]{:S(2)}, u32[]{:S(2)}) collective-permute-start(f32[96,512]{1,0:T(8,128)S(1)} %level2.7.refs_5_.refs_2_), channel_id=1, source_target_pairs={{0,2},{1,3},{2,0},{3,1},{4,6},{5,7},{6,4},{7,5},{8,10},{9,11},{10,... | collective-permute-start | bytes 589832 | tf_op jit(solution)/shard_map/ppermute | solution.py:46
  57.1 0.8 %level1.9.refs_0_ = f32[128,512]{1,0:T(8,128)S(1)} custom-call(f32[128,512]{1,0:T(8,128)S(1)} %level0.9.refs_2_.refs_0_, f32[128,512]{1,0:T(8,128)S(1)} %collective-permute-done.16.refs_1_, f32[128,512]{1,0:T(8,128)S(1)} %order.17.refs_5_.refs_2_, bf16[512,1024]{1,0:T(8,128)(2,1)S(1)} %get-tuple-element.28.refs_2_.refs_3_, ...), custom_call_target="tpu_custom_call" | custom-call | flops 4000000000 | bytes 1000 | tf_op jit(solution)/shard_map/level1/pallas_call | solution.py:101
  57.8 1.2 %collective-permute-start.21 = (f32[128,512]{1,0:T(8,128)S(1)}, f32[128,512]{1,0:T(8,128)S(1)}, u32[]{:S(2)}, u32[]{:S(2)}) collective-permute-start(f32[128,512]{1,0:T(8,128)S(1)} %level1.9.refs_0_), channel_id=1, source_target_pairs={{0,4},{1,5},{2,6},{3,7},{4,0},{5,1},{6,2},{7,3},{8,12},{9,13},{10,... | collective-permute-start | bytes 786440 | tf_op jit(solution)/shard_map/ppermute | solution.py:46
  59.0 0.4 ahead.2.refs_4_.refs_0_
  59.5 1.4 %collective-permute-done.22.refs_1_ = f32[128,512]{1,0:T(8,128)S(1)} collective-permute-done((f32[128,512]{1,0:T(8,128)S(1)}, f32[128,512]{1,0:T(8,128)S(1)}, u32[]{:S(2)}, u32[]{:S(2)}) %collective-permute-start.22) | collective-permute-done | bytes 262176 | tf_op jit(solution)/shard_map/ppermute | solution.py:46
  60.9 0.7 level2.8.refs_4_.refs_3_
  61.7 3.8 %collective-permute-done.21.refs_1_ = f32[128,512]{1,0:T(8,128)S(1)} collective-permute-done((f32[128,512]{1,0:T(8,128)S(1)}, f32[128,512]{1,0:T(8,128)S(1)}, u32[]{:S(2)}, u32[]{:S(2)}) %collective-permute-start.21) | collective-permute-done | bytes 262176 | tf_op jit(solution)/shard_map/ppermute | solution.py:46
  65.5 0.5 level2.9.refs_10_.refs_0_
  66.0 0.7 collective-permute-start.27
  66.7 2.3 %collective-permute-done.26.refs_7_ = f32[128,512]{1,0:T(8,128)S(1)} collective-permute-done((f32[128,512]{1,0:T(8,128)S(1)}, f32[128,512]{1,0:T(8,128)S(1)}, u32[]{:S(2)}, u32[]{:S(2)}) %collective-permute-start.26) | collective-permute-done | bytes 262176 | tf_op jit(solution)/shard_map/ppermute | solution.py:46
  69.0 2.4 %level3.2 = (f32[1,512,512]{2,1,0:T(8,128)}, f32[8,128]{1,0:T(8,128)S(1)}) custom-call(f32[64,512]{1,0:T(8,128)S(1)} %level2.5.refs_5_.refs_0_, f32[96,512]{1,0:T(8,128)S(1)} %level2.6.refs_5_.refs_1_, f32[96,512]{1,0:T(8,128)S(1)} %level2.7.refs_5_.refs_2_, f32[128,512]{1,0:T(8,128)S(1)} %level2.8.refs_4_.refs_3_, ...), custom_call_target="tpu_custom_call" | custom-call | flops 4000000000 | bytes 1000 | tf_op jit(solution)/shard_map/level3/pallas_call | solution.py:101
  71.4 0.5 ahead.3.refs_0_
  71.9 1.9 %collective-permute-done.27.refs_1_ = f32[128,512]{1,0:T(8,128)S(1)} collective-permute-done((f32[128,512]{1,0:T(8,128)S(1)}, f32[128,512]{1,0:T(8,128)S(1)}, u32[]{:S(2)}, u32[]{:S(2)}) %collective-permute-start.27) | collective-permute-done | bytes 262176 | tf_op jit(solution)/shard_map/ppermute | solution.py:46
  73.7 1.7 %level3.3 = (f32[1,512,512]{2,1,0:T(8,128)}, f32[8,128]{1,0:T(8,128)}) custom-call(f32[512,128]{1,0:T(8,128)S(1)} %ahead.3.refs_0_, f32[128,512]{1,0:T(8,128)S(1)} %collective-permute-done.27.refs_1_, bf16[512,1024]{1,0:T(8,128)(2,1)S(1)} %get-tuple-element.31.refs_8_.refs_1_.refs_2_, ...), custom_call_target="tpu_custom_call", output_to_operand_aliasing={{0}: (4, {})} | custom-call | flops 4000000000 | bytes 1000 | tf_op jit(solution)/shard_map/level3/pallas_call | solution.py:101
  (53 shorter events, 2.5 us)
Async XLA Ops:
  1.1 3.0 %copy-start = (f32[1,512,512]{2,1,0:T(8,128)S(1)}, f32[1,512,512]{2,1,0:T(8,128)}, u32[]{:S(2)}) copy-start(f32[1,512,512]{2,1,0:T(8,128)} %refs_0_.7) | copy-start | bytes 3145732
  1.1 7.3 %collective-permute-start = (f32[64,512]{1,0:T(8,128)S(1)}, f32[64,512]{1,0:T(8,128)S(1)}, u32[]{:S(2)}, u32[]{:S(2)}) collective-permute-start(f32[64,512]{1,0:T(8,128)S(1)} %order.9.refs_1_.refs_0_), channel_id=1, source_target_pairs={{0,16},{1,17},{2,18},{3,19},{4,20},{5,21},{6,22},{7,23},{8,24},{9,... | collective-permute-start | bytes 393224 | tf_op jit(solution)/shard_map/ppermute | solution.py:46
  4.7 2.2 %slice-start = ((s8[8388608]{0:T(1024)(128)(4,1)}), s8[4194304]{0:T(1024)(128)(4,1)S(1)}, s32[]{:S(2)}) async-start(s8[8388608]{0:T(1024)(128)(4,1)} %bitcast), calls=%async_computation | async-start | bytes 8388608
  4.7 3.5 %slice-start.1 = ((s8[8388608]{0:T(1024)(128)(4,1)}), s8[4194304]{0:T(1024)(128)(4,1)S(1)}, s32[]{:S(2)}) async-start(s8[8388608]{0:T(1024)(128)(4,1)} %bitcast), calls=%async_computation.1 | async-start | bytes 8388608
  4.7 10.2 %collective-permute-start.3 = (f32[96,512]{1,0:T(8,128)S(1)}, f32[96,512]{1,0:T(8,128)S(1)}, u32[]{:S(2)}, u32[]{:S(2)}) collective-permute-start(f32[96,512]{1,0:T(8,128)S(1)} %order.10.refs_1_.refs_0_), channel_id=1, source_target_pairs={{0,16},{1,17},{2,18},{3,19},{4,20},{5,21},{6,22},{7,23},{8,24},{9,... | collective-permute-start | bytes 589832 | tf_op jit(solution)/shard_map/ppermute | solution.py:46
  5.9 10.9 %collective-permute-start.2 = (f32[96,512]{1,0:T(8,128)S(1)}, f32[96,512]{1,0:T(8,128)S(1)}, u32[]{:S(2)}, u32[]{:S(2)}) collective-permute-start(f32[96,512]{1,0:T(8,128)S(1)} %order.11.refs_1_.refs_0_), channel_id=1, source_target_pairs={{0,16},{1,17},{2,18},{3,19},{4,20},{5,21},{6,22},{7,23},{8,24},{9,... | collective-permute-start | bytes 589832 | tf_op jit(solution)/shard_map/ppermute | solution.py:46
  9.2 8.8 %collective-permute-start.7 = (f32[64,512]{1,0:T(8,128)S(1)}, f32[64,512]{1,0:T(8,128)S(1)}, u32[]{:S(2)}, u32[]{:S(2)}) collective-permute-start(f32[64,512]{1,0:T(8,128)S(1)} %level0.5.refs_1_.refs_0_), channel_id=1, source_target_pairs={{0,8},{1,9},{2,10},{3,11},{4,12},{5,13},{6,14},{7,15},{8,0},{9,1},... | collective-permute-start | bytes 393224 | tf_op jit(solution)/shard_map/ppermute | solution.py:46
  12.6 12.4 %collective-permute-start.5 = (f32[128,512]{1,0:T(8,128)S(1)}, f32[128,512]{1,0:T(8,128)S(1)}, u32[]{:S(2)}, u32[]{:S(2)}) collective-permute-start(f32[128,512]{1,0:T(8,128)S(1)} %order.12.refs_1_.refs_0_), channel_id=1, source_target_pairs={{0,16},{1,17},{2,18},{3,19},{4,20},{5,21},{6,22},{7,23},{8,24},{9,... | collective-permute-start | bytes 786440 | tf_op jit(solution)/shard_map/ppermute | solution.py:46
  14.2 13.4 %collective-permute-start.1 = (f32[128,512]{1,0:T(8,128)S(1)}, f32[128,512]{1,0:T(8,128)S(1)}, u32[]{:S(2)}, u32[]{:S(2)}) collective-permute-start(f32[128,512]{1,0:T(8,128)S(1)} %order.13.refs_1_.refs_0_), channel_id=1, source_target_pairs={{0,16},{1,17},{2,18},{3,19},{4,20},{5,21},{6,22},{7,23},{8,24},{9,... | collective-permute-start | bytes 786440 | tf_op jit(solution)/shard_map/ppermute | solution.py:46
  15.8 6.4 %collective-permute-start.6 = (f32[96,512]{1,0:T(8,128)S(1)}, f32[96,512]{1,0:T(8,128)S(1)}, u32[]{:S(2)}, u32[]{:S(2)}) collective-permute-start(f32[96,512]{1,0:T(8,128)S(1)} %level0.6.refs_4_.refs_0_), channel_id=1, source_target_pairs={{0,1},{1,0},{2,3},{3,2},{4,8},{5,9},{6,10},{7,11},{8,4},{9,5},{10,... | collective-permute-start | bytes 589832 | tf_op jit(solution)/shard_map/ppermute | solution.py:46
  17.6 8.2 %collective-permute-start.4 = (f32[96,512]{1,0:T(8,128)S(1)}, f32[96,512]{1,0:T(8,128)S(1)}, u32[]{:S(2)}, u32[]{:S(2)}) collective-permute-start(f32[96,512]{1,0:T(8,128)S(1)} %level0.7.refs_4_.refs_0_), channel_id=1, source_target_pairs={{0,1},{1,0},{2,3},{3,2},{4,8},{5,9},{6,10},{7,11},{8,4},{9,5},{10,... | collective-permute-start | bytes 589832 | tf_op jit(solution)/shard_map/ppermute | solution.py:46
  18.9 21.3 %collective-permute-start.13 = (f32[64,512]{1,0:T(8,128)S(1)}, f32[64,512]{1,0:T(8,128)S(1)}, u32[]{:S(2)}, u32[]{:S(2)}) collective-permute-start(f32[64,512]{1,0:T(8,128)S(1)} %level1.5.refs_2_.refs_0_), channel_id=1, source_target_pairs={{0,4},{1,5},{2,6},{3,7},{4,0},{5,1},{6,2},{7,3},{8,12},{9,13},{10,... | collective-permute-start | bytes 393224 | tf_op jit(solution)/shard_map/ppermute | solution.py:46
  22.2 11.6 %collective-permute-start.9 = (f32[96,512]{1,0:T(8,128)S(1)}, f32[96,512]{1,0:T(8,128)S(1)}, u32[]{:S(2)}, u32[]{:S(2)}) collective-permute-start(f32[96,512]{1,0:T(8,128)S(1)} %pass.4.refs_4_), channel_id=1, source_target_pairs={{0,4},{1,5},{2,6},{3,7},{4,0},{5,1},{6,2},{7,3},{8,12},{9,13},{10,... | collective-permute-start | bytes 589832 | tf_op jit(solution)/shard_map/ppermute | solution.py:46
  25.7 2.7 %collective-permute-start.10 = (f32[128,512]{1,0:T(8,128)S(1)}, f32[128,512]{1,0:T(8,128)S(1)}, u32[]{:S(2)}, u32[]{:S(2)}) collective-permute-start(f32[128,512]{1,0:T(8,128)S(1)} %level0.8.refs_2_.refs_0_), channel_id=1, source_target_pairs={{0,1},{1,0},{2,3},{3,2},{4,8},{5,9},{6,10},{7,11},{8,4},{9,5},{10,... | collective-permute-start | bytes 786440 | tf_op jit(solution)/shard_map/ppermute | solution.py:46
  25.8 13.8 %collective-permute-start.15 = (f32[96,512]{1,0:T(8,128)S(1)}, f32[96,512]{1,0:T(8,128)S(1)}, u32[]{:S(2)}, u32[]{:S(2)}) collective-permute-start(f32[96,512]{1,0:T(8,128)S(1)} %pass.5.refs_4_), channel_id=1, source_target_pairs={{0,4},{1,5},{2,6},{3,7},{4,0},{5,1},{6,2},{7,3},{8,12},{9,13},{10,... | collective-permute-start | bytes 589832 | tf_op jit(solution)/shard_map/ppermute | solution.py:46
  28.4 5.4 %collective-permute-start.8 = (f32[128,512]{1,0:T(8,128)S(1)}, f32[128,512]{1,0:T(8,128)S(1)}, u32[]{:S(2)}, u32[]{:S(2)}) collective-permute-start(f32[128,512]{1,0:T(8,128)S(1)} %level0.9.refs_2_.refs_0_), channel_id=1, source_target_pairs={{0,1},{1,0},{2,3},{3,2},{4,8},{5,9},{6,10},{7,11},{8,4},{9,5},{10,... | collective-permute-start | bytes 786440 | tf_op jit(solution)/shard_map/ppermute | solution.py:46
  28.5 11.2 %collective-permute-start.14 = (f32[128,512]{1,0:T(8,128)S(1)}, f32[128,512]{1,0:T(8,128)S(1)}, u32[]{:S(2)}, u32[]{:S(2)}) collective-permute-start(f32[128,512]{1,0:T(8,128)S(1)} %pass.6.refs_1_), channel_id=1, source_target_pairs={{0,4},{1,5},{2,6},{3,7},{4,0},{5,1},{6,2},{7,3},{8,12},{9,13},{10,... | collective-permute-start | bytes 786440 | tf_op jit(solution)/shard_map/ppermute | solution.py:46
  33.7 8.9 %collective-permute-start.12 = (f32[96,512]{1,0:T(8,128)S(1)}, f32[96,512]{1,0:T(8,128)S(1)}, u32[]{:S(2)}, u32[]{:S(2)}) collective-permute-start(f32[96,512]{1,0:T(8,128)S(1)} %order.14.refs_2_), channel_id=1, source_target_pairs={{0,1},{1,0},{2,3},{3,2},{4,8},{5,9},{6,10},{7,11},{8,4},{9,5},{10,... | collective-permute-start | bytes 589832 | tf_op jit(solution)/shard_map/ppermute | solution.py:46
  33.8 12.2 %collective-permute-start.11 = (f32[128,512]{1,0:T(8,128)S(1)}, f32[128,512]{1,0:T(8,128)S(1)}, u32[]{:S(2)}, u32[]{:S(2)}) collective-permute-start(f32[128,512]{1,0:T(8,128)S(1)} %pass.7.refs_1_), channel_id=1, source_target_pairs={{0,4},{1,5},{2,6},{3,7},{4,0},{5,1},{6,2},{7,3},{8,12},{9,13},{10,... | collective-permute-start | bytes 786440 | tf_op jit(solution)/shard_map/ppermute | solution.py:46
  39.6 6.3 %collective-permute-start.17 = (f32[96,512]{1,0:T(8,128)S(1)}, f32[96,512]{1,0:T(8,128)S(1)}, u32[]{:S(2)}, u32[]{:S(2)}) collective-permute-start(f32[96,512]{1,0:T(8,128)S(1)} %order.15.refs_1_.refs_2_), channel_id=1, source_target_pairs={{0,1},{1,0},{2,3},{3,2},{4,8},{5,9},{6,10},{7,11},{8,4},{9,5},{10,... | collective-permute-start | bytes 589832 | tf_op jit(solution)/shard_map/ppermute | solution.py:46
  39.7 12.4 %collective-permute-start.19 = (f32[128,512]{1,0:T(8,128)S(1)}, f32[128,512]{1,0:T(8,128)S(1)}, u32[]{:S(2)}, u32[]{:S(2)}) collective-permute-start(f32[128,512]{1,0:T(8,128)S(1)} %order.16.refs_4_.refs_2_), channel_id=1, source_target_pairs={{0,1},{1,0},{2,3},{3,2},{4,8},{5,9},{6,10},{7,11},{8,4},{9,5},{10,... | collective-permute-start | bytes 786440 | tf_op jit(solution)/shard_map/ppermute | solution.py:46
  41.0 25.7 %collective-permute-start.23 = (f32[64,512]{1,0:T(8,128)S(1)}, f32[64,512]{1,0:T(8,128)S(1)}, u32[]{:S(2)}, u32[]{:S(2)}) collective-permute-start(f32[64,512]{1,0:T(8,128)S(1)} %level2.5.refs_5_.refs_0_), channel_id=1, source_target_pairs={{0,2},{1,3},{2,0},{3,1},{4,6},{5,7},{6,4},{7,5},{8,10},{9,11},{10,... | collective-permute-start | bytes 393224 | tf_op jit(solution)/shard_map/ppermute | solution.py:46
  43.4 6.8 %collective-permute-start.20 = (f32[96,512]{1,0:T(8,128)S(1)}, f32[96,512]{1,0:T(8,128)S(1)}, u32[]{:S(2)}, u32[]{:S(2)}) collective-permute-start(f32[96,512]{1,0:T(8,128)S(1)} %level1.6.refs_1_.refs_0_), channel_id=1, source_target_pairs={{0,4},{1,5},{2,6},{3,7},{4,0},{5,1},{6,2},{7,3},{8,12},{9,13},{10,... | collective-permute-start | bytes 589832 | tf_op jit(solution)/shard_map/ppermute | solution.py:46
  45.9 11.1 %collective-permute-start.16 = (f32[128,512]{1,0:T(8,128)S(1)}, f32[128,512]{1,0:T(8,128)S(1)}, u32[]{:S(2)}, u32[]{:S(2)}) collective-permute-start(f32[128,512]{1,0:T(8,128)S(1)} %order.17.refs_5_.refs_2_), channel_id=1, source_target_pairs={{0,1},{1,0},{2,3},{3,2},{4,8},{5,9},{6,10},{7,11},{8,4},{9,5},{10,... | collective-permute-start | bytes 786440 | tf_op jit(solution)/shard_map/ppermute | solution.py:46
  46.7 8.2 %collective-permute-start.18 = (f32[96,512]{1,0:T(8,128)S(1)}, f32[96,512]{1,0:T(8,128)S(1)}, u32[]{:S(2)}, u32[]{:S(2)}) collective-permute-start(f32[96,512]{1,0:T(8,128)S(1)} %level1.7.refs_4_.refs_0_), channel_id=1, source_target_pairs={{0,4},{1,5},{2,6},{3,7},{4,0},{5,1},{6,2},{7,3},{8,12},{9,13},{10,... | collective-permute-start | bytes 589832 | tf_op jit(solution)/shard_map/ppermute | solution.py:46
  51.0 15.7 %collective-permute-start.24 = (f32[96,512]{1,0:T(8,128)S(1)}, f32[96,512]{1,0:T(8,128)S(1)}, u32[]{:S(2)}, u32[]{:S(2)}) collective-permute-start(f32[96,512]{1,0:T(8,128)S(1)} %level2.6.refs_5_.refs_1_), channel_id=1, source_target_pairs={{0,2},{1,3},{2,0},{3,1},{4,6},{5,7},{6,4},{7,5},{8,10},{9,11},{10,... | collective-permute-start | bytes 589832 | tf_op jit(solution)/shard_map/ppermute | solution.py:46
  52.9 8.0 %collective-permute-start.22 = (f32[128,512]{1,0:T(8,128)S(1)}, f32[128,512]{1,0:T(8,128)S(1)}, u32[]{:S(2)}, u32[]{:S(2)}) collective-permute-start(f32[128,512]{1,0:T(8,128)S(1)} %level1.8.refs_4_.refs_0_), channel_id=1, source_target_pairs={{0,4},{1,5},{2,6},{3,7},{4,0},{5,1},{6,2},{7,3},{8,12},{9,13},{10,... | collective-permute-start | bytes 786440 | tf_op jit(solution)/shard_map/ppermute | solution.py:46
  55.7 11.0 %collective-permute-start.25 = (f32[96,512]{1,0:T(8,128)S(1)}, f32[96,512]{1,0:T(8,128)S(1)}, u32[]{:S(2)}, u32[]{:S(2)}) collective-permute-start(f32[96,512]{1,0:T(8,128)S(1)} %level2.7.refs_5_.refs_2_), channel_id=1, source_target_pairs={{0,2},{1,3},{2,0},{3,1},{4,6},{5,7},{6,4},{7,5},{8,10},{9,11},{10,... | collective-permute-start | bytes 589832 | tf_op jit(solution)/shard_map/ppermute | solution.py:46
  57.8 7.7 %collective-permute-start.21 = (f32[128,512]{1,0:T(8,128)S(1)}, f32[128,512]{1,0:T(8,128)S(1)}, u32[]{:S(2)}, u32[]{:S(2)}) collective-permute-start(f32[128,512]{1,0:T(8,128)S(1)} %level1.9.refs_0_), channel_id=1, source_target_pairs={{0,4},{1,5},{2,6},{3,7},{4,0},{5,1},{6,2},{7,3},{8,12},{9,13},{10,... | collective-permute-start | bytes 786440 | tf_op jit(solution)/shard_map/ppermute | solution.py:46
  61.7 7.3 %collective-permute-start.26 = (f32[128,512]{1,0:T(8,128)S(1)}, f32[128,512]{1,0:T(8,128)S(1)}, u32[]{:S(2)}, u32[]{:S(2)}) collective-permute-start(f32[128,512]{1,0:T(8,128)S(1)} %level2.8.refs_4_.refs_3_), channel_id=1, source_target_pairs={{0,2},{1,3},{2,0},{3,1},{4,6},{5,7},{6,4},{7,5},{8,10},{9,11},{10,... | collective-permute-start | bytes 786440 | tf_op jit(solution)/shard_map/ppermute | solution.py:46
  66.0 7.7 %collective-permute-start.27 = (f32[128,512]{1,0:T(8,128)S(1)}, f32[128,512]{1,0:T(8,128)S(1)}, u32[]{:S(2)}, u32[]{:S(2)}) collective-permute-start(f32[128,512]{1,0:T(8,128)S(1)} %level2.9.refs_10_.refs_0_), channel_id=1, source_target_pairs={{0,2},{1,3},{2,0},{3,1},{4,6},{5,7},{6,4},{7,5},{8,10},{9,11},{10,... | collective-permute-start | bytes 786440 | tf_op jit(solution)/shard_map/ppermute | solution.py:46

commit v3 on v2

--- a/solution.py
+++ b/solution.py
@@ -19,7 +19,7 @@
 DIRECT = (0,)
 RESULT_BLOCKS = ((0, 3), (3, 4))
 COST = 4000000000
-COSTS = {}
+COSTS = {'ahead': 1000000000}
 ORDER = (
     "in0 x0 in1 x1",
     "x2 m0 a0 x3",
@@ -28,9 +28,10 @@
     "p2 a4 p3 q1",
     "p4 m3 q2 q3",
     "c0 b1 q4 b2",
-    "c1 b3 c2 b4",
-    "cc4 c3 c4 d0",
-    "dd1 d1",
+    "cc1 c1 b3 cc2",
+    "c2 b4 cc3 cc4",
+    "c3 c4 d0 dd1",
+    "d1",
 )
 
 
@@ -162,10 +163,22 @@
 
         def fetched(c_ref, *refs):
             outs, (held, sem) = refs[:-2], refs[-2:]
-            copy = pltpu.make_async_copy(c_ref.at[0, :, low:high], held, sem)
-            copy.start()
-            copy.wait()
-            lay(held[...], start - low, outs)
+            copies = []
+            for half in range(2):
+                part = slice(half * rank // 2, (half + 1) * rank // 2)
+                copies.append(
+                    pltpu.make_async_copy(
+                        c_ref.at[0, part, low:high], held.at[part], sem.at[half]
+                    )
+                )
+                copies[half].start()
+            for half in range(2):
+                part = slice(half * rank // 2, (half + 1) * rank // 2)
+                copies[half].wait()
+                at = start - low
+                for o_ref in outs:
+                    o_ref[:, part] = held[part, at : at + o_ref.shape[0]].T
+                    at += o_ref.shape[0]
 
         def whole(c_ref, *outs):
             lay(c_ref[0], start, outs)
@@ -175,7 +188,7 @@
                 o_ref[...] = block[:, at : at + o_ref.shape[0]].T
                 at += o_ref.shape[0]
 
-        scratch = [pltpu.VMEM((rank, high - low), F32), pltpu.SemaphoreType.DMA]
+        scratch = [pltpu.VMEM((rank, high - low), F32), pltpu.SemaphoreType.DMA((2,))]
         out = chain(
             "columns",
             whole if part else fetched,

time: 75.5 us -> 75.3 us (level)
  waiting for transfers between devices: 12 us -> 10.8 us
    ppermute x28, waiting for transfers between devices: 12 us -> 10.8 us  [send(): return lax.ppermute(block, AXES, [(i, partner(i)) for i in range(count)])]
    pallas_call x38 -> x41, Pallas kernels: 19.3 us -> 19.8 us  [__call__(): pl.pallas_call(kernel, out_shape=outs, in_specs=specs, out_specs=[HBM, VM...]
  transfers between devices with their start and end apart: 28 -> 28, of which waited for: 8 -> 7; matrix products, arithmetic and copies ran while one was open for 0% -> 0% of each run, Pallas kernels for 22% -> 23%
where the time goes in v3:
time: 75.3 us; the launch traced here: 75.1 us
  starting transfers between devices  42.9 us (57%)
  Pallas kernels  19.8 us (26%)
  waiting for transfers between devices  10.8 us (14%)
  local copies, waits for them, and re-layouts  1.36 us (2%)
    ppermute x28, starting transfers between devices, send(): return lax.ppermute(block, AXES, [(i, partner(i)) for i in range(count)])  42.9 us
    pallas_call x41, Pallas kernels, __call__(): pl.pallas_call(kernel, out_shape=outs, in_specs=specs, out_specs=[HBM, VM...  19.8 us
    ppermute x28, waiting for transfers between devices, send(): return lax.ppermute(block, AXES, [(i, partner(i)) for i in range(count)])  10.8 us
  transfers between devices with their start and end apart: 28, of which 7 were waited for; matrix products, arithmetic and copies ran while one was open for 0% of the time, Pallas kernels for 23%

profile of v3, /device:TPU:0, one launch (start us, length us, event | category | flops | bytes accessed | tf_op | source)
XLA Modules:
  0.0 75.1 jit_solution(16694475605749581119)
XLA Ops:
  0.0 1.1 %columns.2.refs_0_ = f32[64,512]{1,0:T(8,128)S(1)} custom-call(f32[1,512,512]{2,1,0:T(8,128)} %refs_0_.7), custom_call_target="tpu_custom_call" | custom-call | flops 4000000000 | bytes 1000 | tf_op jit(solution)/shard_map/columns/pallas_call | solution.py:102
  1.1 3.0 %collective-permute-start = (f32[64,512]{1,0:T(8,128)S(1)}, f32[64,512]{1,0:T(8,128)S(1)}, u32[]{:S(2)}, u32[]{:S(2)}) collective-permute-start(f32[64,512]{1,0:T(8,128)S(1)} %order.9.refs_1_.refs_0_), channel_id=1, source_target_pairs={{0,16},{1,17},{2,18},{3,19},{4,20},{5,21},{6,22},{7,23},{8,24},{9,... | collective-permute-start | bytes 393224 | tf_op jit(solution)/shard_map/ppermute | solution.py:47
  4.1 0.6 columns.3
  4.7 1.2 %collective-permute-start.3 = (f32[96,512]{1,0:T(8,128)S(1)}, f32[96,512]{1,0:T(8,128)S(1)}, u32[]{:S(2)}, u32[]{:S(2)}) collective-permute-start(f32[96,512]{1,0:T(8,128)S(1)} %order.10.refs_1_.refs_0_), channel_id=1, source_target_pairs={{0,16},{1,17},{2,18},{3,19},{4,20},{5,21},{6,22},{7,23},{8,24},{9,... | collective-permute-start | bytes 589832 | tf_op jit(solution)/shard_map/ppermute | solution.py:47
  5.9 0.9 %collective-permute-start.2 = (f32[96,512]{1,0:T(8,128)S(1)}, f32[96,512]{1,0:T(8,128)S(1)}, u32[]{:S(2)}, u32[]{:S(2)}) collective-permute-start(f32[96,512]{1,0:T(8,128)S(1)} %order.11.refs_1_.refs_0_), channel_id=1, source_target_pairs={{0,16},{1,17},{2,18},{3,19},{4,20},{5,21},{6,22},{7,23},{8,24},{9,... | collective-permute-start | bytes 589832 | tf_op jit(solution)/shard_map/ppermute | solution.py:47
  6.9 1.3 %slice-done.1 = s8[4194304]{0:T(1024)(128)(4,1)S(1)} async-done(((s8[8388608]{0:T(1024)(128)(4,1)}), s8[4194304]{0:T(1024)(128)(4,1)S(1)}, s32[]{:S(2)}) %slice-start.1) | async-done | bytes 4194328
  8.5 0.8 %level0.5.refs_1_.refs_0_ = f32[64,512]{1,0:T(8,128)S(1)} custom-call(f32[64,512]{1,0:T(8,128)S(1)} %order.9.refs_1_.refs_0_, f32[64,512]{1,0:T(8,128)S(1)} %collective-permute-done.refs_1_, bf16[512,1024]{1,0:T(8,128)(2,1)S(1)} %get-tuple-element.24.refs_2_, bf16[512,1024]{1,0:T(8,128)(2,1)S(1)} %get-tuple-element.25.refs_3_), custom_call_target="tpu_custom_call" | custom-call | flops 4000000000 | bytes 1000 | tf_op jit(solution)/shard_map/level0/pallas_call | solution.py:102
  9.3 3.0 %collective-permute-start.7 = (f32[64,512]{1,0:T(8,128)S(1)}, f32[64,512]{1,0:T(8,128)S(1)}, u32[]{:S(2)}, u32[]{:S(2)}) collective-permute-start(f32[64,512]{1,0:T(8,128)S(1)} %level0.5.refs_1_.refs_0_), channel_id=1, source_target_pairs={{0,8},{1,9},{2,10},{3,11},{4,12},{5,13},{6,14},{7,15},{8,0},{9,1},... | collective-permute-start | bytes 393224 | tf_op jit(solution)/shard_map/ppermute | solution.py:47
  12.6 1.6 %collective-permute-start.5 = (f32[128,512]{1,0:T(8,128)S(1)}, f32[128,512]{1,0:T(8,128)S(1)}, u32[]{:S(2)}, u32[]{:S(2)}) collective-permute-start(f32[128,512]{1,0:T(8,128)S(1)} %order.12.refs_1_.refs_0_), channel_id=1, source_target_pairs={{0,16},{1,17},{2,18},{3,19},{4,20},{5,21},{6,22},{7,23},{8,24},{9,... | collective-permute-start | bytes 786440 | tf_op jit(solution)/shard_map/ppermute | solution.py:47
  15.0 0.8 %level0.6.refs_4_.refs_0_ = f32[96,512]{1,0:T(8,128)S(1)} custom-call(f32[96,512]{1,0:T(8,128)S(1)} %order.10.refs_1_.refs_0_, f32[96,512]{1,0:T(8,128)S(1)} %collective-permute-done.3.refs_1_, bf16[512,1024]{1,0:T(8,128)(2,1)S(1)} %get-tuple-element.24.refs_2_, bf16[512,1024]{1,0:T(8,128)(2,1)S(1)} %get-tuple-element.25.refs_3_, ...), custom_call_target="tpu_custom_call" | custom-call | flops 4000000000 | bytes 1000 | tf_op jit(solution)/shard_map/level0/pallas_call | solution.py:102
  15.8 1.0 %collective-permute-done.2.refs_1_ = f32[96,512]{1,0:T(8,128)S(1)} collective-permute-done((f32[96,512]{1,0:T(8,128)S(1)}, f32[96,512]{1,0:T(8,128)S(1)}, u32[]{:S(2)}, u32[]{:S(2)}) %collective-permute-start.2) | collective-permute-done | bytes 196640 | tf_op jit(solution)/shard_map/ppermute | solution.py:47
  16.8 0.8 %level0.7.refs_4_.refs_0_ = f32[96,512]{1,0:T(8,128)S(1)} custom-call(f32[96,512]{1,0:T(8,128)S(1)} %order.11.refs_1_.refs_0_, f32[96,512]{1,0:T(8,128)S(1)} %collective-permute-done.2.refs_1_, bf16[512,1024]{1,0:T(8,128)(2,1)S(1)} %get-tuple-element.24.refs_2_, bf16[512,1024]{1,0:T(8,128)(2,1)S(1)} %get-tuple-element.25.refs_3_, ...), custom_call_target="tpu_custom_call" | custom-call | flops 4000000000 | bytes 1000 | tf_op jit(solution)/shard_map/level0/pallas_call | solution.py:102
  18.1 0.8 %level1.5.refs_2_.refs_0_ = f32[64,512]{1,0:T(8,128)S(1)} custom-call(f32[64,512]{1,0:T(8,128)S(1)} %level0.5.refs_1_.refs_0_, f32[64,512]{1,0:T(8,128)S(1)} %collective-permute-done.7.refs_1_, bf16[512,1024]{1,0:T(8,128)(2,1)S(1)} %get-tuple-element.28.refs_2_.refs_3_, bf16[512,1024]{1,0:T(8,128)(2,1)S(1)} %get-tuple-element.26.refs_1_.refs_3_.refs_4_, ...), custom_call_target="tpu_custom_call" | custom-call | flops 4000000000 | bytes 1000 | tf_op jit(solution)/shard_map/level1/pallas_call | solution.py:102
  18.9 3.2 %collective-permute-start.13 = (f32[64,512]{1,0:T(8,128)S(1)}, f32[64,512]{1,0:T(8,128)S(1)}, u32[]{:S(2)}, u32[]{:S(2)}) collective-permute-start(f32[64,512]{1,0:T(8,128)S(1)} %level1.5.refs_2_.refs_0_), channel_id=1, source_target_pairs={{0,4},{1,5},{2,6},{3,7},{4,0},{5,1},{6,2},{7,3},{8,12},{9,13},{10,... | collective-permute-start | bytes 393224 | tf_op jit(solution)/shard_map/ppermute | solution.py:47
  22.2 2.8 %collective-permute-start.9 = (f32[96,512]{1,0:T(8,128)S(1)}, f32[96,512]{1,0:T(8,128)S(1)}, u32[]{:S(2)}, u32[]{:S(2)}) collective-permute-start(f32[96,512]{1,0:T(8,128)S(1)} %pass.4.refs_4_), channel_id=1, source_target_pairs={{0,4},{1,5},{2,6},{3,7},{4,0},{5,1},{6,2},{7,3},{8,12},{9,13},{10,... | collective-permute-start | bytes 589832 | tf_op jit(solution)/shard_map/ppermute | solution.py:47
  25.0 0.7 level0.8.refs_2_.refs_0_
  25.9 1.8 %collective-permute-start.15 = (f32[96,512]{1,0:T(8,128)S(1)}, f32[96,512]{1,0:T(8,128)S(1)}, u32[]{:S(2)}, u32[]{:S(2)}) collective-permute-start(f32[96,512]{1,0:T(8,128)S(1)} %pass.5.refs_4_), channel_id=1, source_target_pairs={{0,4},{1,5},{2,6},{3,7},{4,0},{5,1},{6,2},{7,3},{8,12},{9,13},{10,... | collective-permute-start | bytes 589832 | tf_op jit(solution)/shard_map/ppermute | solution.py:47
  27.6 0.7 level0.9.refs_2_.refs_0_
  28.5 5.2 %collective-permute-start.14 = (f32[128,512]{1,0:T(8,128)S(1)}, f32[128,512]{1,0:T(8,128)S(1)}, u32[]{:S(2)}, u32[]{:S(2)}) collective-permute-start(f32[128,512]{1,0:T(8,128)S(1)} %pass.6.refs_1_), channel_id=1, source_target_pairs={{0,4},{1,5},{2,6},{3,7},{4,0},{5,1},{6,2},{7,3},{8,12},{9,13},{10,... | collective-permute-start | bytes 786440 | tf_op jit(solution)/shard_map/ppermute | solution.py:47
  33.8 5.6 %collective-permute-start.11 = (f32[128,512]{1,0:T(8,128)S(1)}, f32[128,512]{1,0:T(8,128)S(1)}, u32[]{:S(2)}, u32[]{:S(2)}) collective-permute-start(f32[128,512]{1,0:T(8,128)S(1)} %pass.7.refs_1_), channel_id=1, source_target_pairs={{0,4},{1,5},{2,6},{3,7},{4,0},{5,1},{6,2},{7,3},{8,12},{9,13},{10,... | collective-permute-start | bytes 786440 | tf_op jit(solution)/shard_map/ppermute | solution.py:47
  39.8 0.5 collective-permute-start.18
  40.2 0.8 %level2.5.refs_5_.refs_0_ = f32[64,512]{1,0:T(8,128)S(1)} custom-call(f32[64,512]{1,0:T(8,128)S(1)} %level1.5.refs_2_.refs_0_, f32[64,512]{1,0:T(8,128)S(1)} %collective-permute-done.13.refs_1_, bf16[512,1024]{1,0:T(8,128)(2,1)S(1)} %get-tuple-element.29.refs_2_.refs_1_, bf16[512,1024]{1,0:T(8,128)(2,1)S(1)} %get-tuple-element.27.refs_4_.refs_3_.refs_2_, ...), custom_call_target="tpu_custom_call" | custom-call | flops 4000000000 | bytes 1000 | tf_op jit(solution)/shard_map/level2/pallas_call | solution.py:102
  41.0 1.6 %collective-permute-start.23 = (f32[64,512]{1,0:T(8,128)S(1)}, f32[64,512]{1,0:T(8,128)S(1)}, u32[]{:S(2)}, u32[]{:S(2)}) collective-permute-start(f32[64,512]{1,0:T(8,128)S(1)} %level2.5.refs_5_.refs_0_), channel_id=1, source_target_pairs={{0,2},{1,3},{2,0},{3,1},{4,6},{5,7},{6,4},{7,5},{8,10},{9,11},{10,... | collective-permute-start | bytes 393224 | tf_op jit(solution)/shard_map/ppermute | solution.py:47
  42.6 0.8 %level1.6.refs_1_.refs_0_ = f32[96,512]{1,0:T(8,128)S(1)} custom-call(f32[96,512]{1,0:T(8,128)S(1)} %level0.6.refs_4_.refs_0_, f32[96,512]{1,0:T(8,128)S(1)} %collective-permute-done.12.refs_1_, f32[96,512]{1,0:T(8,128)S(1)} %order.14.refs_2_, bf16[512,1024]{1,0:T(8,128)(2,1)S(1)} %get-tuple-element.28.refs_2_.refs_3_, ...), custom_call_target="tpu_custom_call" | custom-call | flops 4000000000 | bytes 1000 | tf_op jit(solution)/shard_map/level1/pallas_call | solution.py:102
  43.4 2.5 %collective-permute-start.19 = (f32[96,512]{1,0:T(8,128)S(1)}, f32[96,512]{1,0:T(8,128)S(1)}, u32[]{:S(2)}, u32[]{:S(2)}) collective-permute-start(f32[96,512]{1,0:T(8,128)S(1)} %level1.6.refs_1_.refs_0_), channel_id=1, source_target_pairs={{0,4},{1,5},{2,6},{3,7},{4,0},{5,1},{6,2},{7,3},{8,12},{9,13},{10,... | collective-permute-start | bytes 589832 | tf_op jit(solution)/shard_map/ppermute | solution.py:47
  46.0 0.8 %level1.7.refs_3_.refs_0_ = f32[96,512]{1,0:T(8,128)S(1)} custom-call(f32[96,512]{1,0:T(8,128)S(1)} %level0.7.refs_4_.refs_0_, f32[96,512]{1,0:T(8,128)S(1)} %collective-permute-done.17.refs_1_, f32[96,512]{1,0:T(8,128)S(1)} %order.15.refs_1_.refs_2_, bf16[512,1024]{1,0:T(8,128)(2,1)S(1)} %get-tuple-element.28.refs_2_.refs_3_, ...), custom_call_target="tpu_custom_call" | custom-call | flops 4000000000 | bytes 1000 | tf_op jit(solution)/shard_map/level1/pallas_call | solution.py:102
  46.8 2.4 %collective-permute-start.20 = (f32[96,512]{1,0:T(8,128)S(1)}, f32[96,512]{1,0:T(8,128)S(1)}, u32[]{:S(2)}, u32[]{:S(2)}) collective-permute-start(f32[96,512]{1,0:T(8,128)S(1)} %level1.7.refs_3_.refs_0_), channel_id=1, source_target_pairs={{0,4},{1,5},{2,6},{3,7},{4,0},{5,1},{6,2},{7,3},{8,12},{9,13},{10,... | collective-permute-start | bytes 589832 | tf_op jit(solution)/shard_map/ppermute | solution.py:47
  49.2 0.5 ahead.5.refs_0_
  49.7 0.5 collective-permute-done.19.refs_1_
  50.2 0.5 level2.6.refs_5_.refs_1_
  50.7 1.7 %collective-permute-start.24 = (f32[96,512]{1,0:T(8,128)S(1)}, f32[96,512]{1,0:T(8,128)S(1)}, u32[]{:S(2)}, u32[]{:S(2)}) collective-permute-start(f32[96,512]{1,0:T(8,128)S(1)} %level2.6.refs_5_.refs_1_), channel_id=1, source_target_pairs={{0,2},{1,3},{2,0},{3,1},{4,6},{5,7},{6,4},{7,5},{8,10},{9,11},{10,... | collective-permute-start | bytes 589832 | tf_op jit(solution)/shard_map/ppermute | solution.py:47
  52.3 0.8 level1.8.refs_3_.refs_0_
  53.1 1.4 %collective-permute-start.22 = (f32[128,512]{1,0:T(8,128)S(1)}, f32[128,512]{1,0:T(8,128)S(1)}, u32[]{:S(2)}, u32[]{:S(2)}) collective-permute-start(f32[128,512]{1,0:T(8,128)S(1)} %level1.8.refs_3_.refs_0_), channel_id=1, source_target_pairs={{0,4},{1,5},{2,6},{3,7},{4,0},{5,1},{6,2},{7,3},{8,12},{9,13},{10,... | collective-permute-start | bytes 786440 | tf_op jit(solution)/shard_map/ppermute | solution.py:47
  54.5 0.5 ahead.6.refs_0_
  55.0 0.5 level2.7.refs_5_.refs_2_
  55.5 1.6 %collective-permute-start.25 = (f32[96,512]{1,0:T(8,128)S(1)}, f32[96,512]{1,0:T(8,128)S(1)}, u32[]{:S(2)}, u32[]{:S(2)}) collective-permute-start(f32[96,512]{1,0:T(8,128)S(1)} %level2.7.refs_5_.refs_2_), channel_id=1, source_target_pairs={{0,2},{1,3},{2,0},{3,1},{4,6},{5,7},{6,4},{7,5},{8,10},{9,11},{10,... | collective-permute-start | bytes 589832 | tf_op jit(solution)/shard_map/ppermute | solution.py:47
  57.0 0.8 level1.9.refs_3_.refs_0_
  57.8 1.0 %collective-permute-start.21 = (f32[128,512]{1,0:T(8,128)S(1)}, f32[128,512]{1,0:T(8,128)S(1)}, u32[]{:S(2)}, u32[]{:S(2)}) collective-permute-start(f32[128,512]{1,0:T(8,128)S(1)} %level1.9.refs_3_.refs_0_), channel_id=1, source_target_pairs={{0,4},{1,5},{2,6},{3,7},{4,0},{5,1},{6,2},{7,3},{8,12},{9,13},{10,... | collective-permute-start | bytes 786440 | tf_op jit(solution)/shard_map/ppermute | solution.py:47
  59.3 0.5 ahead.8.refs_4_.refs_0_
  59.7 1.2 %collective-permute-done.22.refs_1_ = f32[128,512]{1,0:T(8,128)S(1)} collective-permute-done((f32[128,512]{1,0:T(8,128)S(1)}, f32[128,512]{1,0:T(8,128)S(1)}, u32[]{:S(2)}, u32[]{:S(2)}) %collective-permute-start.22) | collective-permute-done | bytes 262176 | tf_op jit(solution)/shard_map/ppermute | solution.py:47
  61.8 3.7 %collective-permute-done.21.refs_1_ = f32[128,512]{1,0:T(8,128)S(1)} collective-permute-done((f32[128,512]{1,0:T(8,128)S(1)}, f32[128,512]{1,0:T(8,128)S(1)}, u32[]{:S(2)}, u32[]{:S(2)}) %collective-permute-start.21) | collective-permute-done | bytes 262176 | tf_op jit(solution)/shard_map/ppermute | solution.py:47
  65.5 0.5 level2.9.refs_10_.refs_0_
  66.0 0.7 collective-permute-start.27
  66.7 1.7 %collective-permute-done.26.refs_7_ = f32[128,512]{1,0:T(8,128)S(1)} collective-permute-done((f32[128,512]{1,0:T(8,128)S(1)}, f32[128,512]{1,0:T(8,128)S(1)}, u32[]{:S(2)}, u32[]{:S(2)}) %collective-permute-start.26) | collective-permute-done | bytes 262176 | tf_op jit(solution)/shard_map/ppermute | solution.py:47
  68.4 2.4 %level3.2 = (f32[1,512,512]{2,1,0:T(8,128)}, f32[8,128]{1,0:T(8,128)S(1)}) custom-call(f32[64,512]{1,0:T(8,128)S(1)} %level2.5.refs_5_.refs_0_, f32[96,512]{1,0:T(8,128)S(1)} %level2.6.refs_5_.refs_1_, f32[96,512]{1,0:T(8,128)S(1)} %level2.7.refs_5_.refs_2_, f32[128,512]{1,0:T(8,128)S(1)} %level2.8.refs_4_.refs_3_, ...), custom_call_target="tpu_custom_call" | custom-call | flops 4000000000 | bytes 1000 | tf_op jit(solution)/shard_map/level3/pallas_call | solution.py:102
  70.8 0.5 ahead.9.refs_0_
  71.3 2.2 %collective-permute-done.27.refs_1_ = f32[128,512]{1,0:T(8,128)S(1)} collective-permute-done((f32[128,512]{1,0:T(8,128)S(1)}, f32[128,512]{1,0:T(8,128)S(1)}, u32[]{:S(2)}, u32[]{:S(2)}) %collective-permute-start.27) | collective-permute-done | bytes 262176 | tf_op jit(solution)/shard_map/ppermute | solution.py:47
  73.4 1.7 %level3.3 = (f32[1,512,512]{2,1,0:T(8,128)}, f32[8,128]{1,0:T(8,128)}) custom-call(f32[512,128]{1,0:T(8,128)S(1)} %ahead.9.refs_0_, f32[128,512]{1,0:T(8,128)S(1)} %collective-permute-done.27.refs_1_, bf16[512,1024]{1,0:T(8,128)(2,1)S(1)} %get-tuple-element.31.refs_8_.refs_1_.refs_2_, ...), custom_call_target="tpu_custom_call", output_to_operand_aliasing={{0}: (4, {})} | custom-call | flops 4000000000 | bytes 1000 | tf_op jit(solution)/shard_map/level3/pallas_call | solution.py:102
  (56 shorter events, 4.0 us)
Async XLA Ops:
  1.1 3.0 %copy-start = (f32[1,512,512]{2,1,0:T(8,128)S(1)}, f32[1,512,512]{2,1,0:T(8,128)}, u32[]{:S(2)}) copy-start(f32[1,512,512]{2,1,0:T(8,128)} %refs_0_.7) | copy-start | bytes 3145732
  1.1 7.3 %collective-permute-start = (f32[64,512]{1,0:T(8,128)S(1)}, f32[64,512]{1,0:T(8,128)S(1)}, u32[]{:S(2)}, u32[]{:S(2)}) collective-permute-start(f32[64,512]{1,0:T(8,128)S(1)} %order.9.refs_1_.refs_0_), channel_id=1, source_target_pairs={{0,16},{1,17},{2,18},{3,19},{4,20},{5,21},{6,22},{7,23},{8,24},{9,... | collective-permute-start | bytes 393224 | tf_op jit(solution)/shard_map/ppermute | solution.py:47
  4.7 2.2 %slice-start = ((s8[8388608]{0:T(1024)(128)(4,1)}), s8[4194304]{0:T(1024)(128)(4,1)S(1)}, s32[]{:S(2)}) async-start(s8[8388608]{0:T(1024)(128)(4,1)} %bitcast), calls=%async_computation | async-start | bytes 8388608
  4.7 3.5 %slice-start.1 = ((s8[8388608]{0:T(1024)(128)(4,1)}), s8[4194304]{0:T(1024)(128)(4,1)S(1)}, s32[]{:S(2)}) async-start(s8[8388608]{0:T(1024)(128)(4,1)} %bitcast), calls=%async_computation.1 | async-start | bytes 8388608
  4.7 10.2 %collective-permute-start.3 = (f32[96,512]{1,0:T(8,128)S(1)}, f32[96,512]{1,0:T(8,128)S(1)}, u32[]{:S(2)}, u32[]{:S(2)}) collective-permute-start(f32[96,512]{1,0:T(8,128)S(1)} %order.10.refs_1_.refs_0_), channel_id=1, source_target_pairs={{0,16},{1,17},{2,18},{3,19},{4,20},{5,21},{6,22},{7,23},{8,24},{9,... | collective-permute-start | bytes 589832 | tf_op jit(solution)/shard_map/ppermute | solution.py:47
  5.9 10.9 %collective-permute-start.2 = (f32[96,512]{1,0:T(8,128)S(1)}, f32[96,512]{1,0:T(8,128)S(1)}, u32[]{:S(2)}, u32[]{:S(2)}) collective-permute-start(f32[96,512]{1,0:T(8,128)S(1)} %order.11.refs_1_.refs_0_), channel_id=1, source_target_pairs={{0,16},{1,17},{2,18},{3,19},{4,20},{5,21},{6,22},{7,23},{8,24},{9,... | collective-permute-start | bytes 589832 | tf_op jit(solution)/shard_map/ppermute | solution.py:47
  9.3 8.8 %collective-permute-start.7 = (f32[64,512]{1,0:T(8,128)S(1)}, f32[64,512]{1,0:T(8,128)S(1)}, u32[]{:S(2)}, u32[]{:S(2)}) collective-permute-start(f32[64,512]{1,0:T(8,128)S(1)} %level0.5.refs_1_.refs_0_), channel_id=1, source_target_pairs={{0,8},{1,9},{2,10},{3,11},{4,12},{5,13},{6,14},{7,15},{8,0},{9,1},... | collective-permute-start | bytes 393224 | tf_op jit(solution)/shard_map/ppermute | solution.py:47
  12.6 12.4 %collective-permute-start.5 = (f32[128,512]{1,0:T(8,128)S(1)}, f32[128,512]{1,0:T(8,128)S(1)}, u32[]{:S(2)}, u32[]{:S(2)}) collective-permute-start(f32[128,512]{1,0:T(8,128)S(1)} %order.12.refs_1_.refs_0_), channel_id=1, source_target_pairs={{0,16},{1,17},{2,18},{3,19},{4,20},{5,21},{6,22},{7,23},{8,24},{9,... | collective-permute-start | bytes 786440 | tf_op jit(solution)/shard_map/ppermute | solution.py:47
  14.2 13.4 %collective-permute-start.1 = (f32[128,512]{1,0:T(8,128)S(1)}, f32[128,512]{1,0:T(8,128)S(1)}, u32[]{:S(2)}, u32[]{:S(2)}) collective-permute-start(f32[128,512]{1,0:T(8,128)S(1)} %order.13.refs_1_.refs_0_), channel_id=1, source_target_pairs={{0,16},{1,17},{2,18},{3,19},{4,20},{5,21},{6,22},{7,23},{8,24},{9,... | collective-permute-start | bytes 786440 | tf_op jit(solution)/shard_map/ppermute | solution.py:47
  15.8 6.4 %collective-permute-start.6 = (f32[96,512]{1,0:T(8,128)S(1)}, f32[96,512]{1,0:T(8,128)S(1)}, u32[]{:S(2)}, u32[]{:S(2)}) collective-permute-start(f32[96,512]{1,0:T(8,128)S(1)} %level0.6.refs_4_.refs_0_), channel_id=1, source_target_pairs={{0,1},{1,0},{2,3},{3,2},{4,8},{5,9},{6,10},{7,11},{8,4},{9,5},{10,... | collective-permute-start | bytes 589832 | tf_op jit(solution)/shard_map/ppermute | solution.py:47
  17.6 8.2 %collective-permute-start.4 = (f32[96,512]{1,0:T(8,128)S(1)}, f32[96,512]{1,0:T(8,128)S(1)}, u32[]{:S(2)}, u32[]{:S(2)}) collective-permute-start(f32[96,512]{1,0:T(8,128)S(1)} %level0.7.refs_4_.refs_0_), channel_id=1, source_target_pairs={{0,1},{1,0},{2,3},{3,2},{4,8},{5,9},{6,10},{7,11},{8,4},{9,5},{10,... | collective-permute-start | bytes 589832 | tf_op jit(solution)/shard_map/ppermute | solution.py:47
  18.9 21.3 %collective-permute-start.13 = (f32[64,512]{1,0:T(8,128)S(1)}, f32[64,512]{1,0:T(8,128)S(1)}, u32[]{:S(2)}, u32[]{:S(2)}) collective-permute-start(f32[64,512]{1,0:T(8,128)S(1)} %level1.5.refs_2_.refs_0_), channel_id=1, source_target_pairs={{0,4},{1,5},{2,6},{3,7},{4,0},{5,1},{6,2},{7,3},{8,12},{9,13},{10,... | collective-permute-start | bytes 393224 | tf_op jit(solution)/shard_map/ppermute | solution.py:47
  22.2 11.6 %collective-permute-start.9 = (f32[96,512]{1,0:T(8,128)S(1)}, f32[96,512]{1,0:T(8,128)S(1)}, u32[]{:S(2)}, u32[]{:S(2)}) collective-permute-start(f32[96,512]{1,0:T(8,128)S(1)} %pass.4.refs_4_), channel_id=1, source_target_pairs={{0,4},{1,5},{2,6},{3,7},{4,0},{5,1},{6,2},{7,3},{8,12},{9,13},{10,... | collective-permute-start | bytes 589832 | tf_op jit(solution)/shard_map/ppermute | solution.py:47
  25.7 2.7 %collective-permute-start.10 = (f32[128,512]{1,0:T(8,128)S(1)}, f32[128,512]{1,0:T(8,128)S(1)}, u32[]{:S(2)}, u32[]{:S(2)}) collective-permute-start(f32[128,512]{1,0:T(8,128)S(1)} %level0.8.refs_2_.refs_0_), channel_id=1, source_target_pairs={{0,1},{1,0},{2,3},{3,2},{4,8},{5,9},{6,10},{7,11},{8,4},{9,5},{10,... | collective-permute-start | bytes 786440 | tf_op jit(solution)/shard_map/ppermute | solution.py:47
  25.9 13.8 %collective-permute-start.15 = (f32[96,512]{1,0:T(8,128)S(1)}, f32[96,512]{1,0:T(8,128)S(1)}, u32[]{:S(2)}, u32[]{:S(2)}) collective-permute-start(f32[96,512]{1,0:T(8,128)S(1)} %pass.5.refs_4_), channel_id=1, source_target_pairs={{0,4},{1,5},{2,6},{3,7},{4,0},{5,1},{6,2},{7,3},{8,12},{9,13},{10,... | collective-permute-start | bytes 589832 | tf_op jit(solution)/shard_map/ppermute | solution.py:47
  28.4 5.4 %collective-permute-start.8 = (f32[128,512]{1,0:T(8,128)S(1)}, f32[128,512]{1,0:T(8,128)S(1)}, u32[]{:S(2)}, u32[]{:S(2)}) collective-permute-start(f32[128,512]{1,0:T(8,128)S(1)} %level0.9.refs_2_.refs_0_), channel_id=1, source_target_pairs={{0,1},{1,0},{2,3},{3,2},{4,8},{5,9},{6,10},{7,11},{8,4},{9,5},{10,... | collective-permute-start | bytes 786440 | tf_op jit(solution)/shard_map/ppermute | solution.py:47
  28.5 11.2 %collective-permute-start.14 = (f32[128,512]{1,0:T(8,128)S(1)}, f32[128,512]{1,0:T(8,128)S(1)}, u32[]{:S(2)}, u32[]{:S(2)}) collective-permute-start(f32[128,512]{1,0:T(8,128)S(1)} %pass.6.refs_1_), channel_id=1, source_target_pairs={{0,4},{1,5},{2,6},{3,7},{4,0},{5,1},{6,2},{7,3},{8,12},{9,13},{10,... | collective-permute-start | bytes 786440 | tf_op jit(solution)/shard_map/ppermute | solution.py:47
  33.7 8.9 %collective-permute-start.12 = (f32[96,512]{1,0:T(8,128)S(1)}, f32[96,512]{1,0:T(8,128)S(1)}, u32[]{:S(2)}, u32[]{:S(2)}) collective-permute-start(f32[96,512]{1,0:T(8,128)S(1)} %order.14.refs_2_), channel_id=1, source_target_pairs={{0,1},{1,0},{2,3},{3,2},{4,8},{5,9},{6,10},{7,11},{8,4},{9,5},{10,... | collective-permute-start | bytes 589832 | tf_op jit(solution)/shard_map/ppermute | solution.py:47
  33.8 12.2 %collective-permute-start.11 = (f32[128,512]{1,0:T(8,128)S(1)}, f32[128,512]{1,0:T(8,128)S(1)}, u32[]{:S(2)}, u32[]{:S(2)}) collective-permute-start(f32[128,512]{1,0:T(8,128)S(1)} %pass.7.refs_1_), channel_id=1, source_target_pairs={{0,4},{1,5},{2,6},{3,7},{4,0},{5,1},{6,2},{7,3},{8,12},{9,13},{10,... | collective-permute-start | bytes 786440 | tf_op jit(solution)/shard_map/ppermute | solution.py:47
  39.7 6.3 %collective-permute-start.17 = (f32[96,512]{1,0:T(8,128)S(1)}, f32[96,512]{1,0:T(8,128)S(1)}, u32[]{:S(2)}, u32[]{:S(2)}) collective-permute-start(f32[96,512]{1,0:T(8,128)S(1)} %order.15.refs_1_.refs_2_), channel_id=1, source_target_pairs={{0,1},{1,0},{2,3},{3,2},{4,8},{5,9},{6,10},{7,11},{8,4},{9,5},{10,... | collective-permute-start | bytes 589832 | tf_op jit(solution)/shard_map/ppermute | solution.py:47
  39.8 12.6 %collective-permute-start.18 = (f32[128,512]{1,0:T(8,128)S(1)}, f32[128,512]{1,0:T(8,128)S(1)}, u32[]{:S(2)}, u32[]{:S(2)}) collective-permute-start(f32[128,512]{1,0:T(8,128)S(1)} %order.16.refs_4_.refs_2_), channel_id=1, source_target_pairs={{0,1},{1,0},{2,3},{3,2},{4,8},{5,9},{6,10},{7,11},{8,4},{9,5},{10,... | collective-permute-start | bytes 786440 | tf_op jit(solution)/shard_map/ppermute | solution.py:47
  41.0 25.7 %collective-permute-start.23 = (f32[64,512]{1,0:T(8,128)S(1)}, f32[64,512]{1,0:T(8,128)S(1)}, u32[]{:S(2)}, u32[]{:S(2)}) collective-permute-start(f32[64,512]{1,0:T(8,128)S(1)} %level2.5.refs_5_.refs_0_), channel_id=1, source_target_pairs={{0,2},{1,3},{2,0},{3,1},{4,6},{5,7},{6,4},{7,5},{8,10},{9,11},{10,... | collective-permute-start | bytes 393224 | tf_op jit(solution)/shard_map/ppermute | solution.py:47
  43.4 6.8 %collective-permute-start.19 = (f32[96,512]{1,0:T(8,128)S(1)}, f32[96,512]{1,0:T(8,128)S(1)}, u32[]{:S(2)}, u32[]{:S(2)}) collective-permute-start(f32[96,512]{1,0:T(8,128)S(1)} %level1.6.refs_1_.refs_0_), channel_id=1, source_target_pairs={{0,4},{1,5},{2,6},{3,7},{4,0},{5,1},{6,2},{7,3},{8,12},{9,13},{10,... | collective-permute-start | bytes 589832 | tf_op jit(solution)/shard_map/ppermute | solution.py:47
  46.0 11.1 %collective-permute-start.16 = (f32[128,512]{1,0:T(8,128)S(1)}, f32[128,512]{1,0:T(8,128)S(1)}, u32[]{:S(2)}, u32[]{:S(2)}) collective-permute-start(f32[128,512]{1,0:T(8,128)S(1)} %order.17.refs_5_.refs_2_), channel_id=1, source_target_pairs={{0,1},{1,0},{2,3},{3,2},{4,8},{5,9},{6,10},{7,11},{8,4},{9,5},{10,... | collective-permute-start | bytes 786440 | tf_op jit(solution)/shard_map/ppermute | solution.py:47
  46.8 8.2 %collective-permute-start.20 = (f32[96,512]{1,0:T(8,128)S(1)}, f32[96,512]{1,0:T(8,128)S(1)}, u32[]{:S(2)}, u32[]{:S(2)}) collective-permute-start(f32[96,512]{1,0:T(8,128)S(1)} %level1.7.refs_3_.refs_0_), channel_id=1, source_target_pairs={{0,4},{1,5},{2,6},{3,7},{4,0},{5,1},{6,2},{7,3},{8,12},{9,13},{10,... | collective-permute-start | bytes 589832 | tf_op jit(solution)/shard_map/ppermute | solution.py:47
  50.7 16.0 %collective-permute-start.24 = (f32[96,512]{1,0:T(8,128)S(1)}, f32[96,512]{1,0:T(8,128)S(1)}, u32[]{:S(2)}, u32[]{:S(2)}) collective-permute-start(f32[96,512]{1,0:T(8,128)S(1)} %level2.6.refs_5_.refs_1_), channel_id=1, source_target_pairs={{0,2},{1,3},{2,0},{3,1},{4,6},{5,7},{6,4},{7,5},{8,10},{9,11},{10,... | collective-permute-start | bytes 589832 | tf_op jit(solution)/shard_map/ppermute | solution.py:47
  53.1 7.8 %collective-permute-start.22 = (f32[128,512]{1,0:T(8,128)S(1)}, f32[128,512]{1,0:T(8,128)S(1)}, u32[]{:S(2)}, u32[]{:S(2)}) collective-permute-start(f32[128,512]{1,0:T(8,128)S(1)} %level1.8.refs_3_.refs_0_), channel_id=1, source_target_pairs={{0,4},{1,5},{2,6},{3,7},{4,0},{5,1},{6,2},{7,3},{8,12},{9,13},{10,... | collective-permute-start | bytes 786440 | tf_op jit(solution)/shard_map/ppermute | solution.py:47
  55.5 11.3 %collective-permute-start.25 = (f32[96,512]{1,0:T(8,128)S(1)}, f32[96,512]{1,0:T(8,128)S(1)}, u32[]{:S(2)}, u32[]{:S(2)}) collective-permute-start(f32[96,512]{1,0:T(8,128)S(1)} %level2.7.refs_5_.refs_2_), channel_id=1, source_target_pairs={{0,2},{1,3},{2,0},{3,1},{4,6},{5,7},{6,4},{7,5},{8,10},{9,11},{10,... | collective-permute-start | bytes 589832 | tf_op jit(solution)/shard_map/ppermute | solution.py:47
  57.8 7.7 %collective-permute-start.21 = (f32[128,512]{1,0:T(8,128)S(1)}, f32[128,512]{1,0:T(8,128)S(1)}, u32[]{:S(2)}, u32[]{:S(2)}) collective-permute-start(f32[128,512]{1,0:T(8,128)S(1)} %level1.9.refs_3_.refs_0_), channel_id=1, source_target_pairs={{0,4},{1,5},{2,6},{3,7},{4,0},{5,1},{6,2},{7,3},{8,12},{9,13},{10,... | collective-permute-start | bytes 786440 | tf_op jit(solution)/shard_map/ppermute | solution.py:47
  61.4 7.0 %collective-permute-start.26 = (f32[128,512]{1,0:T(8,128)S(1)}, f32[128,512]{1,0:T(8,128)S(1)}, u32[]{:S(2)}, u32[]{:S(2)}) collective-permute-start(f32[128,512]{1,0:T(8,128)S(1)} %level2.8.refs_4_.refs_3_), channel_id=1, source_target_pairs={{0,2},{1,3},{2,0},{3,1},{4,6},{5,7},{6,4},{7,5},{8,10},{9,11},{10,... | collective-permute-start | bytes 786440 | tf_op jit(solution)/shard_map/ppermute | solution.py:47
  66.0 7.4 %collective-permute-start.27 = (f32[128,512]{1,0:T(8,128)S(1)}, f32[128,512]{1,0:T(8,128)S(1)}, u32[]{:S(2)}, u32[]{:S(2)}) collective-permute-start(f32[128,512]{1,0:T(8,128)S(1)} %level2.9.refs_10_.refs_0_), channel_id=1, source_target_pairs={{0,2},{1,3},{2,0},{3,1},{4,6},{5,7},{6,4},{7,5},{8,10},{9,11},{10,... | collective-permute-start | bytes 786440 | tf_op jit(solution)/shard_map/ppermute | solution.py:47

commit v4 on v3

--- a/solution.py
+++ b/solution.py
@@ -346,8 +346,7 @@
             own = joined([r[slice(*p[-1])] for r, p in zip(refs, mine)])
             theirs = joined([r[slice(*p[-1])] for r, p in zip(refs[len(mine) :], other)])
             copies = []
-            for half in range(2):
-                part = slice(half * rank // 2, (half + 1) * rank // 2)
+            for half, part in enumerate((slice(0, 3 * rank // 4), slice(3 * rank // 4, rank))):
                 if key in done:
                     mh, ml = own_half(h.at[part], 3)[1], own_half(l.at[part], 3)[1]
                     held[part] = own[part] + product_t(theirs, mh, ml)

time: 75.3 us -> 75.3 us (level)
  no operation moved by 1% of the time
where the time goes in v4:
time: 75.3 us; the launch traced here: 75.1 us
  starting transfers between devices  42.9 us (57%)
  Pallas kernels  20 us (27%)
  waiting for transfers between devices  10.6 us (14%)
  local copies, waits for them, and re-layouts  1.36 us (2%)
    ppermute x28, starting transfers between devices, send(): return lax.ppermute(block, AXES, [(i, partner(i)) for i in range(count)])  42.9 us
    pallas_call x41, Pallas kernels, __call__(): pl.pallas_call(kernel, out_shape=outs, in_specs=specs, out_specs=[HBM, VM...  20 us
    ppermute x28, waiting for transfers between devices, send(): return lax.ppermute(block, AXES, [(i, partner(i)) for i in range(count)])  10.6 us
  transfers between devices with their start and end apart: 28, of which 7 were waited for; matrix products, arithmetic and copies ran while one was open for 0% of the time, Pallas kernels for 23%

profile of v4, /device:TPU:0, one launch (start us, length us, event | category | flops | bytes accessed | tf_op | source)
XLA Modules:
  0.0 75.1 jit_solution(912554391708761089)
XLA Ops:
  0.0 1.1 %columns.2.refs_0_ = f32[64,512]{1,0:T(8,128)S(1)} custom-call(f32[1,512,512]{2,1,0:T(8,128)} %refs_0_.7), custom_call_target="tpu_custom_call" | custom-call | flops 4000000000 | bytes 1000 | tf_op jit(solution)/shard_map/columns/pallas_call | solution.py:102
  1.1 3.0 %collective-permute-start = (f32[64,512]{1,0:T(8,128)S(1)}, f32[64,512]{1,0:T(8,128)S(1)}, u32[]{:S(2)}, u32[]{:S(2)}) collective-permute-start(f32[64,512]{1,0:T(8,128)S(1)} %order.9.refs_1_.refs_0_), channel_id=1, source_target_pairs={{0,16},{1,17},{2,18},{3,19},{4,20},{5,21},{6,22},{7,23},{8,24},{9,... | collective-permute-start | bytes 393224 | tf_op jit(solution)/shard_map/ppermute | solution.py:47
  4.1 0.6 columns.3
  4.7 1.2 %collective-permute-start.3 = (f32[96,512]{1,0:T(8,128)S(1)}, f32[96,512]{1,0:T(8,128)S(1)}, u32[]{:S(2)}, u32[]{:S(2)}) collective-permute-start(f32[96,512]{1,0:T(8,128)S(1)} %order.10.refs_1_.refs_0_), channel_id=1, source_target_pairs={{0,16},{1,17},{2,18},{3,19},{4,20},{5,21},{6,22},{7,23},{8,24},{9,... | collective-permute-start | bytes 589832 | tf_op jit(solution)/shard_map/ppermute | solution.py:47
  5.9 0.9 %collective-permute-start.2 = (f32[96,512]{1,0:T(8,128)S(1)}, f32[96,512]{1,0:T(8,128)S(1)}, u32[]{:S(2)}, u32[]{:S(2)}) collective-permute-start(f32[96,512]{1,0:T(8,128)S(1)} %order.11.refs_1_.refs_0_), channel_id=1, source_target_pairs={{0,16},{1,17},{2,18},{3,19},{4,20},{5,21},{6,22},{7,23},{8,24},{9,... | collective-permute-start | bytes 589832 | tf_op jit(solution)/shard_map/ppermute | solution.py:47
  6.9 1.3 %slice-done.1 = s8[4194304]{0:T(1024)(128)(4,1)S(1)} async-done(((s8[8388608]{0:T(1024)(128)(4,1)}), s8[4194304]{0:T(1024)(128)(4,1)S(1)}, s32[]{:S(2)}) %slice-start.1) | async-done | bytes 4194328
  8.5 0.8 %level0.5.refs_1_.refs_0_ = f32[64,512]{1,0:T(8,128)S(1)} custom-call(f32[64,512]{1,0:T(8,128)S(1)} %order.9.refs_1_.refs_0_, f32[64,512]{1,0:T(8,128)S(1)} %collective-permute-done.refs_1_, bf16[512,1024]{1,0:T(8,128)(2,1)S(1)} %get-tuple-element.24.refs_2_, bf16[512,1024]{1,0:T(8,128)(2,1)S(1)} %get-tuple-element.25.refs_3_), custom_call_target="tpu_custom_call" | custom-call | flops 4000000000 | bytes 1000 | tf_op jit(solution)/shard_map/level0/pallas_call | solution.py:102
  9.3 3.0 %collective-permute-start.7 = (f32[64,512]{1,0:T(8,128)S(1)}, f32[64,512]{1,0:T(8,128)S(1)}, u32[]{:S(2)}, u32[]{:S(2)}) collective-permute-start(f32[64,512]{1,0:T(8,128)S(1)} %level0.5.refs_1_.refs_0_), channel_id=1, source_target_pairs={{0,8},{1,9},{2,10},{3,11},{4,12},{5,13},{6,14},{7,15},{8,0},{9,1},... | collective-permute-start | bytes 393224 | tf_op jit(solution)/shard_map/ppermute | solution.py:47
  12.6 1.6 %collective-permute-start.5 = (f32[128,512]{1,0:T(8,128)S(1)}, f32[128,512]{1,0:T(8,128)S(1)}, u32[]{:S(2)}, u32[]{:S(2)}) collective-permute-start(f32[128,512]{1,0:T(8,128)S(1)} %order.12.refs_1_.refs_0_), channel_id=1, source_target_pairs={{0,16},{1,17},{2,18},{3,19},{4,20},{5,21},{6,22},{7,23},{8,24},{9,... | collective-permute-start | bytes 786440 | tf_op jit(solution)/shard_map/ppermute | solution.py:47
  15.0 0.8 %level0.6.refs_4_.refs_0_ = f32[96,512]{1,0:T(8,128)S(1)} custom-call(f32[96,512]{1,0:T(8,128)S(1)} %order.10.refs_1_.refs_0_, f32[96,512]{1,0:T(8,128)S(1)} %collective-permute-done.3.refs_1_, bf16[512,1024]{1,0:T(8,128)(2,1)S(1)} %get-tuple-element.24.refs_2_, bf16[512,1024]{1,0:T(8,128)(2,1)S(1)} %get-tuple-element.25.refs_3_, ...), custom_call_target="tpu_custom_call" | custom-call | flops 4000000000 | bytes 1000 | tf_op jit(solution)/shard_map/level0/pallas_call | solution.py:102
  15.8 1.0 %collective-permute-done.2.refs_1_ = f32[96,512]{1,0:T(8,128)S(1)} collective-permute-done((f32[96,512]{1,0:T(8,128)S(1)}, f32[96,512]{1,0:T(8,128)S(1)}, u32[]{:S(2)}, u32[]{:S(2)}) %collective-permute-start.2) | collective-permute-done | bytes 196640 | tf_op jit(solution)/shard_map/ppermute | solution.py:47
  16.8 0.8 %level0.7.refs_4_.refs_0_ = f32[96,512]{1,0:T(8,128)S(1)} custom-call(f32[96,512]{1,0:T(8,128)S(1)} %order.11.refs_1_.refs_0_, f32[96,512]{1,0:T(8,128)S(1)} %collective-permute-done.2.refs_1_, bf16[512,1024]{1,0:T(8,128)(2,1)S(1)} %get-tuple-element.24.refs_2_, bf16[512,1024]{1,0:T(8,128)(2,1)S(1)} %get-tuple-element.25.refs_3_, ...), custom_call_target="tpu_custom_call" | custom-call | flops 4000000000 | bytes 1000 | tf_op jit(solution)/shard_map/level0/pallas_call | solution.py:102
  18.1 0.8 %level1.5.refs_2_.refs_0_ = f32[64,512]{1,0:T(8,128)S(1)} custom-call(f32[64,512]{1,0:T(8,128)S(1)} %level0.5.refs_1_.refs_0_, f32[64,512]{1,0:T(8,128)S(1)} %collective-permute-done.7.refs_1_, bf16[512,1024]{1,0:T(8,128)(2,1)S(1)} %get-tuple-element.28.refs_2_.refs_3_, bf16[512,1024]{1,0:T(8,128)(2,1)S(1)} %get-tuple-element.26.refs_1_.refs_3_.refs_4_, ...), custom_call_target="tpu_custom_call" | custom-call | flops 4000000000 | bytes 1000 | tf_op jit(solution)/shard_map/level1/pallas_call | solution.py:102
  18.9 3.2 %collective-permute-start.13 = (f32[64,512]{1,0:T(8,128)S(1)}, f32[64,512]{1,0:T(8,128)S(1)}, u32[]{:S(2)}, u32[]{:S(2)}) collective-permute-start(f32[64,512]{1,0:T(8,128)S(1)} %level1.5.refs_2_.refs_0_), channel_id=1, source_target_pairs={{0,4},{1,5},{2,6},{3,7},{4,0},{5,1},{6,2},{7,3},{8,12},{9,13},{10,... | collective-permute-start | bytes 393224 | tf_op jit(solution)/shard_map/ppermute | solution.py:47
  22.2 2.8 %collective-permute-start.9 = (f32[96,512]{1,0:T(8,128)S(1)}, f32[96,512]{1,0:T(8,128)S(1)}, u32[]{:S(2)}, u32[]{:S(2)}) collective-permute-start(f32[96,512]{1,0:T(8,128)S(1)} %pass.4.refs_4_), channel_id=1, source_target_pairs={{0,4},{1,5},{2,6},{3,7},{4,0},{5,1},{6,2},{7,3},{8,12},{9,13},{10,... | collective-permute-start | bytes 589832 | tf_op jit(solution)/shard_map/ppermute | solution.py:47
  25.0 0.7 level0.8.refs_2_.refs_0_
  25.9 1.8 %collective-permute-start.15 = (f32[96,512]{1,0:T(8,128)S(1)}, f32[96,512]{1,0:T(8,128)S(1)}, u32[]{:S(2)}, u32[]{:S(2)}) collective-permute-start(f32[96,512]{1,0:T(8,128)S(1)} %pass.5.refs_4_), channel_id=1, source_target_pairs={{0,4},{1,5},{2,6},{3,7},{4,0},{5,1},{6,2},{7,3},{8,12},{9,13},{10,... | collective-permute-start | bytes 589832 | tf_op jit(solution)/shard_map/ppermute | solution.py:47
  27.6 0.7 level0.9.refs_2_.refs_0_
  28.5 5.2 %collective-permute-start.14 = (f32[128,512]{1,0:T(8,128)S(1)}, f32[128,512]{1,0:T(8,128)S(1)}, u32[]{:S(2)}, u32[]{:S(2)}) collective-permute-start(f32[128,512]{1,0:T(8,128)S(1)} %pass.6.refs_1_), channel_id=1, source_target_pairs={{0,4},{1,5},{2,6},{3,7},{4,0},{5,1},{6,2},{7,3},{8,12},{9,13},{10,... | collective-permute-start | bytes 786440 | tf_op jit(solution)/shard_map/ppermute | solution.py:47
  33.8 5.6 %collective-permute-start.11 = (f32[128,512]{1,0:T(8,128)S(1)}, f32[128,512]{1,0:T(8,128)S(1)}, u32[]{:S(2)}, u32[]{:S(2)}) collective-permute-start(f32[128,512]{1,0:T(8,128)S(1)} %pass.7.refs_1_), channel_id=1, source_target_pairs={{0,4},{1,5},{2,6},{3,7},{4,0},{5,1},{6,2},{7,3},{8,12},{9,13},{10,... | collective-permute-start | bytes 786440 | tf_op jit(solution)/shard_map/ppermute | solution.py:47
  39.8 0.5 collective-permute-start.18
  40.2 0.8 %level2.5.refs_5_.refs_0_ = f32[64,512]{1,0:T(8,128)S(1)} custom-call(f32[64,512]{1,0:T(8,128)S(1)} %level1.5.refs_2_.refs_0_, f32[64,512]{1,0:T(8,128)S(1)} %collective-permute-done.13.refs_1_, bf16[512,1024]{1,0:T(8,128)(2,1)S(1)} %get-tuple-element.29.refs_2_.refs_1_, bf16[512,1024]{1,0:T(8,128)(2,1)S(1)} %get-tuple-element.27.refs_4_.refs_3_.refs_2_, ...), custom_call_target="tpu_custom_call" | custom-call | flops 4000000000 | bytes 1000 | tf_op jit(solution)/shard_map/level2/pallas_call | solution.py:102
  41.0 1.6 %collective-permute-start.23 = (f32[64,512]{1,0:T(8,128)S(1)}, f32[64,512]{1,0:T(8,128)S(1)}, u32[]{:S(2)}, u32[]{:S(2)}) collective-permute-start(f32[64,512]{1,0:T(8,128)S(1)} %level2.5.refs_5_.refs_0_), channel_id=1, source_target_pairs={{0,2},{1,3},{2,0},{3,1},{4,6},{5,7},{6,4},{7,5},{8,10},{9,11},{10,... | collective-permute-start | bytes 393224 | tf_op jit(solution)/shard_map/ppermute | solution.py:47
  42.6 0.8 %level1.6.refs_1_.refs_0_ = f32[96,512]{1,0:T(8,128)S(1)} custom-call(f32[96,512]{1,0:T(8,128)S(1)} %level0.6.refs_4_.refs_0_, f32[96,512]{1,0:T(8,128)S(1)} %collective-permute-done.12.refs_1_, f32[96,512]{1,0:T(8,128)S(1)} %order.14.refs_2_, bf16[512,1024]{1,0:T(8,128)(2,1)S(1)} %get-tuple-element.28.refs_2_.refs_3_, ...), custom_call_target="tpu_custom_call" | custom-call | flops 4000000000 | bytes 1000 | tf_op jit(solution)/shard_map/level1/pallas_call | solution.py:102
  43.4 2.5 %collective-permute-start.19 = (f32[96,512]{1,0:T(8,128)S(1)}, f32[96,512]{1,0:T(8,128)S(1)}, u32[]{:S(2)}, u32[]{:S(2)}) collective-permute-start(f32[96,512]{1,0:T(8,128)S(1)} %level1.6.refs_1_.refs_0_), channel_id=1, source_target_pairs={{0,4},{1,5},{2,6},{3,7},{4,0},{5,1},{6,2},{7,3},{8,12},{9,13},{10,... | collective-permute-start | bytes 589832 | tf_op jit(solution)/shard_map/ppermute | solution.py:47
  46.0 0.8 %level1.7.refs_3_.refs_0_ = f32[96,512]{1,0:T(8,128)S(1)} custom-call(f32[96,512]{1,0:T(8,128)S(1)} %level0.7.refs_4_.refs_0_, f32[96,512]{1,0:T(8,128)S(1)} %collective-permute-done.17.refs_1_, f32[96,512]{1,0:T(8,128)S(1)} %order.15.refs_1_.refs_2_, bf16[512,1024]{1,0:T(8,128)(2,1)S(1)} %get-tuple-element.28.refs_2_.refs_3_, ...), custom_call_target="tpu_custom_call" | custom-call | flops 4000000000 | bytes 1000 | tf_op jit(solution)/shard_map/level1/pallas_call | solution.py:102
  46.8 2.4 %collective-permute-start.20 = (f32[96,512]{1,0:T(8,128)S(1)}, f32[96,512]{1,0:T(8,128)S(1)}, u32[]{:S(2)}, u32[]{:S(2)}) collective-permute-start(f32[96,512]{1,0:T(8,128)S(1)} %level1.7.refs_3_.refs_0_), channel_id=1, source_target_pairs={{0,4},{1,5},{2,6},{3,7},{4,0},{5,1},{6,2},{7,3},{8,12},{9,13},{10,... | collective-permute-start | bytes 589832 | tf_op jit(solution)/shard_map/ppermute | solution.py:47
  49.2 0.5 ahead.5.refs_0_
  49.7 0.5 collective-permute-done.19.refs_1_
  50.2 0.5 level2.6.refs_5_.refs_1_
  50.7 1.7 %collective-permute-start.24 = (f32[96,512]{1,0:T(8,128)S(1)}, f32[96,512]{1,0:T(8,128)S(1)}, u32[]{:S(2)}, u32[]{:S(2)}) collective-permute-start(f32[96,512]{1,0:T(8,128)S(1)} %level2.6.refs_5_.refs_1_), channel_id=1, source_target_pairs={{0,2},{1,3},{2,0},{3,1},{4,6},{5,7},{6,4},{7,5},{8,10},{9,11},{10,... | collective-permute-start | bytes 589832 | tf_op jit(solution)/shard_map/ppermute | solution.py:47
  52.3 0.8 level1.8.refs_3_.refs_0_
  53.1 1.4 %collective-permute-start.22 = (f32[128,512]{1,0:T(8,128)S(1)}, f32[128,512]{1,0:T(8,128)S(1)}, u32[]{:S(2)}, u32[]{:S(2)}) collective-permute-start(f32[128,512]{1,0:T(8,128)S(1)} %level1.8.refs_3_.refs_0_), channel_id=1, source_target_pairs={{0,4},{1,5},{2,6},{3,7},{4,0},{5,1},{6,2},{7,3},{8,12},{9,13},{10,... | collective-permute-start | bytes 786440 | tf_op jit(solution)/shard_map/ppermute | solution.py:47
  54.5 0.5 ahead.6.refs_0_
  55.0 0.5 level2.7.refs_5_.refs_2_
  55.5 1.6 %collective-permute-start.25 = (f32[96,512]{1,0:T(8,128)S(1)}, f32[96,512]{1,0:T(8,128)S(1)}, u32[]{:S(2)}, u32[]{:S(2)}) collective-permute-start(f32[96,512]{1,0:T(8,128)S(1)} %level2.7.refs_5_.refs_2_), channel_id=1, source_target_pairs={{0,2},{1,3},{2,0},{3,1},{4,6},{5,7},{6,4},{7,5},{8,10},{9,11},{10,... | collective-permute-start | bytes 589832 | tf_op jit(solution)/shard_map/ppermute | solution.py:47
  57.0 0.8 level1.9.refs_3_.refs_0_
  57.8 1.0 %collective-permute-start.21 = (f32[128,512]{1,0:T(8,128)S(1)}, f32[128,512]{1,0:T(8,128)S(1)}, u32[]{:S(2)}, u32[]{:S(2)}) collective-permute-start(f32[128,512]{1,0:T(8,128)S(1)} %level1.9.refs_3_.refs_0_), channel_id=1, source_target_pairs={{0,4},{1,5},{2,6},{3,7},{4,0},{5,1},{6,2},{7,3},{8,12},{9,13},{10,... | collective-permute-start | bytes 786440 | tf_op jit(solution)/shard_map/ppermute | solution.py:47
  59.3 0.5 ahead.8.refs_4_.refs_0_
  59.7 1.2 %collective-permute-done.22.refs_1_ = f32[128,512]{1,0:T(8,128)S(1)} collective-permute-done((f32[128,512]{1,0:T(8,128)S(1)}, f32[128,512]{1,0:T(8,128)S(1)}, u32[]{:S(2)}, u32[]{:S(2)}) %collective-permute-start.22) | collective-permute-done | bytes 262176 | tf_op jit(solution)/shard_map/ppermute | solution.py:47
  61.8 3.7 %collective-permute-done.21.refs_1_ = f32[128,512]{1,0:T(8,128)S(1)} collective-permute-done((f32[128,512]{1,0:T(8,128)S(1)}, f32[128,512]{1,0:T(8,128)S(1)}, u32[]{:S(2)}, u32[]{:S(2)}) %collective-permute-start.21) | collective-permute-done | bytes 262176 | tf_op jit(solution)/shard_map/ppermute | solution.py:47
  65.5 0.5 level2.9.refs_10_.refs_0_
  66.0 0.7 collective-permute-start.27
  66.7 1.7 %collective-permute-done.26.refs_7_ = f32[128,512]{1,0:T(8,128)S(1)} collective-permute-done((f32[128,512]{1,0:T(8,128)S(1)}, f32[128,512]{1,0:T(8,128)S(1)}, u32[]{:S(2)}, u32[]{:S(2)}) %collective-permute-start.26) | collective-permute-done | bytes 262176 | tf_op jit(solution)/shard_map/ppermute | solution.py:47
  68.4 2.6 %level3.2 = (f32[1,512,512]{2,1,0:T(8,128)}, f32[8,128]{1,0:T(8,128)S(1)}) custom-call(f32[64,512]{1,0:T(8,128)S(1)} %level2.5.refs_5_.refs_0_, f32[96,512]{1,0:T(8,128)S(1)} %level2.6.refs_5_.refs_1_, f32[96,512]{1,0:T(8,128)S(1)} %level2.7.refs_5_.refs_2_, f32[128,512]{1,0:T(8,128)S(1)} %level2.8.refs_4_.refs_3_, ...), custom_call_target="tpu_custom_call" | custom-call | flops 4000000000 | bytes 1000 | tf_op jit(solution)/shard_map/level3/pallas_call | solution.py:102
  71.0 0.5 ahead.9.refs_0_
  71.5 2.0 %collective-permute-done.27.refs_1_ = f32[128,512]{1,0:T(8,128)S(1)} collective-permute-done((f32[128,512]{1,0:T(8,128)S(1)}, f32[128,512]{1,0:T(8,128)S(1)}, u32[]{:S(2)}, u32[]{:S(2)}) %collective-permute-start.27) | collective-permute-done | bytes 262176 | tf_op jit(solution)/shard_map/ppermute | solution.py:47
  73.4 1.7 %level3.3 = (f32[1,512,512]{2,1,0:T(8,128)}, f32[8,128]{1,0:T(8,128)}) custom-call(f32[512,128]{1,0:T(8,128)S(1)} %ahead.9.refs_0_, f32[128,512]{1,0:T(8,128)S(1)} %collective-permute-done.27.refs_1_, bf16[512,1024]{1,0:T(8,128)(2,1)S(1)} %get-tuple-element.31.refs_8_.refs_1_.refs_2_, ...), custom_call_target="tpu_custom_call", output_to_operand_aliasing={{0}: (4, {})} | custom-call | flops 4000000000 | bytes 1000 | tf_op jit(solution)/shard_map/level3/pallas_call | solution.py:102
  (56 shorter events, 4.0 us)
Async XLA Ops:
  1.1 3.0 %copy-start = (f32[1,512,512]{2,1,0:T(8,128)S(1)}, f32[1,512,512]{2,1,0:T(8,128)}, u32[]{:S(2)}) copy-start(f32[1,512,512]{2,1,0:T(8,128)} %refs_0_.7) | copy-start | bytes 3145732
  1.1 7.3 %collective-permute-start = (f32[64,512]{1,0:T(8,128)S(1)}, f32[64,512]{1,0:T(8,128)S(1)}, u32[]{:S(2)}, u32[]{:S(2)}) collective-permute-start(f32[64,512]{1,0:T(8,128)S(1)} %order.9.refs_1_.refs_0_), channel_id=1, source_target_pairs={{0,16},{1,17},{2,18},{3,19},{4,20},{5,21},{6,22},{7,23},{8,24},{9,... | collective-permute-start | bytes 393224 | tf_op jit(solution)/shard_map/ppermute | solution.py:47
  4.7 2.2 %slice-start = ((s8[8388608]{0:T(1024)(128)(4,1)}), s8[4194304]{0:T(1024)(128)(4,1)S(1)}, s32[]{:S(2)}) async-start(s8[8388608]{0:T(1024)(128)(4,1)} %bitcast), calls=%async_computation | async-start | bytes 8388608
  4.7 3.5 %slice-start.1 = ((s8[8388608]{0:T(1024)(128)(4,1)}), s8[4194304]{0:T(1024)(128)(4,1)S(1)}, s32[]{:S(2)}) async-start(s8[8388608]{0:T(1024)(128)(4,1)} %bitcast), calls=%async_computation.1 | async-start | bytes 8388608
  4.7 10.2 %collective-permute-start.3 = (f32[96,512]{1,0:T(8,128)S(1)}, f32[96,512]{1,0:T(8,128)S(1)}, u32[]{:S(2)}, u32[]{:S(2)}) collective-permute-start(f32[96,512]{1,0:T(8,128)S(1)} %order.10.refs_1_.refs_0_), channel_id=1, source_target_pairs={{0,16},{1,17},{2,18},{3,19},{4,20},{5,21},{6,22},{7,23},{8,24},{9,... | collective-permute-start | bytes 589832 | tf_op jit(solution)/shard_map/ppermute | solution.py:47
  5.9 10.9 %collective-permute-start.2 = (f32[96,512]{1,0:T(8,128)S(1)}, f32[96,512]{1,0:T(8,128)S(1)}, u32[]{:S(2)}, u32[]{:S(2)}) collective-permute-start(f32[96,512]{1,0:T(8,128)S(1)} %order.11.refs_1_.refs_0_), channel_id=1, source_target_pairs={{0,16},{1,17},{2,18},{3,19},{4,20},{5,21},{6,22},{7,23},{8,24},{9,... | collective-permute-start | bytes 589832 | tf_op jit(solution)/shard_map/ppermute | solution.py:47
  9.3 8.8 %collective-permute-start.7 = (f32[64,512]{1,0:T(8,128)S(1)}, f32[64,512]{1,0:T(8,128)S(1)}, u32[]{:S(2)}, u32[]{:S(2)}) collective-permute-start(f32[64,512]{1,0:T(8,128)S(1)} %level0.5.refs_1_.refs_0_), channel_id=1, source_target_pairs={{0,8},{1,9},{2,10},{3,11},{4,12},{5,13},{6,14},{7,15},{8,0},{9,1},... | collective-permute-start | bytes 393224 | tf_op jit(solution)/shard_map/ppermute | solution.py:47
  12.6 12.4 %collective-permute-start.5 = (f32[128,512]{1,0:T(8,128)S(1)}, f32[128,512]{1,0:T(8,128)S(1)}, u32[]{:S(2)}, u32[]{:S(2)}) collective-permute-start(f32[128,512]{1,0:T(8,128)S(1)} %order.12.refs_1_.refs_0_), channel_id=1, source_target_pairs={{0,16},{1,17},{2,18},{3,19},{4,20},{5,21},{6,22},{7,23},{8,24},{9,... | collective-permute-start | bytes 786440 | tf_op jit(solution)/shard_map/ppermute | solution.py:47
  14.2 13.4 %collective-permute-start.1 = (f32[128,512]{1,0:T(8,128)S(1)}, f32[128,512]{1,0:T(8,128)S(1)}, u32[]{:S(2)}, u32[]{:S(2)}) collective-permute-start(f32[128,512]{1,0:T(8,128)S(1)} %order.13.refs_1_.refs_0_), channel_id=1, source_target_pairs={{0,16},{1,17},{2,18},{3,19},{4,20},{5,21},{6,22},{7,23},{8,24},{9,... | collective-permute-start | bytes 786440 | tf_op jit(solution)/shard_map/ppermute | solution.py:47
  15.8 6.4 %collective-permute-start.6 = (f32[96,512]{1,0:T(8,128)S(1)}, f32[96,512]{1,0:T(8,128)S(1)}, u32[]{:S(2)}, u32[]{:S(2)}) collective-permute-start(f32[96,512]{1,0:T(8,128)S(1)} %level0.6.refs_4_.refs_0_), channel_id=1, source_target_pairs={{0,1},{1,0},{2,3},{3,2},{4,8},{5,9},{6,10},{7,11},{8,4},{9,5},{10,... | collective-permute-start | bytes 589832 | tf_op jit(solution)/shard_map/ppermute | solution.py:47
  17.6 8.2 %collective-permute-start.4 = (f32[96,512]{1,0:T(8,128)S(1)}, f32[96,512]{1,0:T(8,128)S(1)}, u32[]{:S(2)}, u32[]{:S(2)}) collective-permute-start(f32[96,512]{1,0:T(8,128)S(1)} %level0.7.refs_4_.refs_0_), channel_id=1, source_target_pairs={{0,1},{1,0},{2,3},{3,2},{4,8},{5,9},{6,10},{7,11},{8,4},{9,5},{10,... | collective-permute-start | bytes 589832 | tf_op jit(solution)/shard_map/ppermute | solution.py:47
  18.9 21.3 %collective-permute-start.13 = (f32[64,512]{1,0:T(8,128)S(1)}, f32[64,512]{1,0:T(8,128)S(1)}, u32[]{:S(2)}, u32[]{:S(2)}) collective-permute-start(f32[64,512]{1,0:T(8,128)S(1)} %level1.5.refs_2_.refs_0_), channel_id=1, source_target_pairs={{0,4},{1,5},{2,6},{3,7},{4,0},{5,1},{6,2},{7,3},{8,12},{9,13},{10,... | collective-permute-start | bytes 393224 | tf_op jit(solution)/shard_map/ppermute | solution.py:47
  22.2 11.6 %collective-permute-start.9 = (f32[96,512]{1,0:T(8,128)S(1)}, f32[96,512]{1,0:T(8,128)S(1)}, u32[]{:S(2)}, u32[]{:S(2)}) collective-permute-start(f32[96,512]{1,0:T(8,128)S(1)} %pass.4.refs_4_), channel_id=1, source_target_pairs={{0,4},{1,5},{2,6},{3,7},{4,0},{5,1},{6,2},{7,3},{8,12},{9,13},{10,... | collective-permute-start | bytes 589832 | tf_op jit(solution)/shard_map/ppermute | solution.py:47
  25.7 2.7 %collective-permute-start.10 = (f32[128,512]{1,0:T(8,128)S(1)}, f32[128,512]{1,0:T(8,128)S(1)}, u32[]{:S(2)}, u32[]{:S(2)}) collective-permute-start(f32[128,512]{1,0:T(8,128)S(1)} %level0.8.refs_2_.refs_0_), channel_id=1, source_target_pairs={{0,1},{1,0},{2,3},{3,2},{4,8},{5,9},{6,10},{7,11},{8,4},{9,5},{10,... | collective-permute-start | bytes 786440 | tf_op jit(solution)/shard_map/ppermute | solution.py:47
  25.9 13.8 %collective-permute-start.15 = (f32[96,512]{1,0:T(8,128)S(1)}, f32[96,512]{1,0:T(8,128)S(1)}, u32[]{:S(2)}, u32[]{:S(2)}) collective-permute-start(f32[96,512]{1,0:T(8,128)S(1)} %pass.5.refs_4_), channel_id=1, source_target_pairs={{0,4},{1,5},{2,6},{3,7},{4,0},{5,1},{6,2},{7,3},{8,12},{9,13},{10,... | collective-permute-start | bytes 589832 | tf_op jit(solution)/shard_map/ppermute | solution.py:47
  28.4 5.4 %collective-permute-start.8 = (f32[128,512]{1,0:T(8,128)S(1)}, f32[128,512]{1,0:T(8,128)S(1)}, u32[]{:S(2)}, u32[]{:S(2)}) collective-permute-start(f32[128,512]{1,0:T(8,128)S(1)} %level0.9.refs_2_.refs_0_), channel_id=1, source_target_pairs={{0,1},{1,0},{2,3},{3,2},{4,8},{5,9},{6,10},{7,11},{8,4},{9,5},{10,... | collective-permute-start | bytes 786440 | tf_op jit(solution)/shard_map/ppermute | solution.py:47
  28.5 11.2 %collective-permute-start.14 = (f32[128,512]{1,0:T(8,128)S(1)}, f32[128,512]{1,0:T(8,128)S(1)}, u32[]{:S(2)}, u32[]{:S(2)}) collective-permute-start(f32[128,512]{1,0:T(8,128)S(1)} %pass.6.refs_1_), channel_id=1, source_target_pairs={{0,4},{1,5},{2,6},{3,7},{4,0},{5,1},{6,2},{7,3},{8,12},{9,13},{10,... | collective-permute-start | bytes 786440 | tf_op jit(solution)/shard_map/ppermute | solution.py:47
  33.7 8.9 %collective-permute-start.12 = (f32[96,512]{1,0:T(8,128)S(1)}, f32[96,512]{1,0:T(8,128)S(1)}, u32[]{:S(2)}, u32[]{:S(2)}) collective-permute-start(f32[96,512]{1,0:T(8,128)S(1)} %order.14.refs_2_), channel_id=1, source_target_pairs={{0,1},{1,0},{2,3},{3,2},{4,8},{5,9},{6,10},{7,11},{8,4},{9,5},{10,... | collective-permute-start | bytes 589832 | tf_op jit(solution)/shard_map/ppermute | solution.py:47
  33.8 12.2 %collective-permute-start.11 = (f32[128,512]{1,0:T(8,128)S(1)}, f32[128,512]{1,0:T(8,128)S(1)}, u32[]{:S(2)}, u32[]{:S(2)}) collective-permute-start(f32[128,512]{1,0:T(8,128)S(1)} %pass.7.refs_1_), channel_id=1, source_target_pairs={{0,4},{1,5},{2,6},{3,7},{4,0},{5,1},{6,2},{7,3},{8,12},{9,13},{10,... | collective-permute-start | bytes 786440 | tf_op jit(solution)/shard_map/ppermute | solution.py:47
  39.7 6.3 %collective-permute-start.17 = (f32[96,512]{1,0:T(8,128)S(1)}, f32[96,512]{1,0:T(8,128)S(1)}, u32[]{:S(2)}, u32[]{:S(2)}) collective-permute-start(f32[96,512]{1,0:T(8,128)S(1)} %order.15.refs_1_.refs_2_), channel_id=1, source_target_pairs={{0,1},{1,0},{2,3},{3,2},{4,8},{5,9},{6,10},{7,11},{8,4},{9,5},{10,... | collective-permute-start | bytes 589832 | tf_op jit(solution)/shard_map/ppermute | solution.py:47
  39.8 12.6 %collective-permute-start.18 = (f32[128,512]{1,0:T(8,128)S(1)}, f32[128,512]{1,0:T(8,128)S(1)}, u32[]{:S(2)}, u32[]{:S(2)}) collective-permute-start(f32[128,512]{1,0:T(8,128)S(1)} %order.16.refs_4_.refs_2_), channel_id=1, source_target_pairs={{0,1},{1,0},{2,3},{3,2},{4,8},{5,9},{6,10},{7,11},{8,4},{9,5},{10,... | collective-permute-start | bytes 786440 | tf_op jit(solution)/shard_map/ppermute | solution.py:47
  41.0 25.7 %collective-permute-start.23 = (f32[64,512]{1,0:T(8,128)S(1)}, f32[64,512]{1,0:T(8,128)S(1)}, u32[]{:S(2)}, u32[]{:S(2)}) collective-permute-start(f32[64,512]{1,0:T(8,128)S(1)} %level2.5.refs_5_.refs_0_), channel_id=1, source_target_pairs={{0,2},{1,3},{2,0},{3,1},{4,6},{5,7},{6,4},{7,5},{8,10},{9,11},{10,... | collective-permute-start | bytes 393224 | tf_op jit(solution)/shard_map/ppermute | solution.py:47
  43.4 6.8 %collective-permute-start.19 = (f32[96,512]{1,0:T(8,128)S(1)}, f32[96,512]{1,0:T(8,128)S(1)}, u32[]{:S(2)}, u32[]{:S(2)}) collective-permute-start(f32[96,512]{1,0:T(8,128)S(1)} %level1.6.refs_1_.refs_0_), channel_id=1, source_target_pairs={{0,4},{1,5},{2,6},{3,7},{4,0},{5,1},{6,2},{7,3},{8,12},{9,13},{10,... | collective-permute-start | bytes 589832 | tf_op jit(solution)/shard_map/ppermute | solution.py:47
  46.0 11.1 %collective-permute-start.16 = (f32[128,512]{1,0:T(8,128)S(1)}, f32[128,512]{1,0:T(8,128)S(1)}, u32[]{:S(2)}, u32[]{:S(2)}) collective-permute-start(f32[128,512]{1,0:T(8,128)S(1)} %order.17.refs_5_.refs_2_), channel_id=1, source_target_pairs={{0,1},{1,0},{2,3},{3,2},{4,8},{5,9},{6,10},{7,11},{8,4},{9,5},{10,... | collective-permute-start | bytes 786440 | tf_op jit(solution)/shard_map/ppermute | solution.py:47
  46.8 8.2 %collective-permute-start.20 = (f32[96,512]{1,0:T(8,128)S(1)}, f32[96,512]{1,0:T(8,128)S(1)}, u32[]{:S(2)}, u32[]{:S(2)}) collective-permute-start(f32[96,512]{1,0:T(8,128)S(1)} %level1.7.refs_3_.refs_0_), channel_id=1, source_target_pairs={{0,4},{1,5},{2,6},{3,7},{4,0},{5,1},{6,2},{7,3},{8,12},{9,13},{10,... | collective-permute-start | bytes 589832 | tf_op jit(solution)/shard_map/ppermute | solution.py:47
  50.7 16.0 %collective-permute-start.24 = (f32[96,512]{1,0:T(8,128)S(1)}, f32[96,512]{1,0:T(8,128)S(1)}, u32[]{:S(2)}, u32[]{:S(2)}) collective-permute-start(f32[96,512]{1,0:T(8,128)S(1)} %level2.6.refs_5_.refs_1_), channel_id=1, source_target_pairs={{0,2},{1,3},{2,0},{3,1},{4,6},{5,7},{6,4},{7,5},{8,10},{9,11},{10,... | collective-permute-start | bytes 589832 | tf_op jit(solution)/shard_map/ppermute | solution.py:47
  53.1 7.8 %collective-permute-start.22 = (f32[128,512]{1,0:T(8,128)S(1)}, f32[128,512]{1,0:T(8,128)S(1)}, u32[]{:S(2)}, u32[]{:S(2)}) collective-permute-start(f32[128,512]{1,0:T(8,128)S(1)} %level1.8.refs_3_.refs_0_), channel_id=1, source_target_pairs={{0,4},{1,5},{2,6},{3,7},{4,0},{5,1},{6,2},{7,3},{8,12},{9,13},{10,... | collective-permute-start | bytes 786440 | tf_op jit(solution)/shard_map/ppermute | solution.py:47
  55.5 11.3 %collective-permute-start.25 = (f32[96,512]{1,0:T(8,128)S(1)}, f32[96,512]{1,0:T(8,128)S(1)}, u32[]{:S(2)}, u32[]{:S(2)}) collective-permute-start(f32[96,512]{1,0:T(8,128)S(1)} %level2.7.refs_5_.refs_2_), channel_id=1, source_target_pairs={{0,2},{1,3},{2,0},{3,1},{4,6},{5,7},{6,4},{7,5},{8,10},{9,11},{10,... | collective-permute-start | bytes 589832 | tf_op jit(solution)/shard_map/ppermute | solution.py:47
  57.8 7.7 %collective-permute-start.21 = (f32[128,512]{1,0:T(8,128)S(1)}, f32[128,512]{1,0:T(8,128)S(1)}, u32[]{:S(2)}, u32[]{:S(2)}) collective-permute-start(f32[128,512]{1,0:T(8,128)S(1)} %level1.9.refs_3_.refs_0_), channel_id=1, source_target_pairs={{0,4},{1,5},{2,6},{3,7},{4,0},{5,1},{6,2},{7,3},{8,12},{9,13},{10,... | collective-permute-start | bytes 786440 | tf_op jit(solution)/shard_map/ppermute | solution.py:47
  61.4 7.0 %collective-permute-start.26 = (f32[128,512]{1,0:T(8,128)S(1)}, f32[128,512]{1,0:T(8,128)S(1)}, u32[]{:S(2)}, u32[]{:S(2)}) collective-permute-start(f32[128,512]{1,0:T(8,128)S(1)} %level2.8.refs_4_.refs_3_), channel_id=1, source_target_pairs={{0,2},{1,3},{2,0},{3,1},{4,6},{5,7},{6,4},{7,5},{8,10},{9,11},{10,... | collective-permute-start | bytes 786440 | tf_op jit(solution)/shard_map/ppermute | solution.py:47
  66.0 7.4 %collective-permute-start.27 = (f32[128,512]{1,0:T(8,128)S(1)}, f32[128,512]{1,0:T(8,128)S(1)}, u32[]{:S(2)}, u32[]{:S(2)}) collective-permute-start(f32[128,512]{1,0:T(8,128)S(1)} %level2.9.refs_10_.refs_0_), channel_id=1, source_target_pairs={{0,2},{1,3},{2,0},{3,1},{4,6},{5,7},{6,4},{7,5},{8,10},{9,11},{10,... | collective-permute-start | bytes 786440 | tf_op jit(solution)/shard_map/ppermute | solution.py:47
